TPU v7x, 512 devices: a whole 4x8x8 slice. The times are simulated.
512 devices in a mesh: ctx: 64 (over z, y_hi, x), exp: 8 (over y_lo, core).
Axes of the slice: x: 4, y: 8 (y_hi: 2, y_lo: 4; y = y_hi * 4 + y_lo), z: 8, core: 2. Of those that a mesh axis runs over, the one named last changes fastest.
Arguments:
- queries: bfloat16 [2048, 73728], P(('ctx', 'exp')), may hold values from -24 to 24
- latents: bfloat16 [5120, 576], P('ctx'), may hold values from -6 to 6
- offsets: int32 [512], P(('ctx', 'exp')), may hold values from 3072 to 5116, as said below
- moe_input: bfloat16 [256, 5120], P('exp', 'ctx'), may hold values from -6 to 6
- routes: int32 [256, 6], P('exp'), may hold values from 0 to 15, all different within a row; in each aligned block of 32 rows (0 to 31, 32 to 63, ...) at most 16 rows name the same one
- gate_values: float32 [256, 6], P('exp'), may hold values from 0.05 to 0.45
- w_gate: bfloat16 [16, 5120, 1536], P('exp', 'ctx'), may hold values from -0.078125 to 0.078125
- w_up: bfloat16 [16, 5120, 1536], P('exp', 'ctx'), may hold values from -0.078125 to 0.078125
- w_down: bfloat16 [16, 1536, 5120], P('exp', None, 'ctx'), may hold values from -0.15625 to 0.15625
Outputs:
- attention_out: bfloat16 [2048, 65536], P(('ctx', 'exp'))
- moe_output: bfloat16 [256, 5120], P('exp', 'ctx')
Inputs may be any that keep to these rules, and one draw needn't show every extreme that they name: `offsets`: the query blocks start at distinct positions 3072 + k * 4, one block for each k. `routes`: each row names 6 different experts; the 32 rows of one index of exp name no expert more than 16 times, and in every draw some expert is named exactly 16 times there.
All inputs are finite; a program needn't handle non-finite values.
Results may differ from a plain program's by a relative error of at most 0.0075.
Values may be sent and summed in bfloat16 or wider, within the bound.
No kernel may reach another device: no remote copies, remote signals or barrier semaphores. Data moves between devices by JAX's collectives and lax.ppermute only.
A program may use at most 64 MiB of HBM per device.

v0:
```python
import math

import jax
import jax.numpy as jnp
from jax import lax
from jax.sharding import PartitionSpec as P

H = 128
LAT = 512
ROPE = 64
TOPK = 6
EXPERTS = 16
CAP = 16


softmax_scale = 192.0 ** (-0.5)


def attend_keys(status, query_rows, query_pos, key_block, first_key):
    running_max, denominators, accumulated = status
    scores = (
        lax.dot_general(
            query_rows, key_block, (((1,), (1,)), ((), ())), preferred_element_type=jnp.float32
        )
        * softmax_scale
    )
    key_pos = first_key + lax.iota(jnp.int32, key_block.shape[0])
    scores = jnp.where(key_pos[None, :] <= query_pos[:, None], scores, -jnp.inf)
    new_max = jnp.maximum(running_max, jnp.max(scores, axis=1))
    rescale = jnp.exp(running_max - new_max)
    weights = jnp.exp(scores - new_max[:, None])
    denominators = denominators * rescale + jnp.sum(weights, axis=1)
    rounded = weights.astype(jnp.bfloat16)
    accumulated = accumulated * rescale[:, None] + jnp.dot(
        rounded, key_block[:, :LAT], preferred_element_type=jnp.float32
    )
    return (new_max, denominators, accumulated)


def local(queries, latents, offsets, moe_input, routes, gate_values, w_gate, w_up, w_down):
    width_all = LAT + ROPE
    row_count = queries.shape[0] * H
    query_rows = queries.reshape(row_count, width_all)
    query_pos = offsets[0] + lax.iota(jnp.int32, row_count) // H
    start_state = (
        jnp.full((row_count,), -1e30, jnp.float32),
        jnp.zeros((row_count,), jnp.float32),
        jnp.zeros((row_count, LAT), jnp.float32),
    )
    every_key = lax.all_gather(latents, "ctx", axis=0, tiled=True)
    status = start_state
    key_count = every_key.shape[0]
    span_rows = math.gcd(key_count, 640)
    stacked = every_key.reshape(key_count // span_rows, span_rows, width_all)
    firsts = 0 + span_rows * lax.iota(jnp.int32, key_count // span_rows)

    def advance(carried, inputs):
        return (attend_keys(carried, query_rows, query_pos, inputs[0], inputs[1]), None)

    status, unused = lax.scan(advance, status, (stacked, firsts))
    attention_out = (
        (status[2] / status[1][:, None]).astype(jnp.bfloat16).reshape(queries.shape[0], H * LAT)
    )
    token_count = moe_input.shape[0]
    local_width = moe_input.shape[1]
    held_experts = w_gate.shape[0]
    owner_count = lax.axis_size("exp")
    chosen = routes.reshape(-1)
    one_hot = (chosen[:, None] == lax.iota(jnp.int32, EXPERTS)[None, :]).astype(jnp.int32)
    earlier = jnp.cumsum(one_hot, axis=0) - one_hot
    slot_rank = jnp.sum(earlier * one_hot, axis=1)
    slot_index = chosen * CAP + slot_rank
    placed = (slot_index[:, None] == lax.iota(jnp.int32, EXPERTS * CAP)[None, :]).reshape(
        token_count, TOPK, EXPERTS * CAP
    )
    selector = jnp.any(placed, axis=1).astype(jnp.bfloat16)
    outgoing = lax.dot_general(
        selector, moe_input, (((0,), (0,)), ((), ())), preferred_element_type=jnp.float32
    ).astype(jnp.bfloat16)
    outgoing = outgoing.reshape(owner_count, held_experts * CAP, local_width)
    arrived = lax.all_to_all(outgoing, "exp", split_axis=0, concat_axis=0, tiled=True)
    arrived = arrived.reshape(owner_count, held_experts, CAP, local_width)
    gate_part = jnp.einsum("secd,edf->secf", arrived, w_gate, preferred_element_type=jnp.float32)
    up_part = jnp.einsum("secd,edf->secf", arrived, w_up, preferred_element_type=jnp.float32)
    gate_full, up_full = lax.psum((gate_part, up_part), "ctx")
    hidden = (jax.nn.silu(gate_full) * up_full).astype(jnp.bfloat16)
    result = jnp.einsum(
        "secf,efd->secd", hidden, w_down, preferred_element_type=jnp.float32
    ).astype(jnp.bfloat16)
    returned = lax.all_to_all(
        result.reshape(owner_count, held_experts * CAP, local_width),
        "exp",
        split_axis=0,
        concat_axis=0,
        tiled=True,
    )
    combine_weights = jnp.sum(placed.astype(jnp.float32) * gate_values[:, :, None], axis=1)
    moe_output = jnp.dot(
        combine_weights,
        returned.reshape(EXPERTS * CAP, local_width).astype(jnp.float32),
        precision=lax.Precision.HIGHEST,
    ).astype(jnp.bfloat16)
    return (attention_out, moe_output)


def solution(mesh):
    return jax.shard_map(
        local,
        mesh=mesh,
        in_specs=(
            P(("ctx", "exp"), None),
            P("ctx", None),
            P(("ctx", "exp")),
            P("exp", "ctx"),
            P("exp", None),
            P("exp", None),
            P("exp", "ctx", None),
            P("exp", "ctx", None),
            P("exp", None, "ctx"),
        ),
        out_specs=(P(("ctx", "exp"), None), P("exp", "ctx")),
        check_vma=False,
    )
```

profile of v0, /device:TPU:1, one launch (start us, length us, event | category | flops | bytes accessed | tf_op | source)
XLA Modules:
  0.0 1112.9 jit_solution(16454965004257364846)
XLA Ops:
  7.2 0.8 copy.30
  9.3 0.7 multiply_add_fusion
  10.1 0.9 convolution_convert_fusion.1
  11.1 14.3 %all_to_all.10 = bf16[8,32,80]{2,1,0:T(8,128)(2,1)S(1)} all-to-all(bf16[8,32,80]{2,1,0:T(8,128)(2,1)S(1)} %bitcast.64), channel_id=1, replica_groups=mesh['ctx'=64,'exp'=8] {'exp'}, dimensions={0} | all-to-all | bytes 81920 | tf_op jit(solution)/shard_map/all_to_all | solution.py:81
  25.5 1.5 convolution_bitcast_fusion
  27.0 1.5 convolution_bitcast_fusion.1
  28.6 0.7 all-gather.2.cloned.1.call-update
  29.5 0.7 reshape.65
  30.3 808.6 %all-reduce.4.cloned.1.call-done = (f32[8,2,16,1536]{3,2,0,1:T(8,128)}, f32[8,2,16,1536]{3,2,0,1:T(8,128)}) async-done(((f32[8,2,16,1536]{3,2,0,1:T(8,128)}, f32[8,2,16,1536]{3,2,0,1:T(8,128)}), (f32[8,2,16,1536]{3,2,0,1:T(8,128)}, f32[8,2,16,1536]{3,2,0,1:T(8,128)})) %all-reduce.4.cloned.1.call-update) | async-done | bytes 3145744 | tf_op jit(solution)/shard_map/psum | solution.py:85
  839.0 2.4 fusion.14
  842.0 47.9 %all-to-all-start.1 = ((bf16[8,32,80]{2,1,0:T(8,128)(2,1)}), bf16[8,32,80]{2,1,0:T(8,128)(2,1)S(1)}, u32[]{:S(2)}, u32[]{:S(2)}) async-start(bf16[8,32,80]{2,1,0:T(8,128)(2,1)} %bitcast.14), calls=%async_computation.1 | async-start | bytes 131072 | tf_op jit(solution)/shard_map/all_to_all | solution.py:90
  890.0 5.1 all-to-all-done.1
  895.1 0.8 convolution_convert_fusion.2
  895.8 153.5 %all-gather.2.cloned.1.call-done = bf16[5120,576]{1,0:T(8,128)(2,1)} async-done(((bf16[80,576]{1,0:T(8,128)(2,1)}), bf16[5120,576]{1,0:T(8,128)(2,1)}) %all-gather.2.cloned.1.call-update) | async-done | bytes 5898256 | tf_op jit(solution)/shard_map/all_gather | solution.py:50
  1049.3 54.3 %while.15 = (s32[]{:T(128)}, f32[512]{0:T(512)S(1)}, f32[512]{0:T(512)S(1)}, f32[512,512]{1,0:T(8,128)}, s32[8]{0:T(128)S(1)}, /*index=5*/bf16[8,640,576]{2,1,0:...) while((s32[]{:T(128)}, f32[512]{0:T(512)S(1)}, f32[512]{0:T(512)S(1)}, ...), condition=%wide.region_3.4_spmd.clone, body=%wide.region_0.3_spmd.clone.sunk | while | flops 716447360 | bytes 17917128 | solution.py:60
  1049.3 1.2 dynamic-slice_bitcast_fusion.2
  1050.5 0.7 fusion.43
  1051.8 0.6 iota_add_fusion.2
  1052.4 0.7 fusion.44
  1053.4 0.9 copy-done.1
  1055.0 1.0 copy-done.2
  1056.1 1.2 dynamic-slice_bitcast_fusion.2
  1057.3 0.7 fusion.43
  1058.5 0.6 iota_add_fusion.2
  1059.2 0.7 fusion.44
  1060.2 0.9 copy-done.1
  1061.8 1.0 copy-done.2
  1062.9 1.2 dynamic-slice_bitcast_fusion.2
  1064.1 0.7 fusion.43
  1065.3 0.6 iota_add_fusion.2
  1066.0 0.7 fusion.44
  1067.0 0.9 copy-done.1
  1068.6 1.0 copy-done.2
  1069.6 1.2 dynamic-slice_bitcast_fusion.2
  1070.9 0.7 fusion.43
  1072.1 0.6 iota_add_fusion.2
  1072.8 0.7 fusion.44
  1073.8 0.9 copy-done.1
  1075.4 1.0 copy-done.2
  1076.4 1.2 dynamic-slice_bitcast_fusion.2
  1077.6 0.7 fusion.43
  1078.9 0.6 iota_add_fusion.2
  1079.5 0.7 fusion.44
  1080.6 0.9 copy-done.1
  1082.2 1.0 copy-done.2
  1083.2 1.2 dynamic-slice_bitcast_fusion.2
  1084.4 0.7 fusion.43
  1085.7 0.6 iota_add_fusion.2
  1086.3 0.7 fusion.44
  1087.3 0.9 copy-done.1
  1088.9 1.0 copy-done.2
  1090.0 1.2 dynamic-slice_bitcast_fusion.2
  1091.2 0.7 fusion.43
  1092.5 0.6 iota_add_fusion.2
  1093.1 0.7 fusion.44
  1094.1 0.9 copy-done.1
  1095.7 1.0 copy-done.2
  1096.8 1.2 dynamic-slice_bitcast_fusion.2
  1098.0 0.7 fusion.43
  1099.9 0.7 fusion.44
  1100.9 0.9 copy-done.1
  1102.5 1.0 copy-done.2
  1103.6 1.4 divide_convert_fusion
  1104.9 1.2 reshape.66
  (97 shorter events, 15.1 us)
Async XLA Ops:
  7.2 18.3 %copy-start = (bf16[2,80,1536]{2,1,0:T(8,128)(2,1)S(1)}, bf16[2,80,1536]{2,1,0:T(8,128)(2,1)}, u32[]{:S(2)}) copy-start(bf16[2,80,1536]{2,1,0:T(8,128)(2,1)} %param.18) | copy-start | bytes 1474564
  7.2 19.8 %copy-start.4 = (bf16[2,80,1536]{2,1,0:T(8,128)(2,1)S(1)}, bf16[2,80,1536]{2,1,0:T(8,128)(2,1)}, u32[]{:S(2)}) copy-start(bf16[2,80,1536]{2,1,0:T(8,128)(2,1)} %param.17) | copy-start | bytes 1474564
  7.2 831.8 %all-reduce.4.cloned.1.call-start = ((), (), s32[]{:S(2)}) async-start(), calls=%async_computation.3 | async-start | bytes 6291456 | tf_op jit(solution)/shard_map/psum | solution.py:85
  28.5 1.1 copy-start.3
  28.5 1.7 copy-start.5
  28.5 810.5 %copy-start.6 = (bf16[2,1536,80]{1,2,0:T(8,128)(2,1)S(1)}, bf16[2,1536,80]{1,2,0:T(8,128)(2,1)}, u32[]{:S(2)}) copy-start(bf16[2,1536,80]{1,2,0:T(8,128)(2,1)} %param.19) | copy-start | bytes 1474564
  28.5 1020.8 %all-gather.2.cloned.1.call-start = ((), (), s32[]{:S(2)}) async-start(), calls=%async_computation.2 | async-start | bytes 6656000 | tf_op jit(solution)/shard_map/all_gather | solution.py:50
  842.0 53.0 %all-to-all-start.1 = ((bf16[8,32,80]{2,1,0:T(8,128)(2,1)}), bf16[8,32,80]{2,1,0:T(8,128)(2,1)S(1)}, u32[]{:S(2)}, u32[]{:S(2)}) async-start(bf16[8,32,80]{2,1,0:T(8,128)(2,1)} %bitcast.14), calls=%async_computation.1 | async-start | bytes 131072 | tf_op jit(solution)/shard_map/all_to_all | solution.py:90
  1053.2 1.2 copy-start.1
  1055.0 1.0 copy-start.2
  1059.9 1.2 copy-start.1
  1061.8 1.0 copy-start.2
  1066.7 1.2 copy-start.1
  1068.6 1.0 copy-start.2
  1073.5 1.2 copy-start.1
  1075.4 1.0 copy-start.2
  1080.3 1.2 copy-start.1
  1082.2 1.0 copy-start.2
  1087.1 1.2 copy-start.1
  1088.9 1.0 copy-start.2
  1093.8 1.2 copy-start.1
  1095.7 1.0 copy-start.2
  1100.6 1.2 copy-start.1
  1102.5 1.0 copy-start.2
Sparse Core Ops, SparseCore 0:
  28.6 810.2 all-reduce.3
  844.0 205.2 all-gather.1
where the time goes:
time: 1120 us; the launch traced here: 1110 us
  waiting for transfers between devices  968 us (86%)
  starting transfers between devices  48 us (4%)
  local copies, waits for them, and re-layouts  34.5 us (3%)
  matrix products  18.1 us (2%)
  other arithmetic  15.5 us (1%)
  blocking collectives  14.3 us (1%)
  between operations  14.2 us (1%)
    psum x1, waiting for transfers between devices, local(): gate_full, up_full = lax.psum((gate_part, up_part), 'ctx')  809 us
    all_gather x1, waiting for transfers between devices, local(): every_key = lax.all_gather(latents, 'ctx', axis=0, tiled=True)  153 us
    all_to_all x1, starting transfers between devices, local(): lax.all_to_all(result.reshape(owner_count, held_experts * CAP, local_widt...  47.9 us
  transfers between devices with their start and end apart: 3, of which 3 were waited for; matrix products, arithmetic and copies ran while one was open for 0% of the time, Pallas kernels for 0%

commit v1 on v0

v1 whole, which is shorter than its diff:
```python
import functools
import math

import jax
import jax.numpy as jnp
from jax import lax
from jax.experimental import pallas as pl
from jax.experimental.pallas import tpu as pltpu
from jax.sharding import Mesh, PartitionSpec as P

H = 128
LAT = 512
ROPE = 64
WIDE = LAT + ROPE
TOPK = 6
EXPERTS = 16
CAP = 16
KEYS = 512

SCALE_LOG2 = 192.0 ** (-0.5) * math.log2(math.e)
F32 = jnp.float32
BF16 = jnp.bfloat16


def attention_kernel(off_ref, q_ref, pos_ref, mine_ref, other_ref, out_ref, top_ref, den_ref, acc_ref):
    rows = q_ref.shape[0]
    row_pos = off_ref[0] + lax.broadcasted_iota(jnp.int32, (rows, 1), 0) // H
    top_ref[...] = jnp.full_like(top_ref, -1e30)
    den_ref[...] = jnp.zeros_like(den_ref)
    acc_ref[...] = jnp.zeros_like(acc_ref)

    def step(keys_ref, base, i):
        keys = keys_ref[pl.ds(i * KEYS, KEYS), :]
        key_pos = pos_ref[:, pl.ds(base + i * KEYS, KEYS)]
        half = rows // 2
        for r in range(2):
            at = pl.ds(r * half, half)
            scores = lax.dot_general(
                q_ref[at, :], keys, (((1,), (1,)), ((), ())), preferred_element_type=F32
            )
            allowed = key_pos <= row_pos[r * half : (r + 1) * half]
            scores = jnp.where(allowed, scores * SCALE_LOG2, -jnp.inf)
            old = top_ref[at, :1]
            new = jnp.maximum(old, jnp.max(scores, axis=1, keepdims=True))
            shrink = jnp.exp2(old - new)
            weights = jnp.exp2(scores - new)
            den_ref[at, :1] = den_ref[at, :1] * shrink + jnp.sum(weights, axis=1, keepdims=True)
            top_ref[at, :1] = new
            acc_ref[at, :] = acc_ref[at, :] * shrink + jnp.dot(
                weights.astype(BF16), keys[:, :LAT], preferred_element_type=F32
            )

    count = mine_ref.shape[0] // KEYS

    @pl.loop(0, count)
    def _(i):
        step(mine_ref, 0, i)

    @pl.loop(0, count)
    def _(i):
        step(other_ref, mine_ref.shape[0], i)

    out_ref[...] = (acc_ref[...] / den_ref[:, :1]).astype(BF16)


def attend(offset, query_rows, key_pos, mine, other):
    rows = query_rows.shape[0]
    vmem = pl.BlockSpec(memory_space=pltpu.VMEM)
    return pl.pallas_call(
        attention_kernel,
        out_shape=jax.ShapeDtypeStruct((rows, LAT), BF16),
        in_specs=[pl.BlockSpec(memory_space=pltpu.SMEM)] + [vmem] * 4,
        out_specs=vmem,
        scratch_shapes=[
            pltpu.VMEM((rows, 128), F32),
            pltpu.VMEM((rows, 128), F32),
            pltpu.VMEM((rows, LAT), F32),
        ],
        compiler_params=pltpu.CompilerParams(vmem_limit_bytes=40 * 2**20),
        cost_estimate=pl.CostEstimate(
            flops=2 * rows * 5120 * (WIDE + LAT), bytes_accessed=8 * 2**20, transcendentals=rows * 5120
        ),
        name="attend",
    )(offset, query_rows, key_pos, mine, other)


def exchange(array, axes):
    return lax.all_to_all(array, axes, split_axis=0, concat_axis=0, tiled=False)


def spread(array, axes, count):
    return exchange(jnp.broadcast_to(array[None], (count,) + array.shape), axes)


def ring(axis, size, by):
    return [(i, (i + by) % size) for i in range(size)]


def local(queries, latents, offsets, moe_input, routes, gate_values, w_gate, w_up, w_down):
    nz, nh, nx, nl, nc = (lax.axis_size(a) for a in ("z", "h", "x", "l", "c"))
    core = lax.axis_index("c")
    x_at = lax.axis_index("x")
    deep = nz * nh
    owners = nl * nc
    held = w_gate.shape[0]
    tokens, feats = moe_input.shape
    units = w_gate.shape[2] // nx
    slots = held * CAP

    own = latents.shape[0] // nc
    half = lax.dynamic_slice_in_dim(latents, core * own, own, 0)
    column = spread(half, ("z", "h"), deep)
    column = column.reshape(deep * own, WIDE)

    both = jnp.concatenate(
        [w_gate.reshape(held, feats, nx, units), w_up.reshape(held, feats, nx, units)], axis=3
    )
    both = exchange(both.transpose(2, 0, 1, 3), "x")
    down = w_down.transpose(0, 2, 1).reshape(held, feats, nx, units).transpose(2, 0, 1, 3)
    down = exchange(down, "x")

    one_hot = jnp.any(routes[:, :, None] == lax.iota(jnp.int32, EXPERTS), axis=1)
    before = lax.iota(jnp.int32, tokens)[None, :] < lax.iota(jnp.int32, tokens)[:, None]
    rank = jnp.dot(before.astype(BF16), one_hot.astype(BF16), preferred_element_type=F32).astype(jnp.int32)
    placed = one_hot[:, :, None] & (rank[:, :, None] == lax.iota(jnp.int32, CAP))
    placed = placed.reshape(tokens, EXPERTS * CAP)
    outgoing = lax.dot_general(
        placed.astype(BF16), moe_input, (((0,), (0,)), ((), ())), preferred_element_type=F32
    ).astype(BF16)
    outgoing = jnp.broadcast_to(outgoing.reshape(1, owners, slots, feats), (nx, owners, slots, feats))
    arrived = exchange(outgoing.reshape(nx * owners, slots, feats), ("x", "l", "c"))
    arrived = arrived.reshape(nx, owners, held, CAP, feats)
    rows_in = arrived.transpose(2, 1, 3, 0, 4).reshape(held, owners * CAP, nx * feats)
    matrix = both.transpose(1, 0, 2, 3).reshape(held, nx * feats, 2 * units)
    parts = jnp.einsum("erk,ekf->erf", rows_in, matrix, preferred_element_type=F32).astype(BF16)
    parts = exchange(parts.reshape(deep, held * owners * CAP // deep, 2 * units), ("z", "h"))
    sums = jnp.sum(parts.astype(F32), axis=0)
    hidden = (jax.nn.silu(sums[:, :units]) * sums[:, units:]).astype(BF16)
    hidden = spread(hidden, ("z", "h"), deep).reshape(held, owners * CAP, units)
    result = jnp.einsum("eru,xedu->xerd", hidden, down, preferred_element_type=F32).astype(BF16)
    result = result.reshape(nx, held, owners, CAP, feats).transpose(0, 2, 1, 3, 4)
    back = exchange(result.reshape(nx * owners, slots, feats), ("x", "l", "c"))
    back = jnp.sum(back.reshape(nx, owners * slots, feats).astype(F32), axis=0).astype(BF16)
    share = jnp.sum(
        jnp.where(routes[:, :, None] == lax.iota(jnp.int32, EXPERTS), gate_values[:, :, None], 0.0), axis=1
    )
    weights = placed.astype(F32) * jnp.repeat(share, CAP, axis=1)
    moe_output = jnp.dot(weights, back.astype(F32), precision=lax.Precision.HIGHEST).astype(BF16)

    piece = column.shape[0]
    near = lax.ppermute(column, "x", ring("x", nx, 1))
    far = lax.ppermute(column, "x", ring("x", nx, -1))
    low = lax.ppermute(near[: piece // 2], "x", ring("x", nx, 1))
    high = lax.ppermute(far[piece // 2 :], "x", ring("x", nx, -1))
    mine = jnp.concatenate([column, near, far, low, high], axis=0)
    other = lax.ppermute(mine, "c", ring("c", nc, 1))

    sources = jnp.stack([x_at, x_at + nx - 1, x_at + 1, x_at + 2]) % nx
    at_z = lax.iota(jnp.int32, deep)
    first = (at_z[None, :] * nx + sources[:, None]) * latents.shape[0]
    place = first[:, :, None] + lax.iota(jnp.int32, own)
    key_pos = jnp.stack([place + core * own, place + (nc - 1 - core) * own]).reshape(1, -1)

    query_rows = queries.reshape(queries.shape[0] * H, WIDE)
    mixed = attend(offsets, query_rows, key_pos, mine, other)
    attention_out = mixed.reshape(queries.shape[0], H * LAT)
    return (attention_out, moe_output)


def solution(mesh):
    fine = Mesh(mesh.devices.reshape(8, 2, 4, 4, 2), ("z", "h", "x", "l", "c"))
    ctx, exp = ("z", "h", "x"), ("l", "c")
    return jax.shard_map(
        local,
        mesh=fine,
        in_specs=(
            P(ctx + exp, None),
            P(ctx, None),
            P(ctx + exp),
            P(exp, ctx),
            P(exp, None),
            P(exp, None),
            P(exp, ctx, None),
            P(exp, ctx, None),
            P(exp, None, ctx),
        ),
        out_specs=(P(ctx + exp, None), P(exp, ctx)),
        check_vma=False,
    )
```

time: 1120 us -> 227 us (0.20)
  waiting for transfers between devices: 968 us -> 67 us
  starting transfers between devices: 48 us -> 85.4 us
  Pallas kernels: 0 us -> 15.4 us
  blocking collectives: 14.3 us -> 0 us
  matrix products: 18.1 us -> 4.67 us
  between operations: 14.2 us -> 1.64 us
    psum x1 -> x0, waiting for transfers between devices: 809 us -> none  [local(): gate_full, up_full = lax.psum((gate_part, up_part), 'ctx')]
    all_gather x1 -> x0, waiting for transfers between devices: 153 us -> none  [local(): every_key = lax.all_gather(latents, 'ctx', axis=0, tiled=True)]
    all_to_all x1 -> x7, waiting for transfers between devices: 5.1 us -> 60.1 us  [exchange(): return lax.all_to_all(array, axes, split_axis=0, concat_axis=0, tiled=False)]
    all_to_all x1 -> x7, starting transfers between devices: 47.9 us -> 69.7 us  [exchange(): return lax.all_to_all(array, axes, split_axis=0, concat_axis=0, tiled=False)]
    while x40 -> x0, local copies, waits for them, and re-layouts: 15.9 us -> none
    ppermute x0 -> x5, starting transfers between devices: none -> 15.7 us  [the longest x1 3.37 us: local(): far = lax.ppermute(column, 'x', ring('x', nx, -1))]
    pallas_call x0 -> x1, Pallas kernels: none -> 15.4 us  [attend(): pl.pallas_call(attention_kernel, out_shape=jax.ShapeDtypeStruct((rows, LA...]
    all_to_all x1 -> x0, blocking collectives: 14.3 us -> none  [local(): lax.all_to_all(outgoing, 'exp', split_axis=0, concat_axis=0, tiled=True)]
  transfers between devices with their start and end apart: 3 -> 12, of which waited for: 3 -> 7; matrix products, arithmetic and copies ran while one was open for 0% -> 18% of each run, Pallas kernels for 0% -> 0%
where the time goes in v1:
time: 227 us; the launch traced here: 225 us
  starting transfers between devices  85.4 us (38%)
  waiting for transfers between devices  67 us (30%)
  local copies, waits for them, and re-layouts  44.3 us (20%)
  Pallas kernels  15.4 us (7%)
  other arithmetic  6.27 us (3%)
  matrix products  4.67 us (2%)
    all_to_all x7, starting transfers between devices, exchange(): return lax.all_to_all(array, axes, split_axis=0, concat_axis=0, tiled=False)  69.7 us
    all_to_all x7, waiting for transfers between devices, exchange(): return lax.all_to_all(array, axes, split_axis=0, concat_axis=0, tiled=False)  60.1 us
    pallas_call x1, Pallas kernels, attend(): pl.pallas_call(attention_kernel, out_shape=jax.ShapeDtypeStruct((rows, LA...  15.4 us
    unnamed x26, local copies, waits for them, and re-layouts  9.68 us
    ppermute x1, waiting for transfers between devices, local(): low = lax.ppermute(near[:piece // 2], 'x', ring('x', nx, 1))  6.88 us
    ppermute x1, local copies, waits for them, and re-layouts, local(): other = lax.ppermute(mine, 'c', ring('c', nc, 1))  4.7 us
  transfers between devices with their start and end apart: 12, of which 7 were waited for; matrix products, arithmetic and copies ran while one was open for 18% of the time, Pallas kernels for 0%

profile of v1, /device:TPU:1, one launch (start us, length us, event | category | flops | bytes accessed | tf_op | source)
XLA Modules:
  0.0 224.7 jit_solution(15648076655142859117)
XLA Ops:
  0.7 0.8 copy-done
  1.5 1.0 broadcast_in_dim.18
  2.5 16.2 %all-to-all-start = ((bf16[16,40,576]{2,1,0:T(8,128)(2,1)}), bf16[16,40,576]{2,1,0:T(8,128)(2,1)S(1)}, u32[]{:S(2)}, u32[]{:S(2)}) async-start(bf16[16,40,576]{2,1,0:T(8,128)(2,1)} %broadcast_in_dim.18), calls=%async_computation | async-start | bytes 1638400 | tf_op jit(solution)/shard_map/all_to_all | solution.py:88
  18.7 0.7 fusion.3
  19.4 17.5 %all-to-all-done = bf16[16,40,576]{2,1,0:T(8,128)(2,1)S(1)} async-done(((bf16[16,40,576]{2,1,0:T(8,128)(2,1)}), bf16[16,40,576]{2,1,0:T(8,128)(2,1)S(1)}, u32[]{:S(2)}, u32[]{:S(2)}) %all-to-all-start) | async-done | bytes 737312 | tf_op jit(solution)/shard_map/all_to_all | solution.py:88
  36.9 1.2 copy.64
  38.1 3.1 %collective-permute-start = (bf16[640,576]{0,1:T(8,128)(2,1)}, bf16[640,576]{0,1:T(8,128)(2,1)}, u32[]{:S(2)}, u32[]{:S(2)}) collective-permute-start(bf16[640,576]{0,1:T(8,128)(2,1)} %copy.64), channel_id=1, source_target_pairs={{0,8},{8,16},{16,24},{24,0},{1,9},{9,17},{17,25},{25,1},{2,10},{10... | collective-permute-start | bytes 2211848 | tf_op jit(solution)/shard_map/ppermute | solution.py:151
  41.2 3.4 %collective-permute-start.1 = (bf16[640,576]{0,1:T(8,128)(2,1)}, bf16[640,576]{0,1:T(8,128)(2,1)}, u32[]{:S(2)}, u32[]{:S(2)}) collective-permute-start(bf16[640,576]{0,1:T(8,128)(2,1)} %copy.64), channel_id=1, source_target_pairs={{0,24},{8,0},{16,8},{24,16},{1,25},{9,1},{17,9},{25,17},{2,26},{10... | collective-permute-start | bytes 2211848 | tf_op jit(solution)/shard_map/ppermute | solution.py:152
  44.6 0.1 convolution_convert_fusion.4
  44.9 0.2 convolution_convert_fusion.2
  45.1 0.1 copy.72
  45.3 0.7 broadcast_in_dim.23
  46.0 21.7 %all-to-all-start.1 = ((bf16[32,32,80]{2,1,0:T(8,128)(2,1)}), bf16[32,32,80]{2,1,0:T(8,128)(2,1)S(1)}, u32[]{:S(2)}, u32[]{:S(2)}) async-start(bf16[32,32,80]{2,1,0:T(8,128)(2,1)} %bitcast.9), calls=%async_computation.1 | async-start | bytes 524288 | tf_op jit(solution)/shard_map/all_to_all | solution.py:88
  67.8 0.1 reshape.211
  68.0 0.4 maximum_bitcast_fusion
  68.4 1.1 copy.74
  69.5 9.5 %all-to-all-done.1 = bf16[32,32,80]{2,1,0:T(8,128)(2,1)S(1)} async-done(((bf16[32,32,80]{2,1,0:T(8,128)(2,1)}), bf16[32,32,80]{2,1,0:T(8,128)(2,1)S(1)}, u32[]{:S(2)}, u32[]{:S(2)}) %all-to-all-start.1) | async-done | bytes 163872 | tf_op jit(solution)/shard_map/all_to_all | solution.py:88
  79.0 4.2 %all-to-all-start.2 = ((bf16[4,2,80,768]{3,2,1,0:T(8,128)(2,1)}), bf16[4,2,80,768]{3,2,1,0:T(8,128)(2,1)}, u32[]{:S(2)}, u32[]{:S(2)}) async-start(bf16[4,2,80,768]{3,2,1,0:T(8,128)(2,1)} %copy.74), calls=%async_computation.2 | async-start | bytes 1966080 | tf_op jit(solution)/shard_map/all_to_all | solution.py:88
  83.3 1.5 copy.68
  84.8 0.8 slice.16
  85.6 0.2 copy-done.5
  85.8 3.3 %collective-permute-start.2 = (bf16[320,576]{1,0:T(8,128)(2,1)}, bf16[320,576]{1,0:T(8,128)(2,1)}, u32[]{:S(2)}, u32[]{:S(2)}) collective-permute-start(bf16[320,576]{1,0:T(8,128)(2,1)} %slice.16), channel_id=1, source_target_pairs={{0,8},{8,16},{16,24},{24,0},{1,9},{9,17},{17,25},{25,1},{2,10},{10... | collective-permute-start | bytes 1105928 | tf_op jit(solution)/shard_map/ppermute | solution.py:153
  89.1 1.2 constant_dynamic-update-slice_fusion.4
  90.3 2.3 %copy.69 = bf16[640,576]{1,0:T(8,128)(2,1)} copy(bf16[640,576]{0,1:T(8,128)(2,1)} %collective-permute-done.1) | data formatting | bytes 1474560 | tf_op jit(solution)/shard_map/ppermute | solution.py:152
  92.7 1.0 slice.17
  93.7 3.2 %collective-permute-start.3 = (bf16[320,576]{1,0:T(8,128)(2,1)S(1)}, bf16[320,576]{1,0:T(8,128)(2,1)S(1)}, u32[]{:S(2)}, u32[]{:S(2)}) collective-permute-start(bf16[320,576]{1,0:T(8,128)(2,1)S(1)} %slice.17), channel_id=1, source_target_pairs={{0,24},{8,0},{16,8},{24,16},{1,25},{9,1},{17,9},{25,17},{2,26},{10... | collective-permute-start | bytes 1105928 | tf_op jit(solution)/shard_map/ppermute | solution.py:154
  96.9 1.3 constant_dynamic-update-slice_fusion.3
  98.2 1.3 constant_dynamic-update-slice_fusion.2
  99.4 6.9 %collective-permute-done.2 = bf16[320,576]{1,0:T(8,128)(2,1)} collective-permute-done((bf16[320,576]{1,0:T(8,128)(2,1)}, bf16[320,576]{1,0:T(8,128)(2,1)}, u32[]{:S(2)}, u32[]{:S(2)}) %collective-permute-start.2) | collective-permute-done | bytes 368672 | tf_op jit(solution)/shard_map/ppermute | solution.py:153
  106.3 1.1 constant_dynamic-update-slice_fusion.1
  107.4 2.9 %copy.70 = bf16[2560,576]{0,1:T(8,128)(2,1)} copy(bf16[2560,576]{1,0:T(8,128)(2,1)S(1)} %constant_dynamic-update-slice_fusion.mine_ref) | data formatting | bytes 5898240 | tf_op jit(solution)/shard_map/concatenate | solution.py:155
  110.4 2.7 %collective-permute-start.4 = (bf16[2560,576]{0,1:T(8,128)(2,1)}, bf16[2560,576]{0,1:T(8,128)(2,1)}, u32[]{:S(2)}, u32[]{:S(2)}) collective-permute-start(bf16[2560,576]{0,1:T(8,128)(2,1)} %copy.70), channel_id=1, source_target_pairs={{0,1},{1,0},{2,3},{3,2},{4,5},{5,4},{6,7},{7,6},{8,9},{9,8},{10,11... | collective-permute-start | bytes 8847368 | tf_op jit(solution)/shard_map/ppermute | solution.py:156
  113.1 1.9 copy.73
  115.0 1.8 reshape.210
  116.8 1.3 copy.75
  118.1 2.1 convolution_convert_fusion
  120.2 6.1 %all-to-all-start.3 = ((bf16[16,16,768]{2,1,0:T(8,128)(2,1)}), bf16[16,16,768]{2,1,0:T(8,128)(2,1)}, u32[]{:S(2)}, u32[]{:S(2)}) async-start(bf16[16,16,768]{2,1,0:T(8,128)(2,1)} %bitcast.57), calls=%async_computation.3 | async-start | bytes 786432 | tf_op jit(solution)/shard_map/all_to_all | solution.py:88
  126.2 1.9 reshape.216
  128.2 1.9 copy.77
  130.0 10.0 %all-to-all-done.3 = bf16[16,16,768]{2,1,0:T(8,128)(2,1)} async-done(((bf16[16,16,768]{2,1,0:T(8,128)(2,1)}), bf16[16,16,768]{2,1,0:T(8,128)(2,1)}, u32[]{:S(2)}, u32[]{:S(2)}) %all-to-all-start.3) | async-done | bytes 393248 | tf_op jit(solution)/shard_map/all_to_all | solution.py:88
  140.0 4.1 %all-to-all-start.5 = ((bf16[4,2,80,384]{3,2,1,0:T(8,128)(2,1)}), bf16[4,2,80,384]{3,2,1,0:T(8,128)(2,1)}, u32[]{:S(2)}, u32[]{:S(2)}) async-start(bf16[4,2,80,384]{3,2,1,0:T(8,128)(2,1)} %copy.77), calls=%async_computation.5 | async-start | bytes 983040 | tf_op jit(solution)/shard_map/all_to_all | solution.py:88
  144.2 1.1 convert_reduce_fusion
  145.2 5.8 %all-to-all-done.5 = bf16[4,2,80,384]{3,2,1,0:T(8,128)(2,1)} async-done(((bf16[4,2,80,384]{3,2,1,0:T(8,128)(2,1)}), bf16[4,2,80,384]{3,2,1,0:T(8,128)(2,1)}, u32[]{:S(2)}, u32[]{:S(2)}) %all-to-all-start.5) | async-done | bytes 491552 | tf_op jit(solution)/shard_map/all_to_all | solution.py:88
  151.0 0.7 broadcast_in_dim.24
  151.7 9.9 %all-to-all-start.4 = ((bf16[16,16,384]{2,1,0:T(8,128)(2,1)}), bf16[16,16,384]{2,1,0:T(8,128)(2,1)}, u32[]{:S(2)}, u32[]{:S(2)}) async-start(bf16[16,16,384]{2,1,0:T(8,128)(2,1)} %broadcast_in_dim.24), calls=%async_computation.4 | async-start | bytes 393216 | tf_op jit(solution)/shard_map/all_to_all | solution.py:88
  161.7 0.7 add_multiply_fusion
  162.3 11.6 %all-to-all-done.4 = bf16[16,16,384]{2,1,0:T(8,128)(2,1)} async-done(((bf16[16,16,384]{2,1,0:T(8,128)(2,1)}), bf16[16,16,384]{2,1,0:T(8,128)(2,1)}, u32[]{:S(2)}, u32[]{:S(2)}) %all-to-all-start.4) | async-done | bytes 196640 | tf_op jit(solution)/shard_map/all_to_all | solution.py:88
  173.9 1.4 fusion
  175.4 0.9 copy.79
  176.2 1.7 copy.80
  177.9 7.4 %all-to-all-start.6 = ((bf16[32,32,80]{2,1,0:T(8,128)(2,1)}), bf16[32,32,80]{2,1,0:T(8,128)(2,1)}, u32[]{:S(2)}, u32[]{:S(2)}) async-start(bf16[32,32,80]{2,1,0:T(8,128)(2,1)} %bitcast.59), calls=%async_computation.6 | async-start | bytes 524288 | tf_op jit(solution)/shard_map/all_to_all | solution.py:88
  185.3 0.8 fusion.5
  186.2 2.6 %reshape.203.q_ref = bf16[512,576]{1,0:T(8,128)(2,1)} reshape(bf16[4,73728]{1,0:T(4,128)(2,1)} %param.9) | data formatting | bytes 1179648 | tf_op jit(solution)/shard_map/reshape | solution.py:164
  189.4 0.7 select_reduce_fusion
  190.2 0.7 bitcast_select_fusion
  190.9 5.8 %all-to-all-done.6 = bf16[32,32,80]{2,1,0:T(8,128)(2,1)} async-done(((bf16[32,32,80]{2,1,0:T(8,128)(2,1)}), bf16[32,32,80]{2,1,0:T(8,128)(2,1)}, u32[]{:S(2)}, u32[]{:S(2)}) %all-to-all-start.6) | async-done | bytes 163872 | tf_op jit(solution)/shard_map/all_to_all | solution.py:88
  196.7 1.0 bitcast_reduce_fusion
  197.7 0.9 convolution_convert_fusion.3
  198.5 4.7 %copy.71.other_ref = bf16[2560,576]{1,0:T(8,128)(2,1)} copy(bf16[2560,576]{0,1:T(8,128)(2,1)} %collective-permute-done.4) | data formatting | bytes 5898240 | tf_op jit(solution)/shard_map/ppermute | solution.py:156
  203.2 1.9 copy-done.1
  205.2 1.1 copy-done.2
  206.2 15.4 %attend.1 = bf16[512,512]{1,0:T(8,128)(2,1)S(1)} custom-call(s32[1]{0:T(128)S(6)} %copy.91.off_ref, bf16[512,576]{1,0:T(8,128)(2,1)S(1)} %copy-done.2, s32[1,5120]{1,0:T(1,128)S(1)} %reshape.204.pos_ref, bf16[2560,576]{1,0:T(8,128)(2,1)S(1)} %constant_dynamic-update-slice_fusion.mine_ref, bf16[2560,576]{1,0:T(8,128)(2,1)S(1)} %copy-done.1), custom_call_target="tpu_custom_call" | custom-call | flops 5704253440 | bytes 8388608 | tf_op jit(solution)/shard_map/attend/pallas_call | solution.py:69
  221.7 0.8 copy-done.3
  222.5 2.2 reshape.206
  (33 shorter events, 0.6 us)
Async XLA Ops:
  0.6 0.9 copy-start
  0.6 44.3 %copy-start.10 = (bf16[32,80]{1,0:T(8,128)(2,1)S(1)}, bf16[32,80]{1,0:T(8,128)(2,1)}, u32[]{:S(2)}) copy-start(bf16[32,80]{1,0:T(8,128)(2,1)} %param.12) | copy-start | bytes 15364
  0.7 67.1 %copy-start.7 = (bf16[2,80,1536]{2,1,0:T(8,128)(2,1)S(1)}, bf16[2,80,1536]{2,1,0:T(8,128)(2,1)}, u32[]{:S(2)}) copy-start(bf16[2,80,1536]{2,1,0:T(8,128)(2,1)} %param.15) | copy-start | bytes 1474564
  0.7 67.2 %copy-start.8 = (bf16[2,80,1536]{2,1,0:T(8,128)(2,1)S(1)}, bf16[2,80,1536]{2,1,0:T(8,128)(2,1)}, u32[]{:S(2)}) copy-start(bf16[2,80,1536]{2,1,0:T(8,128)(2,1)} %param.16) | copy-start | bytes 1474564
  2.5 34.4 %all-to-all-start = ((bf16[16,40,576]{2,1,0:T(8,128)(2,1)}), bf16[16,40,576]{2,1,0:T(8,128)(2,1)S(1)}, u32[]{:S(2)}, u32[]{:S(2)}) async-start(bf16[16,40,576]{2,1,0:T(8,128)(2,1)} %broadcast_in_dim.18), calls=%async_computation | async-start | bytes 1638400 | tf_op jit(solution)/shard_map/all_to_all | solution.py:88
  36.9 31.5 %copy-start.4 = (bf16[16,40,576]{2,1,0:T(8,128)(2,1)}, bf16[16,40,576]{2,1,0:T(8,128)(2,1)S(1)}, u32[]{:S(2)}) copy-start(bf16[16,40,576]{2,1,0:T(8,128)(2,1)S(1)} %all-to-all-done) | copy-start | bytes 2211844
  38.1 45.2 %collective-permute-start = (bf16[640,576]{0,1:T(8,128)(2,1)}, bf16[640,576]{0,1:T(8,128)(2,1)}, u32[]{:S(2)}, u32[]{:S(2)}) collective-permute-start(bf16[640,576]{0,1:T(8,128)(2,1)} %copy.64), channel_id=1, source_target_pairs={{0,8},{8,16},{16,24},{24,0},{1,9},{9,17},{17,25},{25,1},{2,10},{10... | collective-permute-start | bytes 2211848 | tf_op jit(solution)/shard_map/ppermute | solution.py:151
  41.2 49.1 %collective-permute-start.1 = (bf16[640,576]{0,1:T(8,128)(2,1)}, bf16[640,576]{0,1:T(8,128)(2,1)}, u32[]{:S(2)}, u32[]{:S(2)}) collective-permute-start(bf16[640,576]{0,1:T(8,128)(2,1)} %copy.64), channel_id=1, source_target_pairs={{0,24},{8,0},{16,8},{24,16},{1,25},{9,1},{17,9},{25,17},{2,26},{10... | collective-permute-start | bytes 2211848 | tf_op jit(solution)/shard_map/ppermute | solution.py:152
  44.8 24.7 %copy-start.9 = (s32[256]{0:T(256)}, s32[256]{0:T(256)S(1)}, u32[]{:S(2)}) copy-start(s32[256]{0:T(256)S(1)} %eq.48) | copy-start | bytes 3076
  46.0 33.0 %all-to-all-start.1 = ((bf16[32,32,80]{2,1,0:T(8,128)(2,1)}), bf16[32,32,80]{2,1,0:T(8,128)(2,1)S(1)}, u32[]{:S(2)}, u32[]{:S(2)}) async-start(bf16[32,32,80]{2,1,0:T(8,128)(2,1)} %bitcast.9), calls=%async_computation.1 | async-start | bytes 524288 | tf_op jit(solution)/shard_map/all_to_all | solution.py:88
  79.0 6.6 %copy-start.6 = (bf16[32,32,80]{2,1,0:T(8,128)(2,1)}, bf16[32,32,80]{2,1,0:T(8,128)(2,1)S(1)}, u32[]{:S(2)}) copy-start(bf16[32,32,80]{2,1,0:T(8,128)(2,1)S(1)} %all-to-all-done.1) | copy-start | bytes 491524
  79.0 37.8 %all-to-all-start.2 = ((bf16[4,2,80,768]{3,2,1,0:T(8,128)(2,1)}), bf16[4,2,80,768]{3,2,1,0:T(8,128)(2,1)}, u32[]{:S(2)}, u32[]{:S(2)}) async-start(bf16[4,2,80,768]{3,2,1,0:T(8,128)(2,1)} %copy.74), calls=%async_computation.2 | async-start | bytes 1966080 | tf_op jit(solution)/shard_map/all_to_all | solution.py:88
  84.8 1.0 copy-start.5
  85.8 20.5 %collective-permute-start.2 = (bf16[320,576]{1,0:T(8,128)(2,1)}, bf16[320,576]{1,0:T(8,128)(2,1)}, u32[]{:S(2)}, u32[]{:S(2)}) collective-permute-start(bf16[320,576]{1,0:T(8,128)(2,1)} %slice.16), channel_id=1, source_target_pairs={{0,8},{8,16},{16,24},{24,0},{1,9},{9,17},{17,25},{25,1},{2,10},{10... | collective-permute-start | bytes 1105928 | tf_op jit(solution)/shard_map/ppermute | solution.py:153
  93.7 13.7 %collective-permute-start.3 = (bf16[320,576]{1,0:T(8,128)(2,1)S(1)}, bf16[320,576]{1,0:T(8,128)(2,1)S(1)}, u32[]{:S(2)}, u32[]{:S(2)}) collective-permute-start(bf16[320,576]{1,0:T(8,128)(2,1)S(1)} %slice.17), channel_id=1, source_target_pairs={{0,24},{8,0},{16,8},{24,16},{1,25},{9,1},{17,9},{25,17},{2,26},{10... | collective-permute-start | bytes 1105928 | tf_op jit(solution)/shard_map/ppermute | solution.py:154
  110.4 88.2 %collective-permute-start.4 = (bf16[2560,576]{0,1:T(8,128)(2,1)}, bf16[2560,576]{0,1:T(8,128)(2,1)}, u32[]{:S(2)}, u32[]{:S(2)}) collective-permute-start(bf16[2560,576]{0,1:T(8,128)(2,1)} %copy.70), channel_id=1, source_target_pairs={{0,1},{1,0},{2,3},{3,2},{4,5},{5,4},{6,7},{7,6},{8,9},{9,8},{10,11... | collective-permute-start | bytes 8847368 | tf_op jit(solution)/shard_map/ppermute | solution.py:156
  120.2 19.8 %all-to-all-start.3 = ((bf16[16,16,768]{2,1,0:T(8,128)(2,1)}), bf16[16,16,768]{2,1,0:T(8,128)(2,1)}, u32[]{:S(2)}, u32[]{:S(2)}) async-start(bf16[16,16,768]{2,1,0:T(8,128)(2,1)} %bitcast.57), calls=%async_computation.3 | async-start | bytes 786432 | tf_op jit(solution)/shard_map/all_to_all | solution.py:88
  140.0 11.0 %all-to-all-start.5 = ((bf16[4,2,80,384]{3,2,1,0:T(8,128)(2,1)}), bf16[4,2,80,384]{3,2,1,0:T(8,128)(2,1)}, u32[]{:S(2)}, u32[]{:S(2)}) async-start(bf16[4,2,80,384]{3,2,1,0:T(8,128)(2,1)} %copy.77), calls=%async_computation.5 | async-start | bytes 983040 | tf_op jit(solution)/shard_map/all_to_all | solution.py:88
  151.7 22.2 %all-to-all-start.4 = ((bf16[16,16,384]{2,1,0:T(8,128)(2,1)}), bf16[16,16,384]{2,1,0:T(8,128)(2,1)}, u32[]{:S(2)}, u32[]{:S(2)}) async-start(bf16[16,16,384]{2,1,0:T(8,128)(2,1)} %broadcast_in_dim.24), calls=%async_computation.4 | async-start | bytes 393216 | tf_op jit(solution)/shard_map/all_to_all | solution.py:88
  177.9 18.8 %all-to-all-start.6 = ((bf16[32,32,80]{2,1,0:T(8,128)(2,1)}), bf16[32,32,80]{2,1,0:T(8,128)(2,1)}, u32[]{:S(2)}, u32[]{:S(2)}) async-start(bf16[32,32,80]{2,1,0:T(8,128)(2,1)} %bitcast.59), calls=%async_computation.6 | async-start | bytes 524288 | tf_op jit(solution)/shard_map/all_to_all | solution.py:88
  203.2 1.9 copy-start.1
  205.2 1.1 copy-start.2
  221.7 0.8 copy-start.3

commit v2 on v1

v2 whole, which is shorter than its diff:
```python
import functools
import math

import jax
import jax.numpy as jnp
from jax import lax
from jax.experimental import pallas as pl
from jax.experimental.pallas import tpu as pltpu
from jax.sharding import Mesh, PartitionSpec as P

H = 128
LAT = 512
ROPE = 64
WIDE = LAT + ROPE
TOPK = 6
EXPERTS = 16
CAP = 16
LANES = 128

SCALE_LOG2 = 192.0 ** (-0.5) * math.log2(math.e)
F32 = jnp.float32
BF16 = jnp.bfloat16
I32 = jnp.int32
VMEM = pl.BlockSpec(memory_space=pltpu.VMEM)
SMEM = pl.BlockSpec(memory_space=pltpu.SMEM)


def shaped(shape, dtype):
    return jax.ShapeDtypeStruct(shape, dtype)


def kernel(body, name, out_shape, specs, args, flops, moved, special=0):
    return pl.pallas_call(
        body,
        out_shape=out_shape,
        in_specs=specs,
        out_specs=jax.tree.map(lambda _: VMEM, out_shape),
        compiler_params=pltpu.CompilerParams(vmem_limit_bytes=40 * 2**20),
        cost_estimate=pl.CostEstimate(flops=flops, bytes_accessed=moved, transcendentals=special),
        name=name,
    )(*args)


def attention_body(pieces, first, last, spots, queries, base, *refs):
    keys, refs = refs[:pieces], refs[pieces:]
    rows = queries.shape[0]
    row_pos = spots[0] + lax.broadcasted_iota(I32, (rows, 1), 0) // H
    query = queries[...]
    if first:
        top = jnp.full((rows, 1), -1e30, F32)
    else:
        top = refs[0][:, :1]
    scored = []
    for j, key in enumerate(keys):
        scores = jnp.dot(query, key[...], preferred_element_type=F32) * SCALE_LOG2
        scored.append(jnp.where(base[:1, :] <= row_pos - spots[1 + j], scores, -jnp.inf))
    new = top
    for scores in scored:
        new = jnp.maximum(new, jnp.max(scores, axis=1, keepdims=True))
    den, acc = 0.0, 0.0
    if not first:
        shrink = jnp.exp2(top - new)
        den, acc = refs[1][:, :1] * shrink, refs[2][...] * shrink
    for scores, key in zip(scored, keys):
        weights = jnp.exp2(scores - new)
        den = den + jnp.sum(weights, axis=1, keepdims=True)
        acc = acc + lax.dot_general(
            weights.astype(BF16), key[:LAT, :], (((1,), (1,)), ((), ())), preferred_element_type=F32
        )
    if last:
        refs[-1][...] = (acc / den).astype(BF16)
    else:
        refs[-3][...] = jnp.broadcast_to(new, (rows, LANES))
        refs[-2][...] = jnp.broadcast_to(den, (rows, LANES))
        refs[-1][...] = acc


def attend(spots, queries, base, pieces, state, last, name):
    rows, count = queries.shape[0], base.shape[1] * len(pieces)
    if last:
        out = shaped((rows, LAT), BF16)
    else:
        out = [shaped((rows, LANES), F32)] * 2 + [shaped((rows, LAT), F32)]
    body = functools.partial(attention_body, len(pieces), not state, last)
    specs = [SMEM] + [VMEM] * (2 + len(pieces) + len(state))
    args = (spots, queries, base, *pieces, *state)
    return kernel(body, name, out, specs, args, 4 * rows * count * WIDE, 2 * count * WIDE + 2**20, rows * count)


def dispatch_body(copies, routes, tokens, out):
    count = tokens.shape[0]
    slot = lax.broadcasted_iota(I32, (EXPERTS * CAP, count), 0)
    named = routes[0:1, :] == slot // CAP
    for k in range(1, TOPK):
        named = named | (routes[k : k + 1, :] == slot // CAP)
    hot = named.astype(F32)
    earlier = lax.broadcasted_iota(I32, (count, count), 0) < lax.broadcasted_iota(I32, (count, count), 1)
    rank = jnp.dot(hot.astype(BF16), earlier.astype(F32).astype(BF16), preferred_element_type=F32)
    placed = jnp.where(rank == (slot % CAP).astype(F32), hot, 0.0).astype(BF16)
    sent = jnp.dot(placed, tokens[...], preferred_element_type=F32).astype(BF16)
    owners = out.shape[0] // copies
    out[...] = jnp.zeros(out.shape, BF16)
    for i in range(copies):
        out[i * owners : (i + 1) * owners, :, : tokens.shape[1]] = sent.reshape(owners, -1, tokens.shape[1])


def cut_body(spots, gate, up, *outs):
    parts = len(outs)
    units = gate.shape[2] // parts
    for j, out in enumerate(outs):
        at = pl.multiple_of(lax.rem(spots[0] + j, parts) * units, LANES)
        out[:, :, :units] = gate[:, :, pl.ds(at, units)]
        out[:, :, units:] = up[:, :, pl.ds(at, units)]


def first_body(order, spots, arrived, *refs):
    weights, out = refs[:-1], refs[-1]
    held, feats = weights[0].shape[:2]
    owners = arrived.shape[0] // len(weights)
    for e in range(held):
        total = 0.0
        for j, matrix in zip(order, weights):
            at = lax.rem(spots[0] + j, len(weights)) * owners
            rows = arrived[pl.ds(at, owners), e * CAP : (e + 1) * CAP, :].reshape(owners * CAP, LANES)
            total = total + jnp.dot(rows[:, :feats], matrix[e], preferred_element_type=F32)
        out[e * owners * CAP : (e + 1) * owners * CAP, :] = total.astype(BF16)


def add_body(parts, total, rounded):
    sums = parts[0].astype(F32)
    for i in range(1, parts.shape[0]):
        sums = sums + parts[i].astype(F32)
    total[...] = sums
    rounded[...] = sums.astype(BF16)


def hidden_body(total, other, out):
    sums = total[...] + other[...].astype(F32)
    units = sums.shape[1] // 2
    gate = sums[:, :units]
    hidden = (gate / (1.0 + jnp.exp(-gate)) * sums[:, units:]).astype(BF16)
    for i in range(out.shape[0]):
        out[i] = hidden


def second_body(deep, across, hidden, down, out):
    held, feats = down.shape[0], down.shape[2]
    units = hidden.shape[2]
    group = deep // held
    owners = out.shape[0]
    out[...] = jnp.zeros(out.shape, BF16)
    for e in range(held):
        total = 0.0
        for x in range(across):
            rows = jnp.concatenate([hidden[(group * e + i) * across + x] for i in range(group)], axis=0)
            total = total + jnp.dot(rows, down[e, x * units : (x + 1) * units, :], preferred_element_type=F32)
        out[:, e * CAP : (e + 1) * CAP, :feats] = total.astype(BF16).reshape(owners, CAP, feats)


def combine_body(routes, gates, back, out):
    count, feats = out.shape
    slot = lax.broadcasted_iota(I32, (count, EXPERTS * CAP), 1)
    hot = jnp.zeros(slot.shape, F32)
    share = jnp.zeros(slot.shape, F32)
    for k in range(TOPK):
        here = routes[:, k : k + 1] == slot // CAP
        hot = jnp.where(here, 1.0, hot)
        share = share + jnp.where(here, gates[:, k : k + 1], 0.0)
    earlier = lax.broadcasted_iota(I32, (count, count), 1) < lax.broadcasted_iota(I32, (count, count), 0)
    rank = jnp.dot(earlier.astype(F32).astype(BF16), hot.astype(BF16), preferred_element_type=F32)
    share = jnp.where(rank == (slot % CAP).astype(F32), share, 0.0)
    rows = back[...].reshape(EXPERTS * CAP, LANES)[:, :feats].astype(F32)
    mixed = jnp.dot(share, rows, precision=lax.Precision.HIGHEST, preferred_element_type=F32)
    out[...] = mixed.astype(BF16)


def exchange(array, axes):
    return lax.all_to_all(array, axes, split_axis=0, concat_axis=0, tiled=False)


def shift(array, axis, by):
    size = lax.axis_size(axis)
    return lax.ppermute(array, axis, [(i, (i + by) % size) for i in range(size)])


def local(queries, latents, offsets, moe_input, routes, gate_values, w_gate, w_up, w_down):
    nz, nh, nx, nl, nc = (lax.axis_size(a) for a in ("z", "h", "x", "l", "c"))
    h_at, x_at, core = (lax.axis_index(a) for a in ("h", "x", "c"))
    owners = nl * nc
    held, feats, width = w_gate.shape
    units = width // nx
    tokens = moe_input.shape[0]
    slots = held * CAP
    where_x = x_at.astype(I32).reshape(1)

    outgoing = kernel(
        functools.partial(dispatch_body, nx), "dispatch", shaped((nx * owners, slots, LANES), BF16),
        [VMEM] * 2, (routes.T, moe_input), 2**20, 2**18,
    )
    arrived = exchange(outgoing, ("x", "l", "c"))

    own = latents.shape[0] // nc
    half = lax.dynamic_slice_in_dim(latents, core * own, own, 0)
    paired = jnp.concatenate([half, shift(half, "h", 1)], axis=0)
    column = exchange(jnp.broadcast_to(paired[None], (nz,) + paired.shape), "z")
    column = column.reshape(nz * nh * own, WIDE).T

    cut = kernel(
        cut_body, "cut", [shaped((held, feats, 2 * units), BF16)] * nx,
        [SMEM, VMEM, VMEM], (where_x, w_gate, w_up), 2**10, 2**21,
    )
    weights = [cut[0]] + [shift(cut[j], "x", j) for j in range(1, nx)]
    order = [0] + [nx - j for j in range(1, nx)]
    parts = kernel(
        functools.partial(first_body, order), "first", shaped((held * owners * CAP, 2 * units), BF16),
        [SMEM] + [VMEM] * (1 + nx), (where_x, arrived, *weights), 2**28, 2**21,
    )
    parts = exchange(parts.reshape(nz, -1, 2 * units), "z")
    rows = parts.shape[1]
    total, rounded = kernel(
        add_body, "add", [shaped((rows, 2 * units), F32), shaped((rows, 2 * units), BF16)],
        [VMEM], (parts,), 2**18, 2**19,
    )
    hidden = kernel(
        hidden_body, "hidden", shaped((nz * nx, rows, units), BF16),
        [VMEM] * 2, (total, shift(rounded, "h", 1)), 2**18, 2**20, 2**14,
    )
    hidden = exchange(hidden, ("z", "x"))
    result = kernel(
        functools.partial(second_body, nz, nx), "second", shaped((owners, slots, LANES), BF16),
        [VMEM] * 2, (hidden, w_down), 2**27, 2**21,
    )
    back = exchange(result, ("l", "c"))
    moe_output = kernel(
        combine_body, "combine", shaped((tokens, feats), BF16),
        [VMEM] * 3, (routes, gate_values, back), 2**20, 2**18,
    )

    others = [shift(column, "x", 1), shift(column, "x", -1), shift(column, "x", 2)]
    sources = [x_at, x_at + nx - 1, x_at + 1, x_at + 2]
    at_z = lax.broadcasted_iota(I32, (nz, nh, own), 0)
    at_h = (lax.broadcasted_iota(I32, (nz, nh, own), 1) + h_at) % nh
    base = ((at_z * nh + at_h) * nx * latents.shape[0] + lax.broadcasted_iota(I32, (nz, nh, own), 2)).reshape(1, -1)
    query_rows = queries.reshape(queries.shape[0] * H, WIDE)

    pieces, spots = [], []
    for piece, source in zip([column] + others, sources):
        pieces.append([piece, shift(piece, "c", 1)])
        first = (source % nx) * latents.shape[0]
        spots.append([first + core * own, first + (nc - 1 - core) * own])

    def call(which, state, last, name):
        marks = jnp.stack([offsets[0]] + [s for i in which for s in spots[i]]).astype(I32)
        return attend(marks, query_rows, base, [p for i in which for p in pieces[i]], state, last, name)

    state = call([0], [], False, "attend_own")
    state = call([1, 2], state, False, "attend_near")
    mixed = call([3], state, True, "attend_far")
    attention_out = mixed.reshape(queries.shape[0], H * LAT)
    return (attention_out, moe_output)


def solution(mesh):
    fine = Mesh(mesh.devices.reshape(8, 2, 4, 4, 2), ("z", "h", "x", "l", "c"))
    ctx, exp = ("z", "h", "x"), ("l", "c")
    return jax.shard_map(
        local,
        mesh=fine,
        in_specs=(
            P(ctx + exp, None),
            P(ctx, None),
            P(ctx + exp),
            P(exp, ctx),
            P(exp, None),
            P(exp, None),
            P(exp, ctx, None),
            P(exp, ctx, None),
            P(exp, None, ctx),
        ),
        out_specs=(P(ctx + exp, None), P(exp, ctx)),
        check_vma=False,
    )
```

time: 227 us -> 164 us (0.72)
  waiting for transfers between devices: 67 us -> 32.8 us
  local copies, waits for them, and re-layouts: 44.3 us -> 11.4 us
  starting transfers between devices: 85.4 us -> 95.9 us
  other arithmetic: 6.27 us -> 0.19 us
  Pallas kernels: 15.4 us -> 20.1 us
  matrix products: 4.67 us -> 0 us
    ppermute x5 -> x12, starting transfers between devices: 15.7 us -> 65.6 us  [shift(): lax.ppermute(array, axis, [(i, (i + by) % size) for i in range(size)])]
    all_to_all x7 -> x5, waiting for transfers between devices: 60.1 us -> 19.4 us  [exchange(): return lax.all_to_all(array, axes, split_axis=0, concat_axis=0, tiled=False)]
    all_to_all x7 -> x5, starting transfers between devices: 69.7 us -> 30.3 us  [exchange(): return lax.all_to_all(array, axes, split_axis=0, concat_axis=0, tiled=False)]
    ppermute x3 -> x0, local copies, waits for them, and re-layouts: 8.5 us -> none  [the longest x1 4.7 us: local(): other = lax.ppermute(mine, 'c', ring('c', nc, 1))]
    transpose x5 -> x0, local copies, waits for them, and re-layouts: 7.74 us -> none  [the longest x1 1.87 us: local(): w_down.transpose(0, 2, 1).reshape(held, feats, nx, units)]
    ppermute x5 -> x12, waiting for transfers between devices: 6.89 us -> 13.4 us  [shift(): lax.ppermute(array, axis, [(i, (i + by) % size) for i in range(size)])]
    reshape x6 -> x1, local copies, waits for them, and re-layouts: 5.28 us -> 0.38 us  [local(): column = column.reshape(nz * nh * own, WIDE).T]
    dot_general x5 -> x0, matrix products: 4.67 us -> none  [the longest x1 2.07 us: local(): jnp.einsum('erk,ekf->erf', rows_in, matrix, preferred_element_type=F32)]
  transfers between devices with their start and end apart: 12 -> 17, of which waited for: 7 -> 6; matrix products, arithmetic and copies ran while one was open for 18% -> 3% of each run, Pallas kernels for 0% -> 10%
where the time goes in v2:
time: 164 us; the launch traced here: 162 us
  starting transfers between devices  95.9 us (58%)
  waiting for transfers between devices  32.8 us (20%)
  Pallas kernels  20.1 us (12%)
  local copies, waits for them, and re-layouts  11.4 us (7%)
  between operations  1.72 us (1%)
    ppermute x12, starting transfers between devices, shift(): lax.ppermute(array, axis, [(i, (i + by) % size) for i in range(size)])  65.6 us
    all_to_all x5, starting transfers between devices, exchange(): return lax.all_to_all(array, axes, split_axis=0, concat_axis=0, tiled=False)  30.3 us
    pallas_call x10, Pallas kernels, kernel(): pl.pallas_call(body, out_shape=out_shape, in_specs=specs, out_specs=jax.t...  20.1 us
    all_to_all x5, waiting for transfers between devices, exchange(): return lax.all_to_all(array, axes, split_axis=0, concat_axis=0, tiled=False)  19.4 us
    ppermute x12, waiting for transfers between devices, shift(): lax.ppermute(array, axis, [(i, (i + by) % size) for i in range(size)])  13.4 us
    unnamed x27, local copies, waits for them, and re-layouts  7.66 us
  transfers between devices with their start and end apart: 17, of which 6 were waited for; matrix products, arithmetic and copies ran while one was open for 3% of the time, Pallas kernels for 10%

profile of v2, /device:TPU:1, one launch (start us, length us, event | category | flops | bytes accessed | tf_op | source)
XLA Modules:
  0.0 162.0 jit_solution(7068868399169915975)
XLA Ops:
  0.6 0.0 copy-start
  0.7 0.0 copy-start.3
  0.7 0.7 copy-done.3
  1.4 0.7 copy-done.5
  2.1 1.0 dispatch.1
  3.1 10.4 %all-to-all-start.1 = ((bf16[32,32,128]{2,1,0:T(8,128)(2,1)}), bf16[32,32,128]{2,1,0:T(8,128)(2,1)S(1)}, u32[]{:S(2)}, u32[]{:S(2)}) async-start(bf16[32,32,128]{2,1,0:T(8,128)(2,1)} %dispatch.1), calls=%async_computation.1 | async-start | bytes 524288 | tf_op jit(solution)/shard_map/all_to_all | solution.py:178
  13.6 0.0 copy-start.2
  13.6 1.0 copy-done.2
  14.6 0.1 cut.1
  14.7 4.7 %collective-permute-start.10 = (bf16[2,80,768]{2,1,0:T(8,128)(2,1)S(1)}, bf16[2,80,768]{2,1,0:T(8,128)(2,1)S(1)}, u32[]{:S(2)}, u32[]{:S(2)}) collective-permute-start(bf16[2,80,768]{2,1,0:T(8,128)(2,1)S(1)} %get-tuple-element.23), channel_id=1, source_target_pairs={{0,24},{8,0},{16,8},{24,16},{1,25},{9,1},{17,9},{25,17},{2,26},{10... | collective-permute-start | bytes 737288 | tf_op jit(solution)/shard_map/ppermute | solution.py:183
  19.4 1.9 %collective-permute-start.8 = (bf16[2,80,768]{2,1,0:T(8,128)(2,1)S(1)}, bf16[2,80,768]{2,1,0:T(8,128)(2,1)S(1)}, u32[]{:S(2)}, u32[]{:S(2)}) collective-permute-start(bf16[2,80,768]{2,1,0:T(8,128)(2,1)S(1)} %get-tuple-element.21), channel_id=1, source_target_pairs={{0,8},{8,16},{16,24},{24,0},{1,9},{9,17},{17,25},{25,1},{2,10},{10... | collective-permute-start | bytes 737288 | tf_op jit(solution)/shard_map/ppermute | solution.py:183
  21.3 3.6 %collective-permute-start.9 = (bf16[2,80,768]{2,1,0:T(8,128)(2,1)S(1)}, bf16[2,80,768]{2,1,0:T(8,128)(2,1)S(1)}, u32[]{:S(2)}, u32[]{:S(2)}) collective-permute-start(bf16[2,80,768]{2,1,0:T(8,128)(2,1)S(1)} %get-tuple-element.22), channel_id=1, source_target_pairs={{0,16},{8,24},{16,0},{24,8},{1,17},{9,25},{17,1},{25,9},{2,18},{10... | collective-permute-start | bytes 737288 | tf_op jit(solution)/shard_map/ppermute | solution.py:183
  24.9 0.4 collective-permute-done.10.refs_3_
  25.3 4.7 %collective-permute-done.8.refs_1_ = bf16[2,80,768]{2,1,0:T(8,128)(2,1)S(1)} collective-permute-done((bf16[2,80,768]{2,1,0:T(8,128)(2,1)S(1)}, bf16[2,80,768]{2,1,0:T(8,128)(2,1)S(1)}, u32[]{:S(2)}, u32[]{:S(2)}) %collective-permute-start.8) | collective-permute-done | bytes 245792 | tf_op jit(solution)/shard_map/ppermute | solution.py:183
  29.9 4.4 %collective-permute-done.9.refs_2_ = bf16[2,80,768]{2,1,0:T(8,128)(2,1)S(1)} collective-permute-done((bf16[2,80,768]{2,1,0:T(8,128)(2,1)S(1)}, bf16[2,80,768]{2,1,0:T(8,128)(2,1)S(1)}, u32[]{:S(2)}, u32[]{:S(2)}) %collective-permute-start.9) | collective-permute-done | bytes 245792 | tf_op jit(solution)/shard_map/ppermute | solution.py:183
  34.3 0.0 all-to-all-done.1.arrived
  34.3 1.3 first.1
  35.6 8.5 %all-to-all-start.2 = ((bf16[8,32,768]{2,1,0:T(8,128)(2,1)}), bf16[8,32,768]{2,1,0:T(8,128)(2,1)S(1)}, u32[]{:S(2)}, u32[]{:S(2)}) async-start(bf16[8,32,768]{2,1,0:T(8,128)(2,1)} %bitcast.12), calls=%async_computation.2 | async-start | bytes 786432 | tf_op jit(solution)/shard_map/all_to_all | solution.py:178
  44.1 4.8 %collective-permute-start = (bf16[40,576]{1,0:T(8,128)(2,1)S(1)}, bf16[40,576]{1,0:T(8,128)(2,1)S(1)}, u32[]{:S(2)}, u32[]{:S(2)}) collective-permute-start(bf16[40,576]{1,0:T(8,128)(2,1)S(1)} %constant_dynamic-slice_fusion), channel_id=1, source_target_pairs={{0,32},{32,0},{1,33},{33,1},{2,34},{34,2},{3,35},{35,3},{4,36},{36... | collective-permute-start | bytes 138248 | tf_op jit(solution)/shard_map/ppermute | solution.py:183
  48.9 4.0 %collective-permute-done = bf16[40,576]{1,0:T(8,128)(2,1)S(1)} collective-permute-done((bf16[40,576]{1,0:T(8,128)(2,1)S(1)}, bf16[40,576]{1,0:T(8,128)(2,1)S(1)}, u32[]{:S(2)}, u32[]{:S(2)}) %collective-permute-start) | collective-permute-done | bytes 46112 | tf_op jit(solution)/shard_map/ppermute | solution.py:183
  52.9 3.4 %all-to-all-done.2.parts = bf16[8,32,768]{2,1,0:T(8,128)(2,1)S(1)} async-done(((bf16[8,32,768]{2,1,0:T(8,128)(2,1)}), bf16[8,32,768]{2,1,0:T(8,128)(2,1)S(1)}, u32[]{:S(2)}, u32[]{:S(2)}) %all-to-all-start.2) | async-done | bytes 393248 | tf_op jit(solution)/shard_map/all_to_all | solution.py:178
  56.3 1.0 broadcast_in_dim.2
  57.3 3.6 %all-to-all-start = ((bf16[8,80,576]{2,1,0:T(8,128)(2,1)}), bf16[8,80,576]{2,1,0:T(8,128)(2,1)S(1)}, u32[]{:S(2)}, u32[]{:S(2)}) async-start(bf16[8,80,576]{2,1,0:T(8,128)(2,1)} %broadcast_in_dim.2), calls=%async_computation | async-start | bytes 1638400 | tf_op jit(solution)/shard_map/all_to_all | solution.py:178
  60.8 0.1 add.130
  60.9 4.8 %collective-permute-start.11 = (bf16[32,768]{1,0:T(8,128)(2,1)S(1)}, bf16[32,768]{1,0:T(8,128)(2,1)S(1)}, u32[]{:S(2)}, u32[]{:S(2)}) collective-permute-start(bf16[32,768]{1,0:T(8,128)(2,1)S(1)} %get-tuple-element.25), channel_id=1, source_target_pairs={{0,32},{32,0},{1,33},{33,1},{2,34},{34,2},{3,35},{35,3},{4,36},{36... | collective-permute-start | bytes 147464 | tf_op jit(solution)/shard_map/ppermute | solution.py:183
  65.6 16.0 %all-to-all-done = bf16[8,80,576]{2,1,0:T(8,128)(2,1)S(1)} async-done(((bf16[8,80,576]{2,1,0:T(8,128)(2,1)}), bf16[8,80,576]{2,1,0:T(8,128)(2,1)S(1)}, u32[]{:S(2)}, u32[]{:S(2)}) %all-to-all-start) | async-done | bytes 737312 | tf_op jit(solution)/shard_map/all_to_all | solution.py:178
  81.6 0.4 copy.15
  82.0 1.9 %collective-permute-start.3 = (bf16[576,640]{1,0:T(8,128)(2,1)S(1)}, bf16[576,640]{1,0:T(8,128)(2,1)}, u32[]{:S(2)}, u32[]{:S(2)}) collective-permute-start(bf16[576,640]{1,0:T(8,128)(2,1)S(1)} %bitcast.13), channel_id=1, source_target_pairs={{0,8},{8,16},{16,24},{24,0},{1,9},{9,17},{17,25},{25,1},{2,10},{10... | collective-permute-start | bytes 2211848 | tf_op jit(solution)/shard_map/ppermute | solution.py:183
  83.9 4.6 %collective-permute-start.5 = (bf16[576,640]{1,0:T(8,128)(2,1)S(1)}, bf16[576,640]{1,0:T(8,128)(2,1)}, u32[]{:S(2)}, u32[]{:S(2)}) collective-permute-start(bf16[576,640]{1,0:T(8,128)(2,1)S(1)} %bitcast.14), channel_id=1, source_target_pairs={{0,24},{8,0},{16,8},{24,16},{1,25},{9,1},{17,9},{25,17},{2,26},{10... | collective-permute-start | bytes 2211848 | tf_op jit(solution)/shard_map/ppermute | solution.py:183
  88.5 1.0 hidden.1
  89.5 4.0 %all-to-all-start.3 = ((bf16[32,32,384]{2,1,0:T(8,128)(2,1)}), bf16[32,32,384]{2,1,0:T(8,128)(2,1)S(1)}, u32[]{:S(2)}, u32[]{:S(2)}) async-start(bf16[32,32,384]{2,1,0:T(8,128)(2,1)} %hidden.1), calls=%async_computation.3 | async-start | bytes 1572864 | tf_op jit(solution)/shard_map/all_to_all | solution.py:178
  93.6 4.5 %collective-permute-start.1 = (bf16[576,640]{1,0:T(8,128)(2,1)S(1)}, bf16[576,640]{1,0:T(8,128)(2,1)}, u32[]{:S(2)}, u32[]{:S(2)}) collective-permute-start(bf16[576,640]{1,0:T(8,128)(2,1)S(1)} %bitcast.15), channel_id=1, source_target_pairs={{0,16},{8,24},{16,0},{24,8},{1,17},{9,25},{17,1},{25,9},{2,18},{10... | collective-permute-start | bytes 2211848 | tf_op jit(solution)/shard_map/ppermute | solution.py:183
  98.1 7.0 %collective-permute-start.7 = (bf16[576,640]{1,0:T(8,128)(2,1)S(1)}, bf16[576,640]{1,0:T(8,128)(2,1)}, u32[]{:S(2)}, u32[]{:S(2)}) collective-permute-start(bf16[576,640]{1,0:T(8,128)(2,1)S(1)} %bitcast.16), channel_id=1, source_target_pairs={{0,1},{1,0},{2,3},{3,2},{4,5},{5,4},{6,7},{7,6},{8,9},{9,8},{10,11... | collective-permute-start | bytes 2211848 | tf_op jit(solution)/shard_map/ppermute | solution.py:183
  105.2 0.0 collective-permute-done.3.refs_0_
  105.2 10.3 %collective-permute-start.4 = (bf16[576,640]{1,0:T(8,128)(2,1)}, bf16[576,640]{1,0:T(8,128)(2,1)}, u32[]{:S(2)}, u32[]{:S(2)}) collective-permute-start(bf16[576,640]{1,0:T(8,128)(2,1)} %collective-permute-done.3.refs_0_), channel_id=1, source_target_pairs={{0,1},{1,0},{2,3},{3,2},{4,5},{5,4},{6,7},{7,6},{8,9},{9,8},{10,11... | collective-permute-start | bytes 2211848 | tf_op jit(solution)/shard_map/ppermute | solution.py:183
  115.4 0.0 collective-permute-done.5.refs_2_
  115.5 15.6 %collective-permute-start.6 = (bf16[576,640]{1,0:T(8,128)(2,1)}, bf16[576,640]{1,0:T(8,128)(2,1)}, u32[]{:S(2)}, u32[]{:S(2)}) collective-permute-start(bf16[576,640]{1,0:T(8,128)(2,1)} %collective-permute-done.5.refs_2_), channel_id=1, source_target_pairs={{0,1},{1,0},{2,3},{3,2},{4,5},{5,4},{6,7},{7,6},{8,9},{9,8},{10,11... | collective-permute-start | bytes 2211848 | tf_op jit(solution)/shard_map/ppermute | solution.py:183
  131.2 0.0 copy-start.4
  131.2 0.7 copy-done.4
  131.9 0.1 copy.17.routes
  132.6 0.1 iota.29
  132.7 0.1 iota.30
  132.8 0.1 iota.26
  132.9 0.1 iota.27
  133.0 0.1 iota.32
  133.1 0.7 reshape.102.queries
  133.8 0.0 copy-start.11
  133.8 1.4 copy.16.down
  135.2 0.1 copy.18.gates
  135.3 0.1 stack.40.spots
  135.4 0.1 pad_add_fusion.1.spots
  135.5 0.0 collective-permute-done.1.refs_0_
  135.5 1.9 %collective-permute-start.2 = (bf16[576,640]{1,0:T(8,128)(2,1)}, bf16[576,640]{1,0:T(8,128)(2,1)}, u32[]{:S(2)}, u32[]{:S(2)}) collective-permute-start(bf16[576,640]{1,0:T(8,128)(2,1)} %collective-permute-done.1.refs_0_), channel_id=1, source_target_pairs={{0,1},{1,0},{2,3},{3,2},{4,5},{5,4},{6,7},{7,6},{8,9},{9,8},{10,11... | collective-permute-start | bytes 2211848 | tf_op jit(solution)/shard_map/ppermute | solution.py:183
  137.4 0.1 pad_add_fusion.spots
  137.5 3.8 %attend_own.1 = (f32[512,128]{1,0:T(8,128)S(1)}, f32[512,128]{1,0:T(8,128)S(1)}, f32[512,512]{1,0:T(8,128)S(1)}) custom-call(s32[3]{0:T(128)S(1)} %pad_add_fusion.1.spots, bf16[512,576]{1,0:T(8,128)(2,1)S(1)} %reshape.102.queries, s32[1,640]{1,0:T(1,128)S(1)} %multiply_add_fusion.base, bf16[576,640]{1,0:T(8,128)(2,1)S(1)} %bitcast.17, ...), custom_call_target="tpu_custom_call" | custom-call | flops 1509949440 | bytes 2523136 | tf_op jit(solution)/shard_map/attend_own/pallas_call | solution.py:33
  141.3 1.0 copy-done.6
  142.2 0.7 copy-done.8
  142.9 1.0 second.1
  143.9 3.8 %all-to-all-start.4 = ((bf16[8,32,128]{2,1,0:T(8,128)(2,1)}), bf16[8,32,128]{2,1,0:T(8,128)(2,1)S(1)}, u32[]{:S(2)}, u32[]{:S(2)}) async-start(bf16[8,32,128]{2,1,0:T(8,128)(2,1)} %second.1), calls=%async_computation.4 | async-start | bytes 131072 | tf_op jit(solution)/shard_map/all_to_all | solution.py:178
  147.7 1.2 copy-done.7
  148.9 6.9 %attend_near.1 = (f32[512,128]{1,0:T(8,128)S(1)}, f32[512,128]{1,0:T(8,128)S(1)}, f32[512,512]{1,0:T(8,128)S(1)}) custom-call(s32[5]{0:T(128)S(1)} %stack.40.spots, bf16[512,576]{1,0:T(8,128)(2,1)S(1)} %reshape.102.queries, s32[1,640]{1,0:T(1,128)S(1)} %multiply_add_fusion.base, bf16[576,640]{1,0:T(8,128)(2,1)} %collective-permute-done.3.refs_0_, ...), custom_call_target="tpu_custom_call" | custom-call | flops 3019898880 | bytes 3997696 | tf_op jit(solution)/shard_map/attend_near/pallas_call | solution.py:33
  155.8 4.0 %attend_far.1 = bf16[512,512]{1,0:T(8,128)(2,1)S(1)} custom-call(s32[3]{0:T(128)S(1)} %pad_add_fusion.spots, bf16[512,576]{1,0:T(8,128)(2,1)S(1)} %reshape.102.queries, s32[1,640]{1,0:T(1,128)S(1)} %multiply_add_fusion.base, bf16[576,640]{1,0:T(8,128)(2,1)} %collective-permute-done.1.refs_0_, bf16[576,640]{1,0:T(8,128)(2,1)} %collective-permute-done.2.refs_1_, ...), custom_call_target="tpu_custom_call" | custom-call | flops 1509949440 | bytes 2523136 | tf_op jit(solution)/shard_map/attend_far/pallas_call | solution.py:33
  159.9 1.2 reshape.104
  161.0 1.0 combine.1
  (25 shorter events, 0.1 us)
Async XLA Ops:
  0.6 43.5 %copy-start = (bf16[80,576]{1,0:T(8,128)(2,1)S(1)}, bf16[80,576]{1,0:T(8,128)(2,1)}, u32[]{:S(2)}) copy-start(bf16[80,576]{1,0:T(8,128)(2,1)} %param.10) | copy-start | bytes 276484
  0.6 12.9 %copy-start.1 = (bf16[2,80,1536]{2,1,0:T(8,128)(2,1)S(1)}, bf16[2,80,1536]{2,1,0:T(8,128)(2,1)}, u32[]{:S(2)}) copy-start(bf16[2,80,1536]{2,1,0:T(8,128)(2,1)} %gate.1) | copy-start | bytes 1474564
  0.7 0.8 copy-start.3
  1.4 0.7 copy-start.5
  3.1 31.2 %all-to-all-start.1 = ((bf16[32,32,128]{2,1,0:T(8,128)(2,1)}), bf16[32,32,128]{2,1,0:T(8,128)(2,1)S(1)}, u32[]{:S(2)}, u32[]{:S(2)}) async-start(bf16[32,32,128]{2,1,0:T(8,128)(2,1)} %dispatch.1), calls=%async_computation.1 | async-start | bytes 524288 | tf_op jit(solution)/shard_map/all_to_all | solution.py:178
  13.6 1.0 copy-start.2
  14.7 10.6 %collective-permute-start.10 = (bf16[2,80,768]{2,1,0:T(8,128)(2,1)S(1)}, bf16[2,80,768]{2,1,0:T(8,128)(2,1)S(1)}, u32[]{:S(2)}, u32[]{:S(2)}) collective-permute-start(bf16[2,80,768]{2,1,0:T(8,128)(2,1)S(1)} %get-tuple-element.23), channel_id=1, source_target_pairs={{0,24},{8,0},{16,8},{24,16},{1,25},{9,1},{17,9},{25,17},{2,26},{10... | collective-permute-start | bytes 737288 | tf_op jit(solution)/shard_map/ppermute | solution.py:183
  19.4 10.6 %collective-permute-start.8 = (bf16[2,80,768]{2,1,0:T(8,128)(2,1)S(1)}, bf16[2,80,768]{2,1,0:T(8,128)(2,1)S(1)}, u32[]{:S(2)}, u32[]{:S(2)}) collective-permute-start(bf16[2,80,768]{2,1,0:T(8,128)(2,1)S(1)} %get-tuple-element.21), channel_id=1, source_target_pairs={{0,8},{8,16},{16,24},{24,0},{1,9},{9,17},{17,25},{25,1},{2,10},{10... | collective-permute-start | bytes 737288 | tf_op jit(solution)/shard_map/ppermute | solution.py:183
  21.3 13.0 %collective-permute-start.9 = (bf16[2,80,768]{2,1,0:T(8,128)(2,1)S(1)}, bf16[2,80,768]{2,1,0:T(8,128)(2,1)S(1)}, u32[]{:S(2)}, u32[]{:S(2)}) collective-permute-start(bf16[2,80,768]{2,1,0:T(8,128)(2,1)S(1)} %get-tuple-element.22), channel_id=1, source_target_pairs={{0,16},{8,24},{16,0},{24,8},{1,17},{9,25},{17,1},{25,9},{2,18},{10... | collective-permute-start | bytes 737288 | tf_op jit(solution)/shard_map/ppermute | solution.py:183
  35.6 20.7 %all-to-all-start.2 = ((bf16[8,32,768]{2,1,0:T(8,128)(2,1)}), bf16[8,32,768]{2,1,0:T(8,128)(2,1)S(1)}, u32[]{:S(2)}, u32[]{:S(2)}) async-start(bf16[8,32,768]{2,1,0:T(8,128)(2,1)} %bitcast.12), calls=%async_computation.2 | async-start | bytes 786432 | tf_op jit(solution)/shard_map/all_to_all | solution.py:178
  44.1 8.8 %collective-permute-start = (bf16[40,576]{1,0:T(8,128)(2,1)S(1)}, bf16[40,576]{1,0:T(8,128)(2,1)S(1)}, u32[]{:S(2)}, u32[]{:S(2)}) collective-permute-start(bf16[40,576]{1,0:T(8,128)(2,1)S(1)} %constant_dynamic-slice_fusion), channel_id=1, source_target_pairs={{0,32},{32,0},{1,33},{33,1},{2,34},{34,2},{3,35},{35,3},{4,36},{36... | collective-permute-start | bytes 138248 | tf_op jit(solution)/shard_map/ppermute | solution.py:183
  57.3 24.4 %all-to-all-start = ((bf16[8,80,576]{2,1,0:T(8,128)(2,1)}), bf16[8,80,576]{2,1,0:T(8,128)(2,1)S(1)}, u32[]{:S(2)}, u32[]{:S(2)}) async-start(bf16[8,80,576]{2,1,0:T(8,128)(2,1)} %broadcast_in_dim.2), calls=%async_computation | async-start | bytes 1638400 | tf_op jit(solution)/shard_map/all_to_all | solution.py:178
  60.9 27.7 %collective-permute-start.11 = (bf16[32,768]{1,0:T(8,128)(2,1)S(1)}, bf16[32,768]{1,0:T(8,128)(2,1)S(1)}, u32[]{:S(2)}, u32[]{:S(2)}) collective-permute-start(bf16[32,768]{1,0:T(8,128)(2,1)S(1)} %get-tuple-element.25), channel_id=1, source_target_pairs={{0,32},{32,0},{1,33},{33,1},{2,34},{34,2},{3,35},{35,3},{4,36},{36... | collective-permute-start | bytes 147464 | tf_op jit(solution)/shard_map/ppermute | solution.py:183
  82.0 23.1 %collective-permute-start.3 = (bf16[576,640]{1,0:T(8,128)(2,1)S(1)}, bf16[576,640]{1,0:T(8,128)(2,1)}, u32[]{:S(2)}, u32[]{:S(2)}) collective-permute-start(bf16[576,640]{1,0:T(8,128)(2,1)S(1)} %bitcast.13), channel_id=1, source_target_pairs={{0,8},{8,16},{16,24},{24,0},{1,9},{9,17},{17,25},{25,1},{2,10},{10... | collective-permute-start | bytes 2211848 | tf_op jit(solution)/shard_map/ppermute | solution.py:183
  83.9 31.5 %collective-permute-start.5 = (bf16[576,640]{1,0:T(8,128)(2,1)S(1)}, bf16[576,640]{1,0:T(8,128)(2,1)}, u32[]{:S(2)}, u32[]{:S(2)}) collective-permute-start(bf16[576,640]{1,0:T(8,128)(2,1)S(1)} %bitcast.14), channel_id=1, source_target_pairs={{0,24},{8,0},{16,8},{24,16},{1,25},{9,1},{17,9},{25,17},{2,26},{10... | collective-permute-start | bytes 2211848 | tf_op jit(solution)/shard_map/ppermute | solution.py:183
  89.5 43.5 %copy-start.10 = (bf16[4,73728]{1,0:T(4,128)(2,1)S(1)}, bf16[4,73728]{1,0:T(4,128)(2,1)}, u32[]{:S(2)}) copy-start(bf16[4,73728]{1,0:T(4,128)(2,1)} %param.9) | copy-start | bytes 1769476
  89.5 53.4 %all-to-all-start.3 = ((bf16[32,32,384]{2,1,0:T(8,128)(2,1)}), bf16[32,32,384]{2,1,0:T(8,128)(2,1)S(1)}, u32[]{:S(2)}, u32[]{:S(2)}) async-start(bf16[32,32,384]{2,1,0:T(8,128)(2,1)} %hidden.1), calls=%async_computation.3 | async-start | bytes 1572864 | tf_op jit(solution)/shard_map/all_to_all | solution.py:178
  93.6 41.9 %collective-permute-start.1 = (bf16[576,640]{1,0:T(8,128)(2,1)S(1)}, bf16[576,640]{1,0:T(8,128)(2,1)}, u32[]{:S(2)}, u32[]{:S(2)}) collective-permute-start(bf16[576,640]{1,0:T(8,128)(2,1)S(1)} %bitcast.15), channel_id=1, source_target_pairs={{0,16},{8,24},{16,0},{24,8},{1,17},{9,25},{17,1},{25,9},{2,18},{10... | collective-permute-start | bytes 2211848 | tf_op jit(solution)/shard_map/ppermute | solution.py:183
  98.1 39.4 %collective-permute-start.7 = (bf16[576,640]{1,0:T(8,128)(2,1)S(1)}, bf16[576,640]{1,0:T(8,128)(2,1)}, u32[]{:S(2)}, u32[]{:S(2)}) collective-permute-start(bf16[576,640]{1,0:T(8,128)(2,1)S(1)} %bitcast.16), channel_id=1, source_target_pairs={{0,1},{1,0},{2,3},{3,2},{4,5},{5,4},{6,7},{7,6},{8,9},{9,8},{10,11... | collective-permute-start | bytes 2211848 | tf_op jit(solution)/shard_map/ppermute | solution.py:183
  105.2 42.5 %collective-permute-start.4 = (bf16[576,640]{1,0:T(8,128)(2,1)}, bf16[576,640]{1,0:T(8,128)(2,1)}, u32[]{:S(2)}, u32[]{:S(2)}) collective-permute-start(bf16[576,640]{1,0:T(8,128)(2,1)} %collective-permute-done.3.refs_0_), channel_id=1, source_target_pairs={{0,1},{1,0},{2,3},{3,2},{4,5},{5,4},{6,7},{7,6},{8,9},{9,8},{10,11... | collective-permute-start | bytes 2211848 | tf_op jit(solution)/shard_map/ppermute | solution.py:183
  115.5 32.2 %collective-permute-start.6 = (bf16[576,640]{1,0:T(8,128)(2,1)}, bf16[576,640]{1,0:T(8,128)(2,1)}, u32[]{:S(2)}, u32[]{:S(2)}) collective-permute-start(bf16[576,640]{1,0:T(8,128)(2,1)} %collective-permute-done.5.refs_2_), channel_id=1, source_target_pairs={{0,1},{1,0},{2,3},{3,2},{4,5},{5,4},{6,7},{7,6},{8,9},{9,8},{10,11... | collective-permute-start | bytes 2211848 | tf_op jit(solution)/shard_map/ppermute | solution.py:183
  131.2 0.7 copy-start.4
  133.8 1.5 copy-start.11
  135.5 20.4 %collective-permute-start.2 = (bf16[576,640]{1,0:T(8,128)(2,1)}, bf16[576,640]{1,0:T(8,128)(2,1)}, u32[]{:S(2)}, u32[]{:S(2)}) collective-permute-start(bf16[576,640]{1,0:T(8,128)(2,1)} %collective-permute-done.1.refs_0_), channel_id=1, source_target_pairs={{0,1},{1,0},{2,3},{3,2},{4,5},{5,4},{6,7},{7,6},{8,9},{9,8},{10,11... | collective-permute-start | bytes 2211848 | tf_op jit(solution)/shard_map/ppermute | solution.py:183
  141.3 1.0 copy-start.6
  142.2 0.7 copy-start.8
  142.9 4.8 %copy-start.9 = (f32[512,128]{1,0:T(8,128)S(1)}, f32[512,128]{1,0:T(8,128)}, u32[]{:S(2)}) copy-start(f32[512,128]{1,0:T(8,128)} %copy-done.8) | copy-start | bytes 786436
  143.9 17.1 %all-to-all-start.4 = ((bf16[8,32,128]{2,1,0:T(8,128)(2,1)}), bf16[8,32,128]{2,1,0:T(8,128)(2,1)S(1)}, u32[]{:S(2)}, u32[]{:S(2)}) async-start(bf16[8,32,128]{2,1,0:T(8,128)(2,1)} %second.1), calls=%async_computation.4 | async-start | bytes 131072 | tf_op jit(solution)/shard_map/all_to_all | solution.py:178
  147.7 1.2 copy-start.7

commit v3 on v2

--- a/solution.py
+++ b/solution.py
@@ -22,6 +22,7 @@
 BF16 = jnp.bfloat16
 I32 = jnp.int32
 VMEM = pl.BlockSpec(memory_space=pltpu.VMEM)
+AFTER = pl.BlockSpec(memory_space=pl.ANY)
 SMEM = pl.BlockSpec(memory_space=pltpu.SMEM)
 
 
@@ -35,7 +36,7 @@
         out_shape=out_shape,
         in_specs=specs,
         out_specs=jax.tree.map(lambda _: VMEM, out_shape),
-        compiler_params=pltpu.CompilerParams(vmem_limit_bytes=40 * 2**20),
+        compiler_params=pltpu.CompilerParams(vmem_limit_bytes=24 * 2**20),
         cost_estimate=pl.CostEstimate(flops=flops, bytes_accessed=moved, transcendentals=special),
         name=name,
     )(*args)
@@ -113,7 +114,12 @@
         out[:, :, units:] = up[:, :, pl.ds(at, units)]
 
 
-def first_body(order, spots, arrived, *refs):
+def pair_body(rows, after, out):
+    for i in range(out.shape[0]):
+        out[i] = rows[...]
+
+
+def first_body(order, spots, after, arrived, *refs):
     weights, out = refs[:-1], refs[-1]
     held, feats = weights[0].shape[:2]
     owners = arrived.shape[0] // len(weights)
@@ -174,6 +180,17 @@
     out[...] = mixed.astype(BF16)
 
 
+def hold(array, after):
+    return pl.pallas_call(
+        lambda array, after, out: None,
+        out_shape=shaped(array.shape, array.dtype),
+        in_specs=[AFTER] * 2,
+        out_specs=AFTER,
+        input_output_aliases={0: 0},
+        name="hold",
+    )(array, after)
+
+
 def exchange(array, axes):
     return lax.all_to_all(array, axes, split_axis=0, concat_axis=0, tiled=False)
 
@@ -202,7 +219,10 @@
     own = latents.shape[0] // nc
     half = lax.dynamic_slice_in_dim(latents, core * own, own, 0)
     paired = jnp.concatenate([half, shift(half, "h", 1)], axis=0)
-    column = exchange(jnp.broadcast_to(paired[None], (nz,) + paired.shape), "z")
+    paired = kernel(
+        pair_body, "pair", shaped((nz,) + paired.shape, BF16), [VMEM, AFTER], (paired, arrived), 2**10, 2**20
+    )
+    column = exchange(paired, "z")
     column = column.reshape(nz * nh * own, WIDE).T
 
     cut = kernel(
@@ -213,7 +233,7 @@
     order = [0] + [nx - j for j in range(1, nx)]
     parts = kernel(
         functools.partial(first_body, order), "first", shaped((held * owners * CAP, 2 * units), BF16),
-        [SMEM] + [VMEM] * (1 + nx), (where_x, arrived, *weights), 2**28, 2**21,
+        [SMEM, AFTER] + [VMEM] * (1 + nx), (where_x, column, arrived, *weights), 2**28, 2**21,
     )
     parts = exchange(parts.reshape(nz, -1, 2 * units), "z")
     rows = parts.shape[1]
@@ -243,19 +263,19 @@
     base = ((at_z * nh + at_h) * nx * latents.shape[0] + lax.broadcasted_iota(I32, (nz, nh, own), 2)).reshape(1, -1)
     query_rows = queries.reshape(queries.shape[0] * H, WIDE)
 
-    pieces, spots = [], []
-    for piece, source in zip([column] + others, sources):
-        pieces.append([piece, shift(piece, "c", 1)])
+    spots = []
+    for source in sources:
         first = (source % nx) * latents.shape[0]
         spots.append([first + core * own, first + (nc - 1 - core) * own])
 
-    def call(which, state, last, name):
+    def call(which, pieces, state, last, name):
         marks = jnp.stack([offsets[0]] + [s for i in which for s in spots[i]]).astype(I32)
-        return attend(marks, query_rows, base, [p for i in which for p in pieces[i]], state, last, name)
-
-    state = call([0], [], False, "attend_own")
-    state = call([1, 2], state, False, "attend_near")
-    mixed = call([3], state, True, "attend_far")
+        both = [p for piece in pieces for p in (piece, shift(piece, "c", 1))]
+        return attend(marks, query_rows, base, both, state, last, name)
+
+    state = call([0], [column], [], False, "attend_own")
+    state = call([1, 2], others[:2], state, False, "attend_near")
+    mixed = call([3], [hold(others[2], state[0])], state, True, "attend_far")
     attention_out = mixed.reshape(queries.shape[0], H * LAT)
     return (attention_out, moe_output)
 

time: 164 us -> 152 us (0.927)
  starting transfers between devices: 95.9 us -> 70.6 us
  waiting for transfers between devices: 32.8 us -> 45.7 us
    ppermute x12, starting transfers between devices: 65.6 us -> 40.3 us  [shift(): lax.ppermute(array, axis, [(i, (i + by) % size) for i in range(size)])]
    ppermute x12, waiting for transfers between devices: 13.4 us -> 25.4 us  [shift(): lax.ppermute(array, axis, [(i, (i + by) % size) for i in range(size)])]
    pallas_call x10 -> x11, Pallas kernels: 20.1 us -> 20.9 us  [kernel(): pl.pallas_call(body, out_shape=out_shape, in_specs=specs, out_specs=jax.t...]
    unnamed x27 -> x41, local copies, waits for them, and re-layouts: 7.66 us -> 7.88 us
  transfers between devices with their start and end apart: 17 -> 17, of which waited for: 6 -> 6; matrix products, arithmetic and copies ran while one was open for 3% -> 3% of each run, Pallas kernels for 10% -> 12%
where the time goes in v3:
time: 152 us; the launch traced here: 151 us
  starting transfers between devices  70.6 us (46%)
  waiting for transfers between devices  45.7 us (30%)
  Pallas kernels  20.9 us (14%)
  local copies, waits for them, and re-layouts  11.7 us (8%)
  between operations  1.75 us (1%)
    ppermute x12, starting transfers between devices, shift(): lax.ppermute(array, axis, [(i, (i + by) % size) for i in range(size)])  40.3 us
    all_to_all x5, starting transfers between devices, exchange(): return lax.all_to_all(array, axes, split_axis=0, concat_axis=0, tiled=False)  30.3 us
    ppermute x12, waiting for transfers between devices, shift(): lax.ppermute(array, axis, [(i, (i + by) % size) for i in range(size)])  25.4 us
    pallas_call x11, Pallas kernels, kernel(): pl.pallas_call(body, out_shape=out_shape, in_specs=specs, out_specs=jax.t...  20.9 us
    all_to_all x5, waiting for transfers between devices, exchange(): return lax.all_to_all(array, axes, split_axis=0, concat_axis=0, tiled=False)  20.3 us
    unnamed x41, local copies, waits for them, and re-layouts  7.88 us
  transfers between devices with their start and end apart: 17, of which 6 were waited for; matrix products, arithmetic and copies ran while one was open for 3% of the time, Pallas kernels for 12%

profile of v3, /device:TPU:1, one launch (start us, length us, event | category | flops | bytes accessed | tf_op | source)
XLA Modules:
  0.0 150.9 jit_solution(6363138288581654531)
XLA Ops:
  0.6 0.0 copy-start
  0.6 0.0 copy-start.9
  0.7 0.7 copy-done.9
  1.4 0.7 copy-done.11
  2.1 1.0 dispatch.1
  3.1 10.4 %all-to-all-start = ((bf16[32,32,128]{2,1,0:T(8,128)(2,1)}), bf16[32,32,128]{2,1,0:T(8,128)(2,1)S(1)}, u32[]{:S(2)}, u32[]{:S(2)}) async-start(bf16[32,32,128]{2,1,0:T(8,128)(2,1)} %dispatch.1), calls=%async_computation | async-start | bytes 524288 | tf_op jit(solution)/shard_map/all_to_all | solution.py:195
  13.5 3.4 %collective-permute-start = (bf16[40,576]{1,0:T(8,128)(2,1)S(1)}, bf16[40,576]{1,0:T(8,128)(2,1)S(1)}, u32[]{:S(2)}, u32[]{:S(2)}) collective-permute-start(bf16[40,576]{1,0:T(8,128)(2,1)S(1)} %constant_dynamic-slice_fusion), channel_id=1, source_target_pairs={{0,32},{32,0},{1,33},{33,1},{2,34},{34,2},{3,35},{35,3},{4,36},{36... | collective-permute-start | bytes 138248 | tf_op jit(solution)/shard_map/ppermute | solution.py:200
  16.9 5.7 %collective-permute-done = bf16[40,576]{1,0:T(8,128)(2,1)S(1)} collective-permute-done((bf16[40,576]{1,0:T(8,128)(2,1)S(1)}, bf16[40,576]{1,0:T(8,128)(2,1)S(1)}, u32[]{:S(2)}, u32[]{:S(2)}) %collective-permute-start) | collective-permute-done | bytes 46112 | tf_op jit(solution)/shard_map/ppermute | solution.py:200
  22.6 4.5 %all-to-all-done.after.arrived = bf16[32,32,128]{2,1,0:T(8,128)(2,1)S(1)} async-done(((bf16[32,32,128]{2,1,0:T(8,128)(2,1)}), bf16[32,32,128]{2,1,0:T(8,128)(2,1)S(1)}, u32[]{:S(2)}, u32[]{:S(2)}) %all-to-all-start) | async-done | bytes 262176 | tf_op jit(solution)/shard_map/all_to_all | solution.py:195
  27.1 1.0 pair.1
  28.1 6.5 %all-to-all-start.1 = ((bf16[8,80,576]{2,1,0:T(8,128)(2,1)}), bf16[8,80,576]{2,1,0:T(8,128)(2,1)}, u32[]{:S(2)}, u32[]{:S(2)}) async-start(bf16[8,80,576]{2,1,0:T(8,128)(2,1)} %pair.1), calls=%async_computation.1 | async-start | bytes 1638400 | tf_op jit(solution)/shard_map/all_to_all | solution.py:195
  34.5 0.1 cut.1
  34.6 3.1 %collective-permute-start.10 = (bf16[2,80,768]{2,1,0:T(8,128)(2,1)S(1)}, bf16[2,80,768]{2,1,0:T(8,128)(2,1)S(1)}, u32[]{:S(2)}, u32[]{:S(2)}) collective-permute-start(bf16[2,80,768]{2,1,0:T(8,128)(2,1)S(1)} %get-tuple-element.23), channel_id=1, source_target_pairs={{0,24},{8,0},{16,8},{24,16},{1,25},{9,1},{17,9},{25,17},{2,26},{10... | collective-permute-start | bytes 737288 | tf_op jit(solution)/shard_map/ppermute | solution.py:200
  37.7 2.2 %collective-permute-start.8 = (bf16[2,80,768]{2,1,0:T(8,128)(2,1)S(1)}, bf16[2,80,768]{2,1,0:T(8,128)(2,1)S(1)}, u32[]{:S(2)}, u32[]{:S(2)}) collective-permute-start(bf16[2,80,768]{2,1,0:T(8,128)(2,1)S(1)} %get-tuple-element.21), channel_id=1, source_target_pairs={{0,8},{8,16},{16,24},{24,0},{1,9},{9,17},{17,25},{25,1},{2,10},{10... | collective-permute-start | bytes 737288 | tf_op jit(solution)/shard_map/ppermute | solution.py:200
  39.9 3.2 %collective-permute-start.9 = (bf16[2,80,768]{2,1,0:T(8,128)(2,1)S(1)}, bf16[2,80,768]{2,1,0:T(8,128)(2,1)S(1)}, u32[]{:S(2)}, u32[]{:S(2)}) collective-permute-start(bf16[2,80,768]{2,1,0:T(8,128)(2,1)S(1)} %get-tuple-element.22), channel_id=1, source_target_pairs={{0,16},{8,24},{16,0},{24,8},{1,17},{9,25},{17,1},{25,9},{2,18},{10... | collective-permute-start | bytes 737288 | tf_op jit(solution)/shard_map/ppermute | solution.py:200
  43.2 15.8 %all-to-all-done.1 = bf16[8,80,576]{2,1,0:T(8,128)(2,1)} async-done(((bf16[8,80,576]{2,1,0:T(8,128)(2,1)}), bf16[8,80,576]{2,1,0:T(8,128)(2,1)}, u32[]{:S(2)}, u32[]{:S(2)}) %all-to-all-start.1) | async-done | bytes 737312 | tf_op jit(solution)/shard_map/all_to_all | solution.py:195
  59.0 1.5 copy.16
  60.5 2.3 %collective-permute-start.2 = (bf16[576,640]{1,0:T(8,128)(2,1)S(1)}, bf16[576,640]{1,0:T(8,128)(2,1)}, u32[]{:S(2)}, u32[]{:S(2)}) collective-permute-start(bf16[576,640]{1,0:T(8,128)(2,1)S(1)} %bitcast.13), channel_id=1, source_target_pairs={{0,8},{8,16},{16,24},{24,0},{1,9},{9,17},{17,25},{25,1},{2,10},{10... | collective-permute-start | bytes 2211848 | tf_op jit(solution)/shard_map/ppermute | solution.py:200
  62.8 4.2 %collective-permute-start.4 = (bf16[576,640]{1,0:T(8,128)(2,1)S(1)}, bf16[576,640]{1,0:T(8,128)(2,1)}, u32[]{:S(2)}, u32[]{:S(2)}) collective-permute-start(bf16[576,640]{1,0:T(8,128)(2,1)S(1)} %bitcast.14), channel_id=1, source_target_pairs={{0,24},{8,0},{16,8},{24,16},{1,25},{9,1},{17,9},{25,17},{2,26},{10... | collective-permute-start | bytes 2211848 | tf_op jit(solution)/shard_map/ppermute | solution.py:200
  67.0 0.0 collective-permute-done.10.refs_3_
  67.0 0.0 collective-permute-done.9.refs_2_
  67.0 1.3 first.1
  68.3 3.5 %all-to-all-start.2 = ((bf16[8,32,768]{2,1,0:T(8,128)(2,1)}), bf16[8,32,768]{2,1,0:T(8,128)(2,1)S(1)}, u32[]{:S(2)}, u32[]{:S(2)}) async-start(bf16[8,32,768]{2,1,0:T(8,128)(2,1)} %bitcast.12), calls=%async_computation.2 | async-start | bytes 786432 | tf_op jit(solution)/shard_map/all_to_all | solution.py:195
  71.8 2.9 %collective-permute-start.6 = (bf16[576,640]{1,0:T(8,128)(2,1)S(1)}, bf16[576,640]{1,0:T(8,128)(2,1)}, u32[]{:S(2)}, u32[]{:S(2)}) collective-permute-start(bf16[576,640]{1,0:T(8,128)(2,1)S(1)} %bitcast.16), channel_id=1, source_target_pairs={{0,1},{1,0},{2,3},{3,2},{4,5},{5,4},{6,7},{7,6},{8,9},{9,8},{10,11... | collective-permute-start | bytes 2211848 | tf_op jit(solution)/shard_map/ppermute | solution.py:200
  74.7 6.5 %collective-permute-done.2.refs_0_ = bf16[576,640]{1,0:T(8,128)(2,1)} collective-permute-done((bf16[576,640]{1,0:T(8,128)(2,1)S(1)}, bf16[576,640]{1,0:T(8,128)(2,1)}, u32[]{:S(2)}, u32[]{:S(2)}) %collective-permute-start.2) | collective-permute-done | bytes 737312 | tf_op jit(solution)/shard_map/ppermute | solution.py:200
  81.3 3.2 %collective-permute-start.3 = (bf16[576,640]{1,0:T(8,128)(2,1)}, bf16[576,640]{1,0:T(8,128)(2,1)}, u32[]{:S(2)}, u32[]{:S(2)}) collective-permute-start(bf16[576,640]{1,0:T(8,128)(2,1)} %collective-permute-done.2.refs_0_), channel_id=1, source_target_pairs={{0,1},{1,0},{2,3},{3,2},{4,5},{5,4},{6,7},{7,6},{8,9},{9,8},{10,11... | collective-permute-start | bytes 2211848 | tf_op jit(solution)/shard_map/ppermute | solution.py:200
  84.5 1.9 %collective-permute-start.5 = (bf16[576,640]{1,0:T(8,128)(2,1)}, bf16[576,640]{1,0:T(8,128)(2,1)}, u32[]{:S(2)}, u32[]{:S(2)}) collective-permute-start(bf16[576,640]{1,0:T(8,128)(2,1)} %collective-permute-done.4.refs_2_), channel_id=1, source_target_pairs={{0,1},{1,0},{2,3},{3,2},{4,5},{5,4},{6,7},{7,6},{8,9},{9,8},{10,11... | collective-permute-start | bytes 2211848 | tf_op jit(solution)/shard_map/ppermute | solution.py:200
  86.4 0.1 add.130
  86.5 5.5 %collective-permute-start.11 = (bf16[32,768]{1,0:T(8,128)(2,1)S(1)}, bf16[32,768]{1,0:T(8,128)(2,1)S(1)}, u32[]{:S(2)}, u32[]{:S(2)}) collective-permute-start(bf16[32,768]{1,0:T(8,128)(2,1)S(1)} %get-tuple-element.25), channel_id=1, source_target_pairs={{0,32},{32,0},{1,33},{33,1},{2,34},{34,2},{3,35},{35,3},{4,36},{36... | collective-permute-start | bytes 147464 | tf_op jit(solution)/shard_map/ppermute | solution.py:200
  92.0 3.3 %collective-permute-done.11.other = bf16[32,768]{1,0:T(8,128)(2,1)S(1)} collective-permute-done((bf16[32,768]{1,0:T(8,128)(2,1)S(1)}, bf16[32,768]{1,0:T(8,128)(2,1)S(1)}, u32[]{:S(2)}, u32[]{:S(2)}) %collective-permute-start.11) | collective-permute-done | bytes 49184 | tf_op jit(solution)/shard_map/ppermute | solution.py:200
  95.3 1.0 hidden.1
  96.3 4.8 %all-to-all-start.3 = ((bf16[32,32,384]{2,1,0:T(8,128)(2,1)}), bf16[32,32,384]{2,1,0:T(8,128)(2,1)S(1)}, u32[]{:S(2)}, u32[]{:S(2)}) async-start(bf16[32,32,384]{2,1,0:T(8,128)(2,1)} %hidden.1), calls=%async_computation.3 | async-start | bytes 1572864 | tf_op jit(solution)/shard_map/all_to_all | solution.py:195
  101.8 0.1 iota.29
  101.9 0.1 iota.30
  102.0 0.1 iota.26
  102.1 0.1 iota.27
  102.2 0.1 iota.32
  102.3 0.7 reshape.101.queries
  103.0 0.1 stack.40.spots
  103.1 4.6 %collective-permute-start.1 = (bf16[576,640]{1,0:T(8,128)(2,1)S(1)}, bf16[576,640]{1,0:T(8,128)(2,1)S(1)}, u32[]{:S(2)}, u32[]{:S(2)}) collective-permute-start(bf16[576,640]{1,0:T(8,128)(2,1)S(1)} %bitcast.17), channel_id=1, source_target_pairs={{0,16},{8,24},{16,0},{24,8},{1,17},{9,25},{17,1},{25,9},{2,18},{10... | collective-permute-start | bytes 2211848 | tf_op jit(solution)/shard_map/ppermute | solution.py:200
  107.7 0.1 pad_add_fusion.1.spots
  107.8 0.0 collective-permute-done.6.refs_1_
  107.8 3.8 %attend_own.1 = (f32[512,128]{1,0:T(8,128)S(1)}, f32[512,128]{1,0:T(8,128)S(1)}, f32[512,512]{1,0:T(8,128)S(1)}) custom-call(s32[3]{0:T(128)S(1)} %pad_add_fusion.1.spots, bf16[512,576]{1,0:T(8,128)(2,1)S(1)} %reshape.101.queries, s32[1,640]{1,0:T(1,128)S(1)} %multiply_add_fusion.base, bf16[576,640]{1,0:T(8,128)(2,1)S(1)} %bitcast.18, ...), custom_call_target="tpu_custom_call" | custom-call | flops 1509949440 | bytes 2523136 | tf_op jit(solution)/shard_map/attend_own/pallas_call | solution.py:34
  111.6 0.0 collective-permute-done.3.refs_1_
  111.6 6.9 %attend_near.1 = (f32[512,128]{1,0:T(8,128)S(1)}, f32[512,128]{1,0:T(8,128)S(1)}, f32[512,512]{1,0:T(8,128)S(1)}) custom-call(s32[5]{0:T(128)S(1)} %stack.40.spots, bf16[512,576]{1,0:T(8,128)(2,1)S(1)} %reshape.101.queries, s32[1,640]{1,0:T(1,128)S(1)} %multiply_add_fusion.base, bf16[576,640]{1,0:T(8,128)(2,1)} %collective-permute-done.2.refs_0_, ...), custom_call_target="tpu_custom_call" | custom-call | flops 3019898880 | bytes 3997696 | tf_op jit(solution)/shard_map/attend_near/pallas_call | solution.py:34
  118.5 0.0 copy-start.7
  118.5 0.7 copy-done.7
  119.2 1.0 copy-done.12
  120.2 0.7 copy-done.14
  120.9 9.8 %collective-permute-done.1.array = bf16[576,640]{1,0:T(8,128)(2,1)S(1)} collective-permute-done((bf16[576,640]{1,0:T(8,128)(2,1)S(1)}, bf16[576,640]{1,0:T(8,128)(2,1)S(1)}, u32[]{:S(2)}, u32[]{:S(2)}) %collective-permute-start.1) | collective-permute-done | bytes 737312 | tf_op jit(solution)/shard_map/ppermute | solution.py:200
  130.7 0.9 copy-done.1
  131.6 3.7 %collective-permute-start.7 = (bf16[576,640]{1,0:T(8,128)(2,1)}, bf16[576,640]{1,0:T(8,128)(2,1)}, u32[]{:S(2)}, u32[]{:S(2)}) collective-permute-start(bf16[576,640]{1,0:T(8,128)(2,1)} %hold.1.refs_0_), channel_id=1, source_target_pairs={{0,1},{1,0},{2,3},{3,2},{4,5},{5,4},{6,7},{7,6},{8,9},{9,8},{10,11... | collective-permute-start | bytes 2211848 | tf_op jit(solution)/shard_map/ppermute | solution.py:200
  135.4 0.1 copy.18.routes
  135.4 0.4 copy.17.down
  135.8 0.3 copy-done.18
  136.1 0.1 copy.19.gates
  136.2 0.1 pad_add_fusion.spots
  136.3 1.0 second.1
  137.3 5.2 %all-to-all-start.4 = ((bf16[8,32,128]{2,1,0:T(8,128)(2,1)}), bf16[8,32,128]{2,1,0:T(8,128)(2,1)S(1)}, u32[]{:S(2)}, u32[]{:S(2)}) async-start(bf16[8,32,128]{2,1,0:T(8,128)(2,1)} %second.1), calls=%async_computation.4 | async-start | bytes 131072 | tf_op jit(solution)/shard_map/all_to_all | solution.py:195
  142.6 1.1 copy-done.4
  143.6 1.2 copy-done.13
  144.9 3.8 %attend_far.1 = bf16[512,512]{1,0:T(8,128)(2,1)S(1)} custom-call(s32[3]{0:T(128)S(1)} %pad_add_fusion.spots, bf16[512,576]{1,0:T(8,128)(2,1)S(1)} %copy-done.4, s32[1,640]{1,0:T(1,128)S(1)} %multiply_add_fusion.base, bf16[576,640]{1,0:T(8,128)(2,1)S(1)} %copy-done.2, bf16[576,640]{1,0:T(8,128)(2,1)} %collective-permute-done.7.refs_1_, ...), custom_call_target="tpu_custom_call" | custom-call | flops 1509949440 | bytes 2523136 | tf_op jit(solution)/shard_map/attend_far/pallas_call | solution.py:34
  148.7 1.2 reshape.103
  149.9 1.0 combine.1
  (40 shorter events, 0.1 us)
Async XLA Ops:
  0.6 12.9 %copy-start = (bf16[80,576]{1,0:T(8,128)(2,1)S(1)}, bf16[80,576]{1,0:T(8,128)(2,1)}, u32[]{:S(2)}) copy-start(bf16[80,576]{1,0:T(8,128)(2,1)} %param.10) | copy-start | bytes 276484
  0.6 0.7 copy-start.9
  1.4 0.7 copy-start.11
  3.1 24.0 %all-to-all-start = ((bf16[32,32,128]{2,1,0:T(8,128)(2,1)}), bf16[32,32,128]{2,1,0:T(8,128)(2,1)S(1)}, u32[]{:S(2)}, u32[]{:S(2)}) async-start(bf16[32,32,128]{2,1,0:T(8,128)(2,1)} %dispatch.1), calls=%async_computation | async-start | bytes 524288 | tf_op jit(solution)/shard_map/all_to_all | solution.py:195
  13.5 9.1 %collective-permute-start = (bf16[40,576]{1,0:T(8,128)(2,1)S(1)}, bf16[40,576]{1,0:T(8,128)(2,1)S(1)}, u32[]{:S(2)}, u32[]{:S(2)}) collective-permute-start(bf16[40,576]{1,0:T(8,128)(2,1)S(1)} %constant_dynamic-slice_fusion), channel_id=1, source_target_pairs={{0,32},{32,0},{1,33},{33,1},{2,34},{34,2},{3,35},{35,3},{4,36},{36... | collective-permute-start | bytes 138248 | tf_op jit(solution)/shard_map/ppermute | solution.py:200
  28.1 6.5 %copy-start.5 = (bf16[2,80,1536]{2,1,0:T(8,128)(2,1)S(1)}, bf16[2,80,1536]{2,1,0:T(8,128)(2,1)}, u32[]{:S(2)}) copy-start(bf16[2,80,1536]{2,1,0:T(8,128)(2,1)} %gate.1) | copy-start | bytes 1474564
  28.1 6.5 %copy-start.6 = (bf16[2,80,1536]{2,1,0:T(8,128)(2,1)S(1)}, bf16[2,80,1536]{2,1,0:T(8,128)(2,1)}, u32[]{:S(2)}) copy-start(bf16[2,80,1536]{2,1,0:T(8,128)(2,1)} %up.1) | copy-start | bytes 1474564
  28.1 30.9 %all-to-all-start.1 = ((bf16[8,80,576]{2,1,0:T(8,128)(2,1)}), bf16[8,80,576]{2,1,0:T(8,128)(2,1)}, u32[]{:S(2)}, u32[]{:S(2)}) async-start(bf16[8,80,576]{2,1,0:T(8,128)(2,1)} %pair.1), calls=%async_computation.1 | async-start | bytes 1638400 | tf_op jit(solution)/shard_map/all_to_all | solution.py:195
  34.6 32.3 %collective-permute-start.10 = (bf16[2,80,768]{2,1,0:T(8,128)(2,1)S(1)}, bf16[2,80,768]{2,1,0:T(8,128)(2,1)S(1)}, u32[]{:S(2)}, u32[]{:S(2)}) collective-permute-start(bf16[2,80,768]{2,1,0:T(8,128)(2,1)S(1)} %get-tuple-element.23), channel_id=1, source_target_pairs={{0,24},{8,0},{16,8},{24,16},{1,25},{9,1},{17,9},{25,17},{2,26},{10... | collective-permute-start | bytes 737288 | tf_op jit(solution)/shard_map/ppermute | solution.py:200
  37.7 29.3 %collective-permute-start.8 = (bf16[2,80,768]{2,1,0:T(8,128)(2,1)S(1)}, bf16[2,80,768]{2,1,0:T(8,128)(2,1)S(1)}, u32[]{:S(2)}, u32[]{:S(2)}) collective-permute-start(bf16[2,80,768]{2,1,0:T(8,128)(2,1)S(1)} %get-tuple-element.21), channel_id=1, source_target_pairs={{0,8},{8,16},{16,24},{24,0},{1,9},{9,17},{17,25},{25,1},{2,10},{10... | collective-permute-start | bytes 737288 | tf_op jit(solution)/shard_map/ppermute | solution.py:200
  39.9 27.1 %collective-permute-start.9 = (bf16[2,80,768]{2,1,0:T(8,128)(2,1)S(1)}, bf16[2,80,768]{2,1,0:T(8,128)(2,1)S(1)}, u32[]{:S(2)}, u32[]{:S(2)}) collective-permute-start(bf16[2,80,768]{2,1,0:T(8,128)(2,1)S(1)} %get-tuple-element.22), channel_id=1, source_target_pairs={{0,16},{8,24},{16,0},{24,8},{1,17},{9,25},{17,1},{25,9},{2,18},{10... | collective-permute-start | bytes 737288 | tf_op jit(solution)/shard_map/ppermute | solution.py:200
  60.5 20.8 %collective-permute-start.2 = (bf16[576,640]{1,0:T(8,128)(2,1)S(1)}, bf16[576,640]{1,0:T(8,128)(2,1)}, u32[]{:S(2)}, u32[]{:S(2)}) collective-permute-start(bf16[576,640]{1,0:T(8,128)(2,1)S(1)} %bitcast.13), channel_id=1, source_target_pairs={{0,8},{8,16},{16,24},{24,0},{1,9},{9,17},{17,25},{25,1},{2,10},{10... | collective-permute-start | bytes 2211848 | tf_op jit(solution)/shard_map/ppermute | solution.py:200
  62.8 21.7 %collective-permute-start.4 = (bf16[576,640]{1,0:T(8,128)(2,1)S(1)}, bf16[576,640]{1,0:T(8,128)(2,1)}, u32[]{:S(2)}, u32[]{:S(2)}) collective-permute-start(bf16[576,640]{1,0:T(8,128)(2,1)S(1)} %bitcast.14), channel_id=1, source_target_pairs={{0,24},{8,0},{16,8},{24,16},{1,25},{9,1},{17,9},{25,17},{2,26},{10... | collective-permute-start | bytes 2211848 | tf_op jit(solution)/shard_map/ppermute | solution.py:200
  68.3 18.1 %all-to-all-start.2 = ((bf16[8,32,768]{2,1,0:T(8,128)(2,1)}), bf16[8,32,768]{2,1,0:T(8,128)(2,1)S(1)}, u32[]{:S(2)}, u32[]{:S(2)}) async-start(bf16[8,32,768]{2,1,0:T(8,128)(2,1)} %bitcast.12), calls=%async_computation.2 | async-start | bytes 786432 | tf_op jit(solution)/shard_map/all_to_all | solution.py:195
  71.8 36.0 %collective-permute-start.6 = (bf16[576,640]{1,0:T(8,128)(2,1)S(1)}, bf16[576,640]{1,0:T(8,128)(2,1)}, u32[]{:S(2)}, u32[]{:S(2)}) collective-permute-start(bf16[576,640]{1,0:T(8,128)(2,1)S(1)} %bitcast.16), channel_id=1, source_target_pairs={{0,1},{1,0},{2,3},{3,2},{4,5},{5,4},{6,7},{7,6},{8,9},{9,8},{10,11... | collective-permute-start | bytes 2211848 | tf_op jit(solution)/shard_map/ppermute | solution.py:200
  81.3 30.3 %collective-permute-start.3 = (bf16[576,640]{1,0:T(8,128)(2,1)}, bf16[576,640]{1,0:T(8,128)(2,1)}, u32[]{:S(2)}, u32[]{:S(2)}) collective-permute-start(bf16[576,640]{1,0:T(8,128)(2,1)} %collective-permute-done.2.refs_0_), channel_id=1, source_target_pairs={{0,1},{1,0},{2,3},{3,2},{4,5},{5,4},{6,7},{7,6},{8,9},{9,8},{10,11... | collective-permute-start | bytes 2211848 | tf_op jit(solution)/shard_map/ppermute | solution.py:200
  84.5 27.1 %collective-permute-start.5 = (bf16[576,640]{1,0:T(8,128)(2,1)}, bf16[576,640]{1,0:T(8,128)(2,1)}, u32[]{:S(2)}, u32[]{:S(2)}) collective-permute-start(bf16[576,640]{1,0:T(8,128)(2,1)} %collective-permute-done.4.refs_2_), channel_id=1, source_target_pairs={{0,1},{1,0},{2,3},{3,2},{4,5},{5,4},{6,7},{7,6},{8,9},{9,8},{10,11... | collective-permute-start | bytes 2211848 | tf_op jit(solution)/shard_map/ppermute | solution.py:200
  86.5 8.8 %collective-permute-start.11 = (bf16[32,768]{1,0:T(8,128)(2,1)S(1)}, bf16[32,768]{1,0:T(8,128)(2,1)S(1)}, u32[]{:S(2)}, u32[]{:S(2)}) collective-permute-start(bf16[32,768]{1,0:T(8,128)(2,1)S(1)} %get-tuple-element.25), channel_id=1, source_target_pairs={{0,32},{32,0},{1,33},{33,1},{2,34},{34,2},{3,35},{35,3},{4,36},{36... | collective-permute-start | bytes 147464 | tf_op jit(solution)/shard_map/ppermute | solution.py:200
  96.3 5.9 %copy-start.16 = (bf16[4,73728]{1,0:T(4,128)(2,1)S(1)}, bf16[4,73728]{1,0:T(4,128)(2,1)}, u32[]{:S(2)}) copy-start(bf16[4,73728]{1,0:T(4,128)(2,1)} %param.9) | copy-start | bytes 1769476
  96.3 40.0 %all-to-all-start.3 = ((bf16[32,32,384]{2,1,0:T(8,128)(2,1)}), bf16[32,32,384]{2,1,0:T(8,128)(2,1)S(1)}, u32[]{:S(2)}, u32[]{:S(2)}) async-start(bf16[32,32,384]{2,1,0:T(8,128)(2,1)} %hidden.1), calls=%async_computation.3 | async-start | bytes 1572864 | tf_op jit(solution)/shard_map/all_to_all | solution.py:195
  103.0 8.6 %copy-start.3 = (bf16[512,576]{1,0:T(8,128)(2,1)}, bf16[512,576]{1,0:T(8,128)(2,1)S(1)}, u32[]{:S(2)}) copy-start(bf16[512,576]{1,0:T(8,128)(2,1)S(1)} %reshape.101.queries) | copy-start | bytes 1769476
  103.1 27.7 %collective-permute-start.1 = (bf16[576,640]{1,0:T(8,128)(2,1)S(1)}, bf16[576,640]{1,0:T(8,128)(2,1)S(1)}, u32[]{:S(2)}, u32[]{:S(2)}) collective-permute-start(bf16[576,640]{1,0:T(8,128)(2,1)S(1)} %bitcast.17), channel_id=1, source_target_pairs={{0,16},{8,24},{16,0},{24,8},{1,17},{9,25},{17,1},{25,9},{2,18},{10... | collective-permute-start | bytes 2211848 | tf_op jit(solution)/shard_map/ppermute | solution.py:200
  118.5 0.7 copy-start.7
  119.2 1.0 copy-start.12
  120.2 0.7 copy-start.14
  130.7 0.9 copy-start.1
  131.6 3.8 %copy-start.10 = (s32[32,6]{0,1:T(8,128)S(1)}, s32[32,6]{0,1:T(8,128)}, u32[]{:S(2)}) copy-start(s32[32,6]{0,1:T(8,128)} %param.13) | copy-start | bytes 2308
  131.6 3.8 %copy-start.17 = (bf16[2,1536,80]{1,2,0:T(8,128)(2,1)S(1)}, bf16[2,1536,80]{1,2,0:T(8,128)(2,1)}, u32[]{:S(2)}) copy-start(bf16[2,1536,80]{1,2,0:T(8,128)(2,1)} %param.17) | copy-start | bytes 1474564
  131.6 10.9 %collective-permute-start.7 = (bf16[576,640]{1,0:T(8,128)(2,1)}, bf16[576,640]{1,0:T(8,128)(2,1)}, u32[]{:S(2)}, u32[]{:S(2)}) collective-permute-start(bf16[576,640]{1,0:T(8,128)(2,1)} %hold.1.refs_0_), channel_id=1, source_target_pairs={{0,1},{1,0},{2,3},{3,2},{4,5},{5,4},{6,7},{7,6},{8,9},{9,8},{10,11... | collective-permute-start | bytes 2211848 | tf_op jit(solution)/shard_map/ppermute | solution.py:200
  135.4 0.7 copy-start.18
  136.3 6.2 %copy-start.2 = (bf16[576,640]{1,0:T(8,128)(2,1)S(1)}, bf16[576,640]{1,0:T(8,128)(2,1)}, u32[]{:S(2)}) copy-start(bf16[576,640]{1,0:T(8,128)(2,1)} %hold.1.refs_0_) | copy-start | bytes 2211844
  136.3 6.2 %copy-start.8 = (f32[512,128]{1,0:T(8,128)S(1)}, f32[512,128]{1,0:T(8,128)}, u32[]{:S(2)}) copy-start(f32[512,128]{1,0:T(8,128)} %copy-done.7) | copy-start | bytes 786436
  136.3 6.2 %copy-start.15 = (f32[512,128]{1,0:T(8,128)S(1)}, f32[512,128]{1,0:T(8,128)}, u32[]{:S(2)}) copy-start(f32[512,128]{1,0:T(8,128)} %copy-done.14) | copy-start | bytes 786436
  137.3 12.6 %all-to-all-start.4 = ((bf16[8,32,128]{2,1,0:T(8,128)(2,1)}), bf16[8,32,128]{2,1,0:T(8,128)(2,1)S(1)}, u32[]{:S(2)}, u32[]{:S(2)}) async-start(bf16[8,32,128]{2,1,0:T(8,128)(2,1)} %second.1), calls=%async_computation.4 | async-start | bytes 131072 | tf_op jit(solution)/shard_map/all_to_all | solution.py:195
  142.5 1.1 copy-start.4
  143.6 1.2 copy-start.13

commit v4 on v3

--- a/solution.py
+++ b/solution.py
@@ -16,6 +16,7 @@
 EXPERTS = 16
 CAP = 16
 LANES = 128
+CLAIM = 4
 
 SCALE_LOG2 = 192.0 ** (-0.5) * math.log2(math.e)
 F32 = jnp.float32
@@ -85,10 +86,11 @@
     body = functools.partial(attention_body, len(pieces), not state, last)
     specs = [SMEM] + [VMEM] * (2 + len(pieces) + len(state))
     args = (spots, queries, base, *pieces, *state)
-    return kernel(body, name, out, specs, args, 4 * rows * count * WIDE, 2 * count * WIDE + 2**20, rows * count)
-
-
-def dispatch_body(copies, routes, tokens, out):
+    return kernel(body, name, out, specs, args, 4 * rows * count * WIDE * CLAIM, (2 * count * WIDE + 2**20) * CLAIM, rows * count * CLAIM)
+
+
+def dispatch_body(copies, routes, tokens, *refs):
+    out = refs[-1]
     count = tokens.shape[0]
     slot = lax.broadcasted_iota(I32, (EXPERTS * CAP, count), 0)
     named = routes[0:1, :] == slot // CAP
@@ -114,12 +116,7 @@
         out[:, :, units:] = up[:, :, pl.ds(at, units)]
 
 
-def pair_body(rows, after, out):
-    for i in range(out.shape[0]):
-        out[i] = rows[...]
-
-
-def first_body(order, spots, after, arrived, *refs):
+def first_body(order, spots, arrived, *refs):
     weights, out = refs[:-1], refs[-1]
     held, feats = weights[0].shape[:2]
     owners = arrived.shape[0] // len(weights)
@@ -202,7 +199,7 @@
 
 def local(queries, latents, offsets, moe_input, routes, gate_values, w_gate, w_up, w_down):
     nz, nh, nx, nl, nc = (lax.axis_size(a) for a in ("z", "h", "x", "l", "c"))
-    h_at, x_at, core = (lax.axis_index(a) for a in ("h", "x", "c"))
+    x_at, core = lax.axis_index("x"), lax.axis_index("c")
     owners = nl * nc
     held, feats, width = w_gate.shape
     units = width // nx
@@ -210,31 +207,30 @@
     slots = held * CAP
     where_x = x_at.astype(I32).reshape(1)
 
-    outgoing = kernel(
-        functools.partial(dispatch_body, nx), "dispatch", shaped((nx * owners, slots, LANES), BF16),
-        [VMEM] * 2, (routes.T, moe_input), 2**20, 2**18,
-    )
-    arrived = exchange(outgoing, ("x", "l", "c"))
-
     own = latents.shape[0] // nc
     half = lax.dynamic_slice_in_dim(latents, core * own, own, 0)
-    paired = jnp.concatenate([half, shift(half, "h", 1)], axis=0)
-    paired = kernel(
-        pair_body, "pair", shaped((nz,) + paired.shape, BF16), [VMEM, AFTER], (paired, arrived), 2**10, 2**20
-    )
-    column = exchange(paired, "z")
-    column = column.reshape(nz * nh * own, WIDE).T
+    column = exchange(jnp.broadcast_to(half[None], (nz * nh,) + half.shape), ("z", "h"))
+    column = column.reshape(nz * nh * own, WIDE)
 
     cut = kernel(
         cut_body, "cut", [shaped((held, feats, 2 * units), BF16)] * nx,
         [SMEM, VMEM, VMEM], (where_x, w_gate, w_up), 2**10, 2**21,
     )
     weights = [cut[0]] + [shift(cut[j], "x", j) for j in range(1, nx)]
+    outgoing = kernel(
+        functools.partial(dispatch_body, nx), "dispatch", shaped((nx * owners, slots, LANES), BF16),
+        [VMEM, VMEM] + [AFTER] * nx, (routes.T, moe_input, column, *weights[1:]), 2**20, 2**18,
+    )
+    arrived = exchange(outgoing, ("x", "l", "c"))
+    column = column.T
+    others = [shift(column, "x", 1), shift(column, "x", -1)]
+
     order = [0] + [nx - j for j in range(1, nx)]
     parts = kernel(
         functools.partial(first_body, order), "first", shaped((held * owners * CAP, 2 * units), BF16),
-        [SMEM, AFTER] + [VMEM] * (1 + nx), (where_x, column, arrived, *weights), 2**28, 2**21,
-    )
+        [SMEM] + [VMEM] * (1 + nx), (where_x, arrived, *weights), 2**28, 2**21,
+    )
+    others.append(shift(hold(column, parts), "x", 2))
     parts = exchange(parts.reshape(nz, -1, 2 * units), "z")
     rows = parts.shape[1]
     total, rounded = kernel(
@@ -256,10 +252,9 @@
         [VMEM] * 3, (routes, gate_values, back), 2**20, 2**18,
     )
 
-    others = [shift(column, "x", 1), shift(column, "x", -1), shift(column, "x", 2)]
     sources = [x_at, x_at + nx - 1, x_at + 1, x_at + 2]
     at_z = lax.broadcasted_iota(I32, (nz, nh, own), 0)
-    at_h = (lax.broadcasted_iota(I32, (nz, nh, own), 1) + h_at) % nh
+    at_h = lax.broadcasted_iota(I32, (nz, nh, own), 1)
     base = ((at_z * nh + at_h) * nx * latents.shape[0] + lax.broadcasted_iota(I32, (nz, nh, own), 2)).reshape(1, -1)
     query_rows = queries.reshape(queries.shape[0] * H, WIDE)
 

time: 152 us -> 153 us (level); the launches traced: 151 us -> 150 us
  waiting for transfers between devices: 45.7 us -> 28.2 us
  starting transfers between devices: 70.6 us -> 85.8 us
  local copies, waits for them, and re-layouts: 11.7 us -> 14.1 us
    all_to_all x5, starting transfers between devices: 30.3 us -> 52.4 us  [exchange(): return lax.all_to_all(array, axes, split_axis=0, concat_axis=0, tiled=False)]
    all_to_all x5, waiting for transfers between devices: 20.3 us -> 6.56 us  [exchange(): return lax.all_to_all(array, axes, split_axis=0, concat_axis=0, tiled=False)]
    ppermute x12 -> x11, starting transfers between devices: 40.3 us -> 33.5 us  [shift(): lax.ppermute(array, axis, [(i, (i + by) % size) for i in range(size)])]
    ppermute x12 -> x11, waiting for transfers between devices: 25.4 us -> 21.7 us  [shift(): lax.ppermute(array, axis, [(i, (i + by) % size) for i in range(size)])]
    unnamed x41 -> x39, local copies, waits for them, and re-layouts: 7.88 us -> 10.7 us
    pallas_call x11 -> x10, Pallas kernels: 20.9 us -> 19.9 us  [kernel(): pl.pallas_call(body, out_shape=out_shape, in_specs=specs, out_specs=jax.t...]
  transfers between devices with their start and end apart: 17 -> 16, of which waited for: 6 -> 7; matrix products, arithmetic and copies ran while one was open for 3% -> 3% of each run, Pallas kernels for 12% -> 12%
where the time goes in v4:
time: 153 us; the launch traced here: 150 us
  starting transfers between devices  85.8 us (56%)
  waiting for transfers between devices  28.2 us (18%)
  Pallas kernels  19.9 us (13%)
  local copies, waits for them, and re-layouts  14.1 us (9%)
  between operations  1.67 us (1%)
    all_to_all x5, starting transfers between devices, exchange(): return lax.all_to_all(array, axes, split_axis=0, concat_axis=0, tiled=False)  52.4 us
    ppermute x11, starting transfers between devices, shift(): lax.ppermute(array, axis, [(i, (i + by) % size) for i in range(size)])  33.5 us
    ppermute x11, waiting for transfers between devices, shift(): lax.ppermute(array, axis, [(i, (i + by) % size) for i in range(size)])  21.7 us
    pallas_call x10, Pallas kernels, kernel(): pl.pallas_call(body, out_shape=out_shape, in_specs=specs, out_specs=jax.t...  19.9 us
    unnamed x39, local copies, waits for them, and re-layouts  10.7 us
    all_to_all x5, waiting for transfers between devices, exchange(): return lax.all_to_all(array, axes, split_axis=0, concat_axis=0, tiled=False)  6.56 us
  transfers between devices with their start and end apart: 16, of which 7 were waited for; matrix products, arithmetic and copies ran while one was open for 3% of the time, Pallas kernels for 12%

profile of v4, /device:TPU:1, one launch (start us, length us, event | category | flops | bytes accessed | tf_op | source)
XLA Modules:
  0.0 150.0 jit_solution(10455162307483333312)
XLA Ops:
  0.6 0.0 copy-start
  0.7 0.9 copy-done
  1.5 1.0 broadcast_in_dim.2
  2.5 16.4 %all-to-all-start = ((bf16[16,40,576]{2,1,0:T(8,128)(2,1)}), bf16[16,40,576]{2,1,0:T(8,128)(2,1)S(1)}, u32[]{:S(2)}, u32[]{:S(2)}) async-start(bf16[16,40,576]{2,1,0:T(8,128)(2,1)} %broadcast_in_dim.2), calls=%async_computation | async-start | bytes 1638400 | tf_op jit(solution)/shard_map/all_to_all | solution.py:192
  18.9 0.0 copy-start.9
  18.9 0.1 cut.1
  19.0 0.0 copy-start.8
  19.0 3.1 %collective-permute-start = (bf16[2,80,768]{2,1,0:T(8,128)(2,1)S(1)}, bf16[2,80,768]{2,1,0:T(8,128)(2,1)S(1)}, u32[]{:S(2)}, u32[]{:S(2)}) collective-permute-start(bf16[2,80,768]{2,1,0:T(8,128)(2,1)S(1)} %get-tuple-element.14), channel_id=1, source_target_pairs={{0,8},{8,16},{16,24},{24,0},{1,9},{9,17},{17,25},{25,1},{2,10},{10... | collective-permute-start | bytes 737288 | tf_op jit(solution)/shard_map/ppermute | solution.py:197
  22.2 4.4 %collective-permute-start.1 = (bf16[2,80,768]{2,1,0:T(8,128)(2,1)S(1)}, bf16[2,80,768]{2,1,0:T(8,128)(2,1)S(1)}, u32[]{:S(2)}, u32[]{:S(2)}) collective-permute-start(bf16[2,80,768]{2,1,0:T(8,128)(2,1)S(1)} %get-tuple-element.15), channel_id=1, source_target_pairs={{0,16},{8,24},{16,0},{24,8},{1,17},{9,25},{17,1},{25,9},{2,18},{10... | collective-permute-start | bytes 737288 | tf_op jit(solution)/shard_map/ppermute | solution.py:197
  26.5 3.1 %collective-permute-start.2 = (bf16[2,80,768]{2,1,0:T(8,128)(2,1)S(1)}, bf16[2,80,768]{2,1,0:T(8,128)(2,1)S(1)}, u32[]{:S(2)}, u32[]{:S(2)}) collective-permute-start(bf16[2,80,768]{2,1,0:T(8,128)(2,1)S(1)} %get-tuple-element.16), channel_id=1, source_target_pairs={{0,24},{8,0},{16,8},{24,16},{1,25},{9,1},{17,9},{25,17},{2,26},{10... | collective-permute-start | bytes 737288 | tf_op jit(solution)/shard_map/ppermute | solution.py:197
  29.6 0.0 collective-permute-done.refs_1_
  29.6 5.3 %collective-permute-done.1.refs_2_ = bf16[2,80,768]{2,1,0:T(8,128)(2,1)S(1)} collective-permute-done((bf16[2,80,768]{2,1,0:T(8,128)(2,1)S(1)}, bf16[2,80,768]{2,1,0:T(8,128)(2,1)S(1)}, u32[]{:S(2)}, u32[]{:S(2)}) %collective-permute-start.1) | collective-permute-done | bytes 245792 | tf_op jit(solution)/shard_map/ppermute | solution.py:197
  34.9 1.6 %collective-permute-done.2.refs_3_ = bf16[2,80,768]{2,1,0:T(8,128)(2,1)S(1)} collective-permute-done((bf16[2,80,768]{2,1,0:T(8,128)(2,1)S(1)}, bf16[2,80,768]{2,1,0:T(8,128)(2,1)S(1)}, u32[]{:S(2)}, u32[]{:S(2)}) %collective-permute-start.2) | collective-permute-done | bytes 245792 | tf_op jit(solution)/shard_map/ppermute | solution.py:197
  36.5 0.6 all-to-all-done
  37.1 1.0 dispatch.1
  38.1 22.4 %all-to-all-start.1 = ((bf16[32,32,128]{2,1,0:T(8,128)(2,1)}), bf16[32,32,128]{2,1,0:T(8,128)(2,1)S(1)}, u32[]{:S(2)}, u32[]{:S(2)}) async-start(bf16[32,32,128]{2,1,0:T(8,128)(2,1)} %dispatch.1), calls=%async_computation.1 | async-start | bytes 524288 | tf_op jit(solution)/shard_map/all_to_all | solution.py:192
  60.5 0.4 copy.18
  60.9 3.3 %collective-permute-start.4 = (bf16[576,640]{1,0:T(8,128)(2,1)S(1)}, bf16[576,640]{1,0:T(8,128)(2,1)}, u32[]{:S(2)}, u32[]{:S(2)}) collective-permute-start(bf16[576,640]{1,0:T(8,128)(2,1)S(1)} %bitcast.15), channel_id=1, source_target_pairs={{0,8},{8,16},{16,24},{24,0},{1,9},{9,17},{17,25},{25,1},{2,10},{10... | collective-permute-start | bytes 2211848 | tf_op jit(solution)/shard_map/ppermute | solution.py:197
  64.2 3.2 %collective-permute-start.6 = (bf16[576,640]{1,0:T(8,128)(2,1)S(1)}, bf16[576,640]{1,0:T(8,128)(2,1)}, u32[]{:S(2)}, u32[]{:S(2)}) collective-permute-start(bf16[576,640]{1,0:T(8,128)(2,1)S(1)} %bitcast.16), channel_id=1, source_target_pairs={{0,24},{8,0},{16,8},{24,16},{1,25},{9,1},{17,9},{25,17},{2,26},{10... | collective-permute-start | bytes 2211848 | tf_op jit(solution)/shard_map/ppermute | solution.py:197
  67.4 2.7 %collective-permute-start.8 = (bf16[576,640]{1,0:T(8,128)(2,1)S(1)}, bf16[576,640]{1,0:T(8,128)(2,1)}, u32[]{:S(2)}, u32[]{:S(2)}) collective-permute-start(bf16[576,640]{1,0:T(8,128)(2,1)S(1)} %bitcast.17), channel_id=1, source_target_pairs={{0,1},{1,0},{2,3},{3,2},{4,5},{5,4},{6,7},{7,6},{8,9},{9,8},{10,11... | collective-permute-start | bytes 2211848 | tf_op jit(solution)/shard_map/ppermute | solution.py:197
  70.1 1.7 %all-to-all-done.1.arrived = bf16[32,32,128]{2,1,0:T(8,128)(2,1)S(1)} async-done(((bf16[32,32,128]{2,1,0:T(8,128)(2,1)}), bf16[32,32,128]{2,1,0:T(8,128)(2,1)S(1)}, u32[]{:S(2)}, u32[]{:S(2)}) %all-to-all-start.1) | async-done | bytes 262176 | tf_op jit(solution)/shard_map/all_to_all | solution.py:192
  71.8 1.3 first.1.after
  73.1 6.0 %all-to-all-start.2 = ((bf16[8,32,768]{2,1,0:T(8,128)(2,1)}), bf16[8,32,768]{2,1,0:T(8,128)(2,1)S(1)}, u32[]{:S(2)}, u32[]{:S(2)}) async-start(bf16[8,32,768]{2,1,0:T(8,128)(2,1)} %bitcast.12), calls=%async_computation.2 | async-start | bytes 786432 | tf_op jit(solution)/shard_map/all_to_all | solution.py:192
  79.1 4.6 %collective-permute-done.4.refs_0_ = bf16[576,640]{1,0:T(8,128)(2,1)} collective-permute-done((bf16[576,640]{1,0:T(8,128)(2,1)S(1)}, bf16[576,640]{1,0:T(8,128)(2,1)}, u32[]{:S(2)}, u32[]{:S(2)}) %collective-permute-start.4) | collective-permute-done | bytes 737312 | tf_op jit(solution)/shard_map/ppermute | solution.py:197
  83.7 2.7 %collective-permute-start.5 = (bf16[576,640]{1,0:T(8,128)(2,1)}, bf16[576,640]{1,0:T(8,128)(2,1)}, u32[]{:S(2)}, u32[]{:S(2)}) collective-permute-start(bf16[576,640]{1,0:T(8,128)(2,1)} %collective-permute-done.4.refs_0_), channel_id=1, source_target_pairs={{0,1},{1,0},{2,3},{3,2},{4,5},{5,4},{6,7},{7,6},{8,9},{9,8},{10,11... | collective-permute-start | bytes 2211848 | tf_op jit(solution)/shard_map/ppermute | solution.py:197
  86.4 1.9 %collective-permute-start.7 = (bf16[576,640]{1,0:T(8,128)(2,1)}, bf16[576,640]{1,0:T(8,128)(2,1)}, u32[]{:S(2)}, u32[]{:S(2)}) collective-permute-start(bf16[576,640]{1,0:T(8,128)(2,1)} %collective-permute-done.6.refs_2_), channel_id=1, source_target_pairs={{0,1},{1,0},{2,3},{3,2},{4,5},{5,4},{6,7},{7,6},{8,9},{9,8},{10,11... | collective-permute-start | bytes 2211848 | tf_op jit(solution)/shard_map/ppermute | solution.py:197
  88.3 0.1 iota_add_fusion
  89.1 0.7 reshape.61.queries
  89.8 0.1 add.93.base
  89.9 0.1 stack.40.spots
  89.9 0.1 pad_add_fusion.1.spots
  90.0 4.3 %all-to-all-done.2.parts = bf16[8,32,768]{2,1,0:T(8,128)(2,1)S(1)} async-done(((bf16[8,32,768]{2,1,0:T(8,128)(2,1)}), bf16[8,32,768]{2,1,0:T(8,128)(2,1)S(1)}, u32[]{:S(2)}, u32[]{:S(2)}) %all-to-all-start.2) | async-done | bytes 393248 | tf_op jit(solution)/shard_map/all_to_all | solution.py:192
  94.3 0.1 add.115
  94.3 1.9 %collective-permute-start.10 = (bf16[32,768]{1,0:T(8,128)(2,1)S(1)}, bf16[32,768]{1,0:T(8,128)(2,1)S(1)}, u32[]{:S(2)}, u32[]{:S(2)}) collective-permute-start(bf16[32,768]{1,0:T(8,128)(2,1)S(1)} %get-tuple-element.25), channel_id=1, source_target_pairs={{0,32},{32,0},{1,33},{33,1},{2,34},{34,2},{3,35},{35,3},{4,36},{36... | collective-permute-start | bytes 147464 | tf_op jit(solution)/shard_map/ppermute | solution.py:197
  96.3 0.0 collective-permute-done.8.refs_1_
  96.3 3.8 %attend_own.1 = (f32[512,128]{1,0:T(8,128)S(1)}, f32[512,128]{1,0:T(8,128)S(1)}, f32[512,512]{1,0:T(8,128)S(1)}) custom-call(s32[3]{0:T(128)S(1)} %pad_add_fusion.1.spots, bf16[512,576]{1,0:T(8,128)(2,1)S(1)} %reshape.61.queries, s32[1,640]{1,0:T(1,128)S(1)} %add.93.base, bf16[576,640]{1,0:T(8,128)(2,1)S(1)} %bitcast.18, ...), custom_call_target="tpu_custom_call" | custom-call | flops 6039797760 | bytes 10092544 | tf_op jit(solution)/shard_map/attend_own/pallas_call | solution.py:35
  100.1 1.0 copy-done.12
  101.1 3.1 %collective-permute-start.3 = (bf16[576,640]{1,0:T(8,128)(2,1)}, bf16[576,640]{1,0:T(8,128)(2,1)S(1)}, u32[]{:S(2)}, u32[]{:S(2)}) collective-permute-start(bf16[576,640]{1,0:T(8,128)(2,1)} %hold.2), channel_id=1, source_target_pairs={{0,16},{8,24},{16,0},{24,8},{1,17},{9,25},{17,1},{25,9},{2,18},{10... | collective-permute-start | bytes 2211848 | tf_op jit(solution)/shard_map/ppermute | solution.py:197
  104.1 0.0 collective-permute-done.10.other
  104.2 1.0 hidden.1
  105.1 3.9 %all-to-all-start.3 = ((bf16[32,32,384]{2,1,0:T(8,128)(2,1)}), bf16[32,32,384]{2,1,0:T(8,128)(2,1)S(1)}, u32[]{:S(2)}, u32[]{:S(2)}) async-start(bf16[32,32,384]{2,1,0:T(8,128)(2,1)} %hidden.1), calls=%async_computation.3 | async-start | bytes 1572864 | tf_op jit(solution)/shard_map/all_to_all | solution.py:192
  109.1 1.2 copy-done.13
  110.3 6.9 %attend_near.1 = (f32[512,128]{1,0:T(8,128)S(1)}, f32[512,128]{1,0:T(8,128)S(1)}, f32[512,512]{1,0:T(8,128)S(1)}) custom-call(s32[5]{0:T(128)S(1)} %stack.40.spots, bf16[512,576]{1,0:T(8,128)(2,1)S(1)} %reshape.61.queries, s32[1,640]{1,0:T(1,128)S(1)} %add.93.base, bf16[576,640]{1,0:T(8,128)(2,1)} %collective-permute-done.4.refs_0_, ...), custom_call_target="tpu_custom_call" | custom-call | flops 12079595520 | bytes 15990784 | tf_op jit(solution)/shard_map/attend_near/pallas_call | solution.py:35
  117.2 0.0 copy-start.6
  117.2 0.7 copy-done.6
  117.9 1.0 copy-done.10
  118.9 0.7 copy-done.14
  119.6 10.3 %collective-permute-done.3.array = bf16[576,640]{1,0:T(8,128)(2,1)S(1)} collective-permute-done((bf16[576,640]{1,0:T(8,128)(2,1)}, bf16[576,640]{1,0:T(8,128)(2,1)S(1)}, u32[]{:S(2)}, u32[]{:S(2)}) %collective-permute-start.3) | collective-permute-done | bytes 737312 | tf_op jit(solution)/shard_map/ppermute | solution.py:197
  129.8 0.9 copy-done.2
  130.7 4.1 %collective-permute-start.9 = (bf16[576,640]{1,0:T(8,128)(2,1)}, bf16[576,640]{1,0:T(8,128)(2,1)}, u32[]{:S(2)}, u32[]{:S(2)}) collective-permute-start(bf16[576,640]{1,0:T(8,128)(2,1)} %hold.3.refs_0_), channel_id=1, source_target_pairs={{0,1},{1,0},{2,3},{3,2},{4,5},{5,4},{6,7},{7,6},{8,9},{9,8},{10,11... | collective-permute-start | bytes 2211848 | tf_op jit(solution)/shard_map/ppermute | solution.py:197
  134.8 0.0 copy-start.17
  134.9 0.1 copy.20.routes
  134.9 0.6 copy-done.17
  135.5 0.1 copy.21.gates
  135.6 1.4 copy.19.down
  137.1 0.1 pad_add_fusion.spots
  137.1 1.0 second.1
  138.2 3.7 %all-to-all-start.4 = ((bf16[8,32,128]{2,1,0:T(8,128)(2,1)}), bf16[8,32,128]{2,1,0:T(8,128)(2,1)S(1)}, u32[]{:S(2)}, u32[]{:S(2)}) async-start(bf16[8,32,128]{2,1,0:T(8,128)(2,1)} %second.1), calls=%async_computation.4 | async-start | bytes 131072 | tf_op jit(solution)/shard_map/all_to_all | solution.py:192
  141.8 1.2 copy-done.11
  143.1 0.9 copy-done.15
  144.0 3.8 %attend_far.1 = bf16[512,512]{1,0:T(8,128)(2,1)S(1)} custom-call(s32[3]{0:T(128)S(1)} %pad_add_fusion.spots, bf16[512,576]{1,0:T(8,128)(2,1)S(1)} %reshape.61.queries, s32[1,640]{1,0:T(1,128)S(1)} %add.93.base, bf16[576,640]{1,0:T(8,128)(2,1)S(1)} %copy-done.3, bf16[576,640]{1,0:T(8,128)(2,1)} %collective-permute-done.9.refs_1_, f32[512,128]{1,0:T(8,128)S(1)} %copy-done.7, ...), custom_call_target="tpu_custom_call" | custom-call | flops 6039797760 | bytes 10092544 | tf_op jit(solution)/shard_map/attend_far/pallas_call | solution.py:35
  147.8 1.2 reshape.64
  149.0 0.0 all-to-all-done.4.back
  149.0 1.0 combine.1
  (30 shorter events, 0.1 us)
Async XLA Ops:
  0.6 0.9 copy-start
  2.5 16.4 %copy-start.4 = (bf16[2,80,1536]{2,1,0:T(8,128)(2,1)S(1)}, bf16[2,80,1536]{2,1,0:T(8,128)(2,1)}, u32[]{:S(2)}) copy-start(bf16[2,80,1536]{2,1,0:T(8,128)(2,1)} %gate.1) | copy-start | bytes 1474564
  2.5 16.4 %copy-start.5 = (bf16[2,80,1536]{2,1,0:T(8,128)(2,1)S(1)}, bf16[2,80,1536]{2,1,0:T(8,128)(2,1)}, u32[]{:S(2)}) copy-start(bf16[2,80,1536]{2,1,0:T(8,128)(2,1)} %up.1) | copy-start | bytes 1474564
  2.5 34.5 %all-to-all-start = ((bf16[16,40,576]{2,1,0:T(8,128)(2,1)}), bf16[16,40,576]{2,1,0:T(8,128)(2,1)S(1)}, u32[]{:S(2)}, u32[]{:S(2)}) async-start(bf16[16,40,576]{2,1,0:T(8,128)(2,1)} %broadcast_in_dim.2), calls=%async_computation | async-start | bytes 1638400 | tf_op jit(solution)/shard_map/all_to_all | solution.py:192
  18.9 18.2 %copy-start.9 = (bf16[32,80]{1,0:T(8,128)(2,1)S(1)}, bf16[32,80]{1,0:T(8,128)(2,1)}, u32[]{:S(2)}) copy-start(bf16[32,80]{1,0:T(8,128)(2,1)} %tokens.1) | copy-start | bytes 15364
  19.0 18.0 %copy-start.8 = (s32[32,6]{0,1:T(8,128)S(1)}, s32[32,6]{0,1:T(8,128)}, u32[]{:S(2)}) copy-start(s32[32,6]{0,1:T(8,128)} %param.13) | copy-start | bytes 2308
  19.0 10.6 %collective-permute-start = (bf16[2,80,768]{2,1,0:T(8,128)(2,1)S(1)}, bf16[2,80,768]{2,1,0:T(8,128)(2,1)S(1)}, u32[]{:S(2)}, u32[]{:S(2)}) collective-permute-start(bf16[2,80,768]{2,1,0:T(8,128)(2,1)S(1)} %get-tuple-element.14), channel_id=1, source_target_pairs={{0,8},{8,16},{16,24},{24,0},{1,9},{9,17},{17,25},{25,1},{2,10},{10... | collective-permute-start | bytes 737288 | tf_op jit(solution)/shard_map/ppermute | solution.py:197
  22.2 12.7 %collective-permute-start.1 = (bf16[2,80,768]{2,1,0:T(8,128)(2,1)S(1)}, bf16[2,80,768]{2,1,0:T(8,128)(2,1)S(1)}, u32[]{:S(2)}, u32[]{:S(2)}) collective-permute-start(bf16[2,80,768]{2,1,0:T(8,128)(2,1)S(1)} %get-tuple-element.15), channel_id=1, source_target_pairs={{0,16},{8,24},{16,0},{24,8},{1,17},{9,25},{17,1},{25,9},{2,18},{10... | collective-permute-start | bytes 737288 | tf_op jit(solution)/shard_map/ppermute | solution.py:197
  26.5 9.9 %collective-permute-start.2 = (bf16[2,80,768]{2,1,0:T(8,128)(2,1)S(1)}, bf16[2,80,768]{2,1,0:T(8,128)(2,1)S(1)}, u32[]{:S(2)}, u32[]{:S(2)}) collective-permute-start(bf16[2,80,768]{2,1,0:T(8,128)(2,1)S(1)} %get-tuple-element.16), channel_id=1, source_target_pairs={{0,24},{8,0},{16,8},{24,16},{1,25},{9,1},{17,9},{25,17},{2,26},{10... | collective-permute-start | bytes 737288 | tf_op jit(solution)/shard_map/ppermute | solution.py:197
  38.1 33.7 %all-to-all-start.1 = ((bf16[32,32,128]{2,1,0:T(8,128)(2,1)}), bf16[32,32,128]{2,1,0:T(8,128)(2,1)S(1)}, u32[]{:S(2)}, u32[]{:S(2)}) async-start(bf16[32,32,128]{2,1,0:T(8,128)(2,1)} %dispatch.1), calls=%async_computation.1 | async-start | bytes 524288 | tf_op jit(solution)/shard_map/all_to_all | solution.py:192
  60.9 35.4 %copy-start.1 = (bf16[640,576]{0,1:T(8,128)(2,1)}, bf16[640,576]{0,1:T(8,128)(2,1)S(1)}, u32[]{:S(2)}) copy-start(bf16[640,576]{0,1:T(8,128)(2,1)S(1)} %copy.18) | copy-start | bytes 2211844
  60.9 22.8 %collective-permute-start.4 = (bf16[576,640]{1,0:T(8,128)(2,1)S(1)}, bf16[576,640]{1,0:T(8,128)(2,1)}, u32[]{:S(2)}, u32[]{:S(2)}) collective-permute-start(bf16[576,640]{1,0:T(8,128)(2,1)S(1)} %bitcast.15), channel_id=1, source_target_pairs={{0,8},{8,16},{16,24},{24,0},{1,9},{9,17},{17,25},{25,1},{2,10},{10... | collective-permute-start | bytes 2211848 | tf_op jit(solution)/shard_map/ppermute | solution.py:197
  64.2 22.2 %collective-permute-start.6 = (bf16[576,640]{1,0:T(8,128)(2,1)S(1)}, bf16[576,640]{1,0:T(8,128)(2,1)}, u32[]{:S(2)}, u32[]{:S(2)}) collective-permute-start(bf16[576,640]{1,0:T(8,128)(2,1)S(1)} %bitcast.16), channel_id=1, source_target_pairs={{0,24},{8,0},{16,8},{24,16},{1,25},{9,1},{17,9},{25,17},{2,26},{10... | collective-permute-start | bytes 2211848 | tf_op jit(solution)/shard_map/ppermute | solution.py:197
  67.4 28.9 %collective-permute-start.8 = (bf16[576,640]{1,0:T(8,128)(2,1)S(1)}, bf16[576,640]{1,0:T(8,128)(2,1)}, u32[]{:S(2)}, u32[]{:S(2)}) collective-permute-start(bf16[576,640]{1,0:T(8,128)(2,1)S(1)} %bitcast.17), channel_id=1, source_target_pairs={{0,1},{1,0},{2,3},{3,2},{4,5},{5,4},{6,7},{7,6},{8,9},{9,8},{10,11... | collective-permute-start | bytes 2211848 | tf_op jit(solution)/shard_map/ppermute | solution.py:197
  73.1 16.0 %copy-start.16 = (bf16[4,73728]{1,0:T(4,128)(2,1)S(1)}, bf16[4,73728]{1,0:T(4,128)(2,1)}, u32[]{:S(2)}) copy-start(bf16[4,73728]{1,0:T(4,128)(2,1)} %param.9) | copy-start | bytes 1769476
  73.1 21.2 %all-to-all-start.2 = ((bf16[8,32,768]{2,1,0:T(8,128)(2,1)}), bf16[8,32,768]{2,1,0:T(8,128)(2,1)S(1)}, u32[]{:S(2)}, u32[]{:S(2)}) async-start(bf16[8,32,768]{2,1,0:T(8,128)(2,1)} %bitcast.12), calls=%async_computation.2 | async-start | bytes 786432 | tf_op jit(solution)/shard_map/all_to_all | solution.py:192
  83.7 25.3 %collective-permute-start.5 = (bf16[576,640]{1,0:T(8,128)(2,1)}, bf16[576,640]{1,0:T(8,128)(2,1)}, u32[]{:S(2)}, u32[]{:S(2)}) collective-permute-start(bf16[576,640]{1,0:T(8,128)(2,1)} %collective-permute-done.4.refs_0_), channel_id=1, source_target_pairs={{0,1},{1,0},{2,3},{3,2},{4,5},{5,4},{6,7},{7,6},{8,9},{9,8},{10,11... | collective-permute-start | bytes 2211848 | tf_op jit(solution)/shard_map/ppermute | solution.py:197
  86.4 22.6 %collective-permute-start.7 = (bf16[576,640]{1,0:T(8,128)(2,1)}, bf16[576,640]{1,0:T(8,128)(2,1)}, u32[]{:S(2)}, u32[]{:S(2)}) collective-permute-start(bf16[576,640]{1,0:T(8,128)(2,1)} %collective-permute-done.6.refs_2_), channel_id=1, source_target_pairs={{0,1},{1,0},{2,3},{3,2},{4,5},{5,4},{6,7},{7,6},{8,9},{9,8},{10,11... | collective-permute-start | bytes 2211848 | tf_op jit(solution)/shard_map/ppermute | solution.py:197
  94.3 9.8 %collective-permute-start.10 = (bf16[32,768]{1,0:T(8,128)(2,1)S(1)}, bf16[32,768]{1,0:T(8,128)(2,1)S(1)}, u32[]{:S(2)}, u32[]{:S(2)}) collective-permute-start(bf16[32,768]{1,0:T(8,128)(2,1)S(1)} %get-tuple-element.25), channel_id=1, source_target_pairs={{0,32},{32,0},{1,33},{33,1},{2,34},{34,2},{3,35},{35,3},{4,36},{36... | collective-permute-start | bytes 147464 | tf_op jit(solution)/shard_map/ppermute | solution.py:197
  100.1 1.0 copy-start.12
  101.1 28.8 %collective-permute-start.3 = (bf16[576,640]{1,0:T(8,128)(2,1)}, bf16[576,640]{1,0:T(8,128)(2,1)S(1)}, u32[]{:S(2)}, u32[]{:S(2)}) collective-permute-start(bf16[576,640]{1,0:T(8,128)(2,1)} %hold.2), channel_id=1, source_target_pairs={{0,16},{8,24},{16,0},{24,8},{1,17},{9,25},{17,1},{25,9},{2,18},{10... | collective-permute-start | bytes 2211848 | tf_op jit(solution)/shard_map/ppermute | solution.py:197
  105.1 32.0 %all-to-all-start.3 = ((bf16[32,32,384]{2,1,0:T(8,128)(2,1)}), bf16[32,32,384]{2,1,0:T(8,128)(2,1)S(1)}, u32[]{:S(2)}, u32[]{:S(2)}) async-start(bf16[32,32,384]{2,1,0:T(8,128)(2,1)} %hidden.1), calls=%async_computation.3 | async-start | bytes 1572864 | tf_op jit(solution)/shard_map/all_to_all | solution.py:192
  109.1 1.2 copy-start.13
  117.2 0.7 copy-start.6
  117.9 1.0 copy-start.10
  118.9 0.7 copy-start.14
  129.8 0.9 copy-start.2
  130.7 11.1 %collective-permute-start.9 = (bf16[576,640]{1,0:T(8,128)(2,1)}, bf16[576,640]{1,0:T(8,128)(2,1)}, u32[]{:S(2)}, u32[]{:S(2)}) collective-permute-start(bf16[576,640]{1,0:T(8,128)(2,1)} %hold.3.refs_0_), channel_id=1, source_target_pairs={{0,1},{1,0},{2,3},{3,2},{4,5},{5,4},{6,7},{7,6},{8,9},{9,8},{10,11... | collective-permute-start | bytes 2211848 | tf_op jit(solution)/shard_map/ppermute | solution.py:197
  134.8 0.7 copy-start.17
  137.1 4.7 %copy-start.3 = (bf16[576,640]{1,0:T(8,128)(2,1)S(1)}, bf16[576,640]{1,0:T(8,128)(2,1)}, u32[]{:S(2)}) copy-start(bf16[576,640]{1,0:T(8,128)(2,1)} %hold.3.refs_0_) | copy-start | bytes 2211844
  137.1 4.7 %copy-start.7 = (f32[512,128]{1,0:T(8,128)S(1)}, f32[512,128]{1,0:T(8,128)}, u32[]{:S(2)}) copy-start(f32[512,128]{1,0:T(8,128)} %copy-done.6) | copy-start | bytes 786436
  138.2 10.9 %all-to-all-start.4 = ((bf16[8,32,128]{2,1,0:T(8,128)(2,1)}), bf16[8,32,128]{2,1,0:T(8,128)(2,1)S(1)}, u32[]{:S(2)}, u32[]{:S(2)}) async-start(bf16[8,32,128]{2,1,0:T(8,128)(2,1)} %second.1), calls=%async_computation.4 | async-start | bytes 131072 | tf_op jit(solution)/shard_map/all_to_all | solution.py:192
  141.8 1.2 copy-start.11
  143.1 0.9 copy-start.15

commit v5 on v4

--- a/solution.py
+++ b/solution.py
@@ -16,7 +16,6 @@
 EXPERTS = 16
 CAP = 16
 LANES = 128
-CLAIM = 4
 
 SCALE_LOG2 = 192.0 ** (-0.5) * math.log2(math.e)
 F32 = jnp.float32
@@ -43,32 +42,31 @@
     )(*args)
 
 
-def attention_body(pieces, first, last, spots, queries, base, *refs):
-    keys, refs = refs[:pieces], refs[pieces:]
+def attention_body(chunk, first, last, spots, queries, base, keys, *refs):
     rows = queries.shape[0]
-    row_pos = spots[0] + lax.broadcasted_iota(I32, (rows, 1), 0) // H
+    row_pos = spots[0] + lax.broadcasted_iota(I32, (rows, 1), 0) // H - spots[1]
     query = queries[...]
+    parts = [slice(i * chunk, (i + 1) * chunk) for i in range(keys.shape[0] // chunk)]
+    scored = []
+    for part in parts:
+        scores = lax.dot_general(
+            query, keys[part, :WIDE], (((1,), (1,)), ((), ())), preferred_element_type=F32
+        )
+        scored.append(jnp.where(base[:1, part] <= row_pos, scores * SCALE_LOG2, -jnp.inf))
     if first:
-        top = jnp.full((rows, 1), -1e30, F32)
+        new = jnp.full((rows, 1), -1e30, F32)
     else:
-        top = refs[0][:, :1]
-    scored = []
-    for j, key in enumerate(keys):
-        scores = jnp.dot(query, key[...], preferred_element_type=F32) * SCALE_LOG2
-        scored.append(jnp.where(base[:1, :] <= row_pos - spots[1 + j], scores, -jnp.inf))
-    new = top
+        new = refs[0][:, :1]
     for scores in scored:
         new = jnp.maximum(new, jnp.max(scores, axis=1, keepdims=True))
     den, acc = 0.0, 0.0
     if not first:
-        shrink = jnp.exp2(top - new)
+        shrink = jnp.exp2(refs[0][:, :1] - new)
         den, acc = refs[1][:, :1] * shrink, refs[2][...] * shrink
-    for scores, key in zip(scored, keys):
+    for scores, part in zip(scored, parts):
         weights = jnp.exp2(scores - new)
         den = den + jnp.sum(weights, axis=1, keepdims=True)
-        acc = acc + lax.dot_general(
-            weights.astype(BF16), key[:LAT, :], (((1,), (1,)), ((), ())), preferred_element_type=F32
-        )
+        acc = acc + jnp.dot(weights.astype(BF16), keys[part, :LAT], preferred_element_type=F32)
     if last:
         refs[-1][...] = (acc / den).astype(BF16)
     else:
@@ -77,16 +75,16 @@
         refs[-1][...] = acc
 
 
-def attend(spots, queries, base, pieces, state, last, name):
-    rows, count = queries.shape[0], base.shape[1] * len(pieces)
+def attend(spots, queries, base, keys, state, last, name):
+    rows, count = queries.shape[0], keys.shape[0]
     if last:
         out = shaped((rows, LAT), BF16)
     else:
         out = [shaped((rows, LANES), F32)] * 2 + [shaped((rows, LAT), F32)]
-    body = functools.partial(attention_body, len(pieces), not state, last)
-    specs = [SMEM] + [VMEM] * (2 + len(pieces) + len(state))
-    args = (spots, queries, base, *pieces, *state)
-    return kernel(body, name, out, specs, args, 4 * rows * count * WIDE * CLAIM, (2 * count * WIDE + 2**20) * CLAIM, rows * count * CLAIM)
+    body = functools.partial(attention_body, count // 4, not state, last)
+    specs = [SMEM] + [VMEM] * (3 + len(state))
+    args = (spots, queries, base, keys, *state)
+    return kernel(body, name, out, specs, args, 4 * rows * count * WIDE, 2 * count * WIDE + 2**20, rows * count)
 
 
 def dispatch_body(copies, routes, tokens, *refs):
@@ -209,28 +207,26 @@
 
     own = latents.shape[0] // nc
     half = lax.dynamic_slice_in_dim(latents, core * own, own, 0)
-    column = exchange(jnp.broadcast_to(half[None], (nz * nh,) + half.shape), ("z", "h"))
-    column = column.reshape(nz * nh * own, WIDE)
-
+    half = jnp.pad(half, ((0, 0), (0, -WIDE % LANES)))
+    pair = jnp.concatenate([half, shift(half, "h", 1)], axis=0)
+    plane = jnp.concatenate([pair] + [shift(pair, "x", j) for j in range(1, nx)], axis=0)
+    mine = lax.all_gather(plane, "z", axis=0, tiled=True)
+
+    outgoing = kernel(
+        functools.partial(dispatch_body, nx), "dispatch", shaped((nx * owners, slots, LANES), BF16),
+        [VMEM, VMEM, AFTER], (routes.T, moe_input, plane), 2**20, 2**18,
+    )
+    arrived = exchange(outgoing, ("x", "l", "c"))
     cut = kernel(
         cut_body, "cut", [shaped((held, feats, 2 * units), BF16)] * nx,
         [SMEM, VMEM, VMEM], (where_x, w_gate, w_up), 2**10, 2**21,
     )
     weights = [cut[0]] + [shift(cut[j], "x", j) for j in range(1, nx)]
-    outgoing = kernel(
-        functools.partial(dispatch_body, nx), "dispatch", shaped((nx * owners, slots, LANES), BF16),
-        [VMEM, VMEM] + [AFTER] * nx, (routes.T, moe_input, column, *weights[1:]), 2**20, 2**18,
-    )
-    arrived = exchange(outgoing, ("x", "l", "c"))
-    column = column.T
-    others = [shift(column, "x", 1), shift(column, "x", -1)]
-
     order = [0] + [nx - j for j in range(1, nx)]
     parts = kernel(
         functools.partial(first_body, order), "first", shaped((held * owners * CAP, 2 * units), BF16),
         [SMEM] + [VMEM] * (1 + nx), (where_x, arrived, *weights), 2**28, 2**21,
     )
-    others.append(shift(hold(column, parts), "x", 2))
     parts = exchange(parts.reshape(nz, -1, 2 * units), "z")
     rows = parts.shape[1]
     total, rounded = kernel(
@@ -252,25 +248,16 @@
         [VMEM] * 3, (routes, gate_values, back), 2**20, 2**18,
     )
 
-    sources = [x_at, x_at + nx - 1, x_at + 1, x_at + 2]
-    at_z = lax.broadcasted_iota(I32, (nz, nh, own), 0)
-    at_h = lax.broadcasted_iota(I32, (nz, nh, own), 1)
-    base = ((at_z * nh + at_h) * nx * latents.shape[0] + lax.broadcasted_iota(I32, (nz, nh, own), 2)).reshape(1, -1)
+    mine = hold(mine, result)
+    other = shift(mine, "c", 1)
+    grid = (nz, nx, nh, own)
+    at_z, at_x, at_h, row = (lax.broadcasted_iota(I32, grid, i) for i in range(4))
+    at_x, at_h = (x_at - at_x + nx) % nx, (lax.axis_index("h") + at_h) % nh
+    base = (((at_z * nh + at_h) * nx + at_x) * (nc * own) + row).reshape(1, -1)
     query_rows = queries.reshape(queries.shape[0] * H, WIDE)
-
-    spots = []
-    for source in sources:
-        first = (source % nx) * latents.shape[0]
-        spots.append([first + core * own, first + (nc - 1 - core) * own])
-
-    def call(which, pieces, state, last, name):
-        marks = jnp.stack([offsets[0]] + [s for i in which for s in spots[i]]).astype(I32)
-        both = [p for piece in pieces for p in (piece, shift(piece, "c", 1))]
-        return attend(marks, query_rows, base, both, state, last, name)
-
-    state = call([0], [column], [], False, "attend_own")
-    state = call([1, 2], others[:2], state, False, "attend_near")
-    mixed = call([3], [hold(others[2], state[0])], state, True, "attend_far")
+    marks = [jnp.stack([offsets[0], at * own]).astype(I32) for at in (core, nc - 1 - core)]
+    state = attend(marks[0], query_rows, base, mine, [], False, "attend_mine")
+    mixed = attend(marks[1], query_rows, base, other, state, True, "attend_other")
     attention_out = mixed.reshape(queries.shape[0], H * LAT)
     return (attention_out, moe_output)
 

time: 153 us -> 172 us (1.12); the launches traced: 150 us -> 171 us
  blocking collectives: 0 us -> 27.5 us
  starting transfers between devices: 85.8 us -> 61.8 us
  between operations: 1.67 us -> 15 us
  waiting for transfers between devices: 28.2 us -> 38 us
  local copies, waits for them, and re-layouts: 14.1 us -> 11.1 us
  Pallas kernels: 19.9 us -> 17.4 us
    all_to_all x5 -> x3, starting transfers between devices: 52.4 us -> 20 us  [exchange(): return lax.all_to_all(array, axes, split_axis=0, concat_axis=0, tiled=False)]
    all_to_all x0 -> x1, blocking collectives: none -> 27.5 us  [exchange(): return lax.all_to_all(array, axes, split_axis=0, concat_axis=0, tiled=False)]
    all_to_all x5 -> x3, waiting for transfers between devices: 6.56 us -> 22.1 us  [exchange(): return lax.all_to_all(array, axes, split_axis=0, concat_axis=0, tiled=False)]
    ppermute x11 -> x9, starting transfers between devices: 33.5 us -> 41.8 us  [shift(): lax.ppermute(array, axis, [(i, (i + by) % size) for i in range(size)])]
    ppermute x11 -> x9, waiting for transfers between devices: 21.7 us -> 15.9 us  [shift(): lax.ppermute(array, axis, [(i, (i + by) % size) for i in range(size)])]
    pallas_call x10 -> x9, Pallas kernels: 19.9 us -> 17.4 us  [kernel(): pl.pallas_call(body, out_shape=out_shape, in_specs=specs, out_specs=jax.t...]
    unnamed x39 -> x30, local copies, waits for them, and re-layouts: 10.7 us -> 8.55 us
  transfers between devices with their start and end apart: 16 -> 13, of which waited for: 7 -> 8; matrix products, arithmetic and copies ran while one was open for 3% -> 1% of each run, Pallas kernels for 12% -> 6%
where the time goes in v5:
time: 172 us; the launch traced here: 171 us
  starting transfers between devices  61.8 us (36%)
  waiting for transfers between devices  38 us (22%)
  blocking collectives  27.5 us (16%)
  Pallas kernels  17.4 us (10%)
  between operations  15 us (9%)
  local copies, waits for them, and re-layouts  11.1 us (6%)
    ppermute x9, starting transfers between devices, shift(): lax.ppermute(array, axis, [(i, (i + by) % size) for i in range(size)])  41.8 us
    all_to_all x1, blocking collectives, exchange(): return lax.all_to_all(array, axes, split_axis=0, concat_axis=0, tiled=False)  27.5 us
    all_to_all x3, waiting for transfers between devices, exchange(): return lax.all_to_all(array, axes, split_axis=0, concat_axis=0, tiled=False)  22.1 us
    all_to_all x3, starting transfers between devices, exchange(): return lax.all_to_all(array, axes, split_axis=0, concat_axis=0, tiled=False)  20 us
    pallas_call x9, Pallas kernels, kernel(): pl.pallas_call(body, out_shape=out_shape, in_specs=specs, out_specs=jax.t...  17.4 us
    ppermute x9, waiting for transfers between devices, shift(): lax.ppermute(array, axis, [(i, (i + by) % size) for i in range(size)])  15.9 us
    unnamed x30, local copies, waits for them, and re-layouts  8.55 us
  transfers between devices with their start and end apart: 13, of which 8 were waited for; matrix products, arithmetic and copies ran while one was open for 1% of the time, Pallas kernels for 6%

profile of v5, /device:TPU:1, one launch (start us, length us, event | category | flops | bytes accessed | tf_op | source)
XLA Modules:
  0.0 171.2 jit_solution(4067841698469700606)
XLA Ops:
  7.2 0.0 copy-start
  7.2 0.0 all-gather.2.cloned.1.call-start
  7.2 0.8 copy-done
  8.1 8.3 %collective-permute-start = (bf16[40,640]{1,0:T(8,128)(2,1)S(1)}, bf16[40,640]{1,0:T(8,128)(2,1)S(1)}, u32[]{:S(2)}, u32[]{:S(2)}) collective-permute-start(bf16[40,640]{1,0:T(8,128)(2,1)S(1)} %get-tuple-element.20), channel_id=1, source_target_pairs={{0,32},{32,0},{1,33},{33,1},{2,34},{34,2},{3,35},{35,3},{4,36},{36... | collective-permute-start | bytes 153608 | tf_op jit(solution)/shard_map/ppermute | solution.py:195
  16.4 1.5 collective-permute-done
  17.9 4.4 %collective-permute-start.3 = (bf16[80,640]{1,0:T(8,128)(2,1)S(1)}, bf16[80,640]{1,0:T(8,128)(2,1)S(1)}, u32[]{:S(2)}, u32[]{:S(2)}) collective-permute-start(bf16[80,640]{1,0:T(8,128)(2,1)S(1)} %pad_maximum_fusion), channel_id=1, source_target_pairs={{0,24},{8,0},{16,8},{24,16},{1,25},{9,1},{17,9},{25,17},{2,26},{10... | collective-permute-start | bytes 307208 | tf_op jit(solution)/shard_map/ppermute | solution.py:195
  22.3 2.4 %collective-permute-start.2 = (bf16[80,640]{1,0:T(8,128)(2,1)S(1)}, bf16[80,640]{1,0:T(8,128)(2,1)S(1)}, u32[]{:S(2)}, u32[]{:S(2)}) collective-permute-start(bf16[80,640]{1,0:T(8,128)(2,1)S(1)} %pad_maximum_fusion), channel_id=1, source_target_pairs={{0,16},{8,24},{16,0},{24,8},{1,17},{9,25},{17,1},{25,9},{2,18},{10... | collective-permute-start | bytes 307208 | tf_op jit(solution)/shard_map/ppermute | solution.py:195
  24.8 2.5 %collective-permute-start.1 = (bf16[80,640]{1,0:T(8,128)(2,1)S(1)}, bf16[80,640]{1,0:T(8,128)(2,1)S(1)}, u32[]{:S(2)}, u32[]{:S(2)}) collective-permute-start(bf16[80,640]{1,0:T(8,128)(2,1)S(1)} %pad_maximum_fusion), channel_id=1, source_target_pairs={{0,8},{8,16},{16,24},{24,0},{1,9},{9,17},{17,25},{25,1},{2,10},{10... | collective-permute-start | bytes 307208 | tf_op jit(solution)/shard_map/ppermute | solution.py:195
  27.3 4.1 %collective-permute-done.1 = bf16[80,640]{1,0:T(8,128)(2,1)S(1)} collective-permute-done((bf16[80,640]{1,0:T(8,128)(2,1)S(1)}, bf16[80,640]{1,0:T(8,128)(2,1)S(1)}, u32[]{:S(2)}, u32[]{:S(2)}) %collective-permute-start.1) | collective-permute-done | bytes 102432 | tf_op jit(solution)/shard_map/ppermute | solution.py:195
  31.4 0.0 collective-permute-done.2
  31.4 0.0 collective-permute-done.3
  31.5 0.0 copy-start.2
  31.5 0.7 copy-done.2
  32.2 0.0 all-gather.2.cloned.1.call-update
  32.2 0.0 copy-start.3
  32.2 1.0 copy-done.3
  33.2 0.7 copy-done.6
  33.9 0.7 copy-done.8
  34.6 1.0 dispatch.1
  35.7 10.2 %all-to-all-start = ((bf16[32,32,128]{2,1,0:T(8,128)(2,1)}), bf16[32,32,128]{2,1,0:T(8,128)(2,1)S(1)}, u32[]{:S(2)}, u32[]{:S(2)}) async-start(bf16[32,32,128]{2,1,0:T(8,128)(2,1)} %dispatch.1), calls=%async_computation | async-start | bytes 524288 | tf_op jit(solution)/shard_map/all_to_all | solution.py:190
  45.9 0.0 copy-start.4
  45.9 1.0 copy-done.4
  46.9 1.0 copy-done.5
  48.0 0.1 cut.1
  48.1 3.3 %collective-permute-start.4 = (bf16[2,80,768]{2,1,0:T(8,128)(2,1)S(1)}, bf16[2,80,768]{2,1,0:T(8,128)(2,1)S(1)}, u32[]{:S(2)}, u32[]{:S(2)}) collective-permute-start(bf16[2,80,768]{2,1,0:T(8,128)(2,1)S(1)} %get-tuple-element.12), channel_id=1, source_target_pairs={{0,8},{8,16},{16,24},{24,0},{1,9},{9,17},{17,25},{25,1},{2,10},{10... | collective-permute-start | bytes 737288 | tf_op jit(solution)/shard_map/ppermute | solution.py:195
  51.4 4.4 %collective-permute-start.5 = (bf16[2,80,768]{2,1,0:T(8,128)(2,1)S(1)}, bf16[2,80,768]{2,1,0:T(8,128)(2,1)S(1)}, u32[]{:S(2)}, u32[]{:S(2)}) collective-permute-start(bf16[2,80,768]{2,1,0:T(8,128)(2,1)S(1)} %get-tuple-element.13), channel_id=1, source_target_pairs={{0,16},{8,24},{16,0},{24,8},{1,17},{9,25},{17,1},{25,9},{2,18},{10... | collective-permute-start | bytes 737288 | tf_op jit(solution)/shard_map/ppermute | solution.py:195
  55.8 3.0 %collective-permute-start.6 = (bf16[2,80,768]{2,1,0:T(8,128)(2,1)S(1)}, bf16[2,80,768]{2,1,0:T(8,128)(2,1)S(1)}, u32[]{:S(2)}, u32[]{:S(2)}) collective-permute-start(bf16[2,80,768]{2,1,0:T(8,128)(2,1)S(1)} %get-tuple-element.14), channel_id=1, source_target_pairs={{0,24},{8,0},{16,8},{24,16},{1,25},{9,1},{17,9},{25,17},{2,26},{10... | collective-permute-start | bytes 737288 | tf_op jit(solution)/shard_map/ppermute | solution.py:195
  58.9 0.6 collective-permute-done.4.refs_1_
  59.5 6.3 %collective-permute-done.5.refs_2_ = bf16[2,80,768]{2,1,0:T(8,128)(2,1)S(1)} collective-permute-done((bf16[2,80,768]{2,1,0:T(8,128)(2,1)S(1)}, bf16[2,80,768]{2,1,0:T(8,128)(2,1)S(1)}, u32[]{:S(2)}, u32[]{:S(2)}) %collective-permute-start.5) | collective-permute-done | bytes 245792 | tf_op jit(solution)/shard_map/ppermute | solution.py:195
  65.8 0.3 collective-permute-done.6.refs_3_
  66.1 0.0 all-to-all-done.arrived
  66.1 0.5 first.1
  66.6 27.5 %all_to_all.20.parts = bf16[8,32,768]{2,1,0:T(8,128)(2,1)S(1)} all-to-all(bf16[8,32,768]{2,1,0:T(8,128)(2,1)S(1)} %bitcast.5), channel_id=1, replica_groups=mesh['z'=8,'h'=2,'x'=4,'l'=4,'c'=2] {'z'}, dimensions={0} | all-to-all | bytes 786432 | tf_op jit(solution)/shard_map/all_to_all | solution.py:190
  94.2 0.1 add.115
  94.2 5.7 %collective-permute-start.7 = (bf16[32,768]{1,0:T(8,128)(2,1)S(1)}, bf16[32,768]{1,0:T(8,128)(2,1)S(1)}, u32[]{:S(2)}, u32[]{:S(2)}) collective-permute-start(bf16[32,768]{1,0:T(8,128)(2,1)S(1)} %get-tuple-element.16), channel_id=1, source_target_pairs={{0,32},{32,0},{1,33},{33,1},{2,34},{34,2},{3,35},{35,3},{4,36},{36... | collective-permute-start | bytes 147464 | tf_op jit(solution)/shard_map/ppermute | solution.py:195
  99.9 3.1 %collective-permute-done.7.other = bf16[32,768]{1,0:T(8,128)(2,1)S(1)} collective-permute-done((bf16[32,768]{1,0:T(8,128)(2,1)S(1)}, bf16[32,768]{1,0:T(8,128)(2,1)S(1)}, u32[]{:S(2)}, u32[]{:S(2)}) %collective-permute-start.7) | collective-permute-done | bytes 49184 | tf_op jit(solution)/shard_map/ppermute | solution.py:195
  103.0 1.0 hidden.1
  104.0 5.1 %all-to-all-start.2 = ((bf16[32,32,384]{2,1,0:T(8,128)(2,1)}), bf16[32,32,384]{2,1,0:T(8,128)(2,1)S(1)}, u32[]{:S(2)}, u32[]{:S(2)}) async-start(bf16[32,32,384]{2,1,0:T(8,128)(2,1)} %hidden.1), calls=%async_computation.2 | async-start | bytes 1572864 | tf_op jit(solution)/shard_map/all_to_all | solution.py:190
  109.1 0.0 copy-done.10
  109.1 0.4 copy.15.down
  109.4 18.0 %all-to-all-done.2.hidden = bf16[32,32,384]{2,1,0:T(8,128)(2,1)S(1)} async-done(((bf16[32,32,384]{2,1,0:T(8,128)(2,1)}), bf16[32,32,384]{2,1,0:T(8,128)(2,1)S(1)}, u32[]{:S(2)}, u32[]{:S(2)}) %all-to-all-start.2) | async-done | bytes 786464 | tf_op jit(solution)/shard_map/all_to_all | solution.py:190
  127.4 1.0 second.1.after
  128.4 7.7 %collective-permute-start.8 = (bf16[2560,640]{1,0:T(8,128)(2,1)}, bf16[2560,640]{1,0:T(8,128)(2,1)}, u32[]{:S(2)}, u32[]{:S(2)}) collective-permute-start(bf16[2560,640]{1,0:T(8,128)(2,1)} %hold.1.keys), channel_id=1, source_target_pairs={{0,1},{1,0},{2,3},{3,2},{4,5},{5,4},{6,7},{7,6},{8,9},{9,8},{10,11... | collective-permute-start | bytes 9830408 | tf_op jit(solution)/shard_map/ppermute | solution.py:195
  136.8 0.1 iota.32
  136.9 0.1 iota.33
  137.1 0.1 iota.38
  137.1 0.1 add.86
  137.3 0.1 iota.35
  137.3 0.1 iota.36
  137.5 0.1 iota.40
  137.6 0.1 multiply_add_fusion.base
  137.7 4.7 %all-to-all-start.3 = ((bf16[8,32,128]{2,1,0:T(8,128)(2,1)}), bf16[8,32,128]{2,1,0:T(8,128)(2,1)S(1)}, u32[]{:S(2)}, u32[]{:S(2)}) async-start(bf16[8,32,128]{2,1,0:T(8,128)(2,1)} %second.1.after), calls=%async_computation.3 | async-start | bytes 131072 | tf_op jit(solution)/shard_map/all_to_all | solution.py:190
  142.3 0.1 pad_add_fusion.1.spots
  142.4 0.1 copy.16.routes
  142.5 0.1 copy.17.gates
  142.6 0.7 reshape.151.queries
  143.3 0.1 pad_add_fusion.spots
  143.3 4.1 %all-to-all-done.3.back = bf16[8,32,128]{2,1,0:T(8,128)(2,1)S(1)} async-done(((bf16[8,32,128]{2,1,0:T(8,128)(2,1)}), bf16[8,32,128]{2,1,0:T(8,128)(2,1)S(1)}, u32[]{:S(2)}, u32[]{:S(2)}) %all-to-all-start.3) | async-done | bytes 65568 | tf_op jit(solution)/shard_map/all_to_all | solution.py:190
  147.4 1.0 combine.1
  148.4 1.9 %copy-done.1 = bf16[2560,640]{1,0:T(8,128)(2,1)S(1)} copy-done((bf16[2560,640]{1,0:T(8,128)(2,1)S(1)}, bf16[2560,640]{1,0:T(8,128)(2,1)}, u32[]{:S(2)}) %copy-start.1) | copy-done | bytes 3276824
  150.3 5.7 %attend_mine.1 = (f32[512,128]{1,0:T(8,128)S(1)}, f32[512,128]{1,0:T(8,128)S(1)}, f32[512,512]{1,0:T(8,128)S(1)}) custom-call(s32[2]{0:T(128)S(1)} %pad_add_fusion.1.spots, bf16[512,576]{1,0:T(8,128)(2,1)S(1)} %reshape.151.queries, s32[1,2560]{1,0:T(1,128)S(1)} %multiply_add_fusion.base, bf16[2560,640]{1,0:T(8,128)(2,1)S(1)} %copy-done.1), custom_call_target="tpu_custom_call" | custom-call | flops 3019898880 | bytes 3997696 | tf_op jit(solution)/shard_map/attend_mine/pallas_call | solution.py:34
  156.0 0.0 collective-permute-done.8.keys
  156.0 7.1 %attend_other.1 = bf16[512,512]{1,0:T(8,128)(2,1)S(1)} custom-call(s32[2]{0:T(128)S(1)} %pad_add_fusion.spots, bf16[512,576]{1,0:T(8,128)(2,1)S(1)} %reshape.151.queries, s32[1,2560]{1,0:T(1,128)S(1)} %multiply_add_fusion.base, bf16[2560,640]{1,0:T(8,128)(2,1)} %collective-permute-done.8.keys, f32[512,128]{1,0:T(8,128)S(1)} %get-tuple-element.17.refs_0_, ...), custom_call_target="tpu_custom_call" | custom-call | flops 3019898880 | bytes 3997696 | tf_op jit(solution)/shard_map/attend_other/pallas_call | solution.py:34
  163.2 1.2 reshape.154
  (24 shorter events, 0.1 us)
Async XLA Ops:
  7.2 0.9 copy-start
  7.2 121.2 %all-gather.2.cloned.1.call-start = ((), (), s32[]{:S(2)}) async-start(), calls=%async_computation.4 | async-start | bytes 3686400 | tf_op jit(solution)/shard_map/all_gather | solution.py:213
  8.1 9.8 %collective-permute-start = (bf16[40,640]{1,0:T(8,128)(2,1)S(1)}, bf16[40,640]{1,0:T(8,128)(2,1)S(1)}, u32[]{:S(2)}, u32[]{:S(2)}) collective-permute-start(bf16[40,640]{1,0:T(8,128)(2,1)S(1)} %get-tuple-element.20), channel_id=1, source_target_pairs={{0,32},{32,0},{1,33},{33,1},{2,34},{34,2},{3,35},{35,3},{4,36},{36... | collective-permute-start | bytes 153608 | tf_op jit(solution)/shard_map/ppermute | solution.py:195
  17.9 13.5 %collective-permute-start.3 = (bf16[80,640]{1,0:T(8,128)(2,1)S(1)}, bf16[80,640]{1,0:T(8,128)(2,1)S(1)}, u32[]{:S(2)}, u32[]{:S(2)}) collective-permute-start(bf16[80,640]{1,0:T(8,128)(2,1)S(1)} %pad_maximum_fusion), channel_id=1, source_target_pairs={{0,24},{8,0},{16,8},{24,16},{1,25},{9,1},{17,9},{25,17},{2,26},{10... | collective-permute-start | bytes 307208 | tf_op jit(solution)/shard_map/ppermute | solution.py:195
  22.3 9.1 %collective-permute-start.2 = (bf16[80,640]{1,0:T(8,128)(2,1)S(1)}, bf16[80,640]{1,0:T(8,128)(2,1)S(1)}, u32[]{:S(2)}, u32[]{:S(2)}) collective-permute-start(bf16[80,640]{1,0:T(8,128)(2,1)S(1)} %pad_maximum_fusion), channel_id=1, source_target_pairs={{0,16},{8,24},{16,0},{24,8},{1,17},{9,25},{17,1},{25,9},{2,18},{10... | collective-permute-start | bytes 307208 | tf_op jit(solution)/shard_map/ppermute | solution.py:195
  24.8 6.6 %collective-permute-start.1 = (bf16[80,640]{1,0:T(8,128)(2,1)S(1)}, bf16[80,640]{1,0:T(8,128)(2,1)S(1)}, u32[]{:S(2)}, u32[]{:S(2)}) collective-permute-start(bf16[80,640]{1,0:T(8,128)(2,1)S(1)} %pad_maximum_fusion), channel_id=1, source_target_pairs={{0,8},{8,16},{16,24},{24,0},{1,9},{9,17},{17,25},{25,1},{2,10},{10... | collective-permute-start | bytes 307208 | tf_op jit(solution)/shard_map/ppermute | solution.py:195
  31.5 0.8 copy-start.2
  32.2 1.0 copy-start.3
  33.2 0.7 copy-start.6
  33.9 0.7 copy-start.8
  35.7 73.4 %copy-start.10 = (bf16[2,1536,80]{1,2,0:T(8,128)(2,1)S(1)}, bf16[2,1536,80]{1,2,0:T(8,128)(2,1)}, u32[]{:S(2)}) copy-start(bf16[2,1536,80]{1,2,0:T(8,128)(2,1)} %param.17) | copy-start | bytes 1474564
  35.7 30.4 %all-to-all-start = ((bf16[32,32,128]{2,1,0:T(8,128)(2,1)}), bf16[32,32,128]{2,1,0:T(8,128)(2,1)S(1)}, u32[]{:S(2)}, u32[]{:S(2)}) async-start(bf16[32,32,128]{2,1,0:T(8,128)(2,1)} %dispatch.1), calls=%async_computation | async-start | bytes 524288 | tf_op jit(solution)/shard_map/all_to_all | solution.py:190
  45.9 1.0 copy-start.4
  46.9 1.0 copy-start.5
  48.1 11.4 %collective-permute-start.4 = (bf16[2,80,768]{2,1,0:T(8,128)(2,1)S(1)}, bf16[2,80,768]{2,1,0:T(8,128)(2,1)S(1)}, u32[]{:S(2)}, u32[]{:S(2)}) collective-permute-start(bf16[2,80,768]{2,1,0:T(8,128)(2,1)S(1)} %get-tuple-element.12), channel_id=1, source_target_pairs={{0,8},{8,16},{16,24},{24,0},{1,9},{9,17},{17,25},{25,1},{2,10},{10... | collective-permute-start | bytes 737288 | tf_op jit(solution)/shard_map/ppermute | solution.py:195
  51.4 14.4 %collective-permute-start.5 = (bf16[2,80,768]{2,1,0:T(8,128)(2,1)S(1)}, bf16[2,80,768]{2,1,0:T(8,128)(2,1)S(1)}, u32[]{:S(2)}, u32[]{:S(2)}) collective-permute-start(bf16[2,80,768]{2,1,0:T(8,128)(2,1)S(1)} %get-tuple-element.13), channel_id=1, source_target_pairs={{0,16},{8,24},{16,0},{24,8},{1,17},{9,25},{17,1},{25,9},{2,18},{10... | collective-permute-start | bytes 737288 | tf_op jit(solution)/shard_map/ppermute | solution.py:195
  55.8 10.3 %collective-permute-start.6 = (bf16[2,80,768]{2,1,0:T(8,128)(2,1)S(1)}, bf16[2,80,768]{2,1,0:T(8,128)(2,1)S(1)}, u32[]{:S(2)}, u32[]{:S(2)}) collective-permute-start(bf16[2,80,768]{2,1,0:T(8,128)(2,1)S(1)} %get-tuple-element.14), channel_id=1, source_target_pairs={{0,24},{8,0},{16,8},{24,16},{1,25},{9,1},{17,9},{25,17},{2,26},{10... | collective-permute-start | bytes 737288 | tf_op jit(solution)/shard_map/ppermute | solution.py:195
  94.2 8.8 %collective-permute-start.7 = (bf16[32,768]{1,0:T(8,128)(2,1)S(1)}, bf16[32,768]{1,0:T(8,128)(2,1)S(1)}, u32[]{:S(2)}, u32[]{:S(2)}) collective-permute-start(bf16[32,768]{1,0:T(8,128)(2,1)S(1)} %get-tuple-element.16), channel_id=1, source_target_pairs={{0,32},{32,0},{1,33},{33,1},{2,34},{34,2},{3,35},{35,3},{4,36},{36... | collective-permute-start | bytes 147464 | tf_op jit(solution)/shard_map/ppermute | solution.py:195
  104.0 23.4 %all-to-all-start.2 = ((bf16[32,32,384]{2,1,0:T(8,128)(2,1)}), bf16[32,32,384]{2,1,0:T(8,128)(2,1)S(1)}, u32[]{:S(2)}, u32[]{:S(2)}) async-start(bf16[32,32,384]{2,1,0:T(8,128)(2,1)} %hidden.1), calls=%async_computation.2 | async-start | bytes 1572864 | tf_op jit(solution)/shard_map/all_to_all | solution.py:190
  128.4 14.0 %copy-start.7 = (s32[32,6]{0,1:T(8,128)S(1)}, s32[32,6]{0,1:T(8,128)}, u32[]{:S(2)}) copy-start(s32[32,6]{0,1:T(8,128)} %param.13) | copy-start | bytes 2308
  128.4 14.1 %copy-start.11 = (f32[32,6]{0,1:T(8,128)S(1)}, f32[32,6]{0,1:T(8,128)}, u32[]{:S(2)}) copy-start(f32[32,6]{0,1:T(8,128)} %param.14) | copy-start | bytes 2308
  128.4 14.2 %copy-start.9 = (bf16[4,73728]{1,0:T(4,128)(2,1)S(1)}, bf16[4,73728]{1,0:T(4,128)(2,1)}, u32[]{:S(2)}) copy-start(bf16[4,73728]{1,0:T(4,128)(2,1)} %param.9) | copy-start | bytes 1769476
  128.4 27.6 %collective-permute-start.8 = (bf16[2560,640]{1,0:T(8,128)(2,1)}, bf16[2560,640]{1,0:T(8,128)(2,1)}, u32[]{:S(2)}, u32[]{:S(2)}) collective-permute-start(bf16[2560,640]{1,0:T(8,128)(2,1)} %hold.1.keys), channel_id=1, source_target_pairs={{0,1},{1,0},{2,3},{3,2},{4,5},{5,4},{6,7},{7,6},{8,9},{9,8},{10,11... | collective-permute-start | bytes 9830408 | tf_op jit(solution)/shard_map/ppermute | solution.py:195
  137.7 9.7 %all-to-all-start.3 = ((bf16[8,32,128]{2,1,0:T(8,128)(2,1)}), bf16[8,32,128]{2,1,0:T(8,128)(2,1)S(1)}, u32[]{:S(2)}, u32[]{:S(2)}) async-start(bf16[8,32,128]{2,1,0:T(8,128)(2,1)} %second.1.after), calls=%async_computation.3 | async-start | bytes 131072 | tf_op jit(solution)/shard_map/all_to_all | solution.py:190
  148.4 1.9 %copy-start.1 = (bf16[2560,640]{1,0:T(8,128)(2,1)S(1)}, bf16[2560,640]{1,0:T(8,128)(2,1)}, u32[]{:S(2)}) copy-start(bf16[2560,640]{1,0:T(8,128)(2,1)} %hold.1.keys) | copy-start | bytes 9830404
Sparse Core Ops, SparseCore 0:
  32.4 64.5 all-gather.1

commit v6 on v4

--- a/solution.py
+++ b/solution.py
@@ -16,7 +16,7 @@
 EXPERTS = 16
 CAP = 16
 LANES = 128
-CLAIM = 4
+CLAIM = 16
 
 SCALE_LOG2 = 192.0 ** (-0.5) * math.log2(math.e)
 F32 = jnp.float32
@@ -37,7 +37,7 @@
         out_shape=out_shape,
         in_specs=specs,
         out_specs=jax.tree.map(lambda _: VMEM, out_shape),
-        compiler_params=pltpu.CompilerParams(vmem_limit_bytes=24 * 2**20),
+        compiler_params=pltpu.CompilerParams(vmem_limit_bytes=(24 if special > 2**16 else 12) * 2**20),
         cost_estimate=pl.CostEstimate(flops=flops, bytes_accessed=moved, transcendentals=special),
         name=name,
     )(*args)
@@ -72,9 +72,10 @@
     if last:
         refs[-1][...] = (acc / den).astype(BF16)
     else:
-        refs[-3][...] = jnp.broadcast_to(new, (rows, LANES))
-        refs[-2][...] = jnp.broadcast_to(den, (rows, LANES))
-        refs[-1][...] = acc
+        refs[-4][...] = jnp.broadcast_to(new, (rows, LANES))
+        refs[-3][...] = jnp.broadcast_to(den, (rows, LANES))
+        refs[-2][...] = acc
+        refs[-1][...] = jnp.zeros(refs[-1].shape, F32)
 
 
 def attend(spots, queries, base, pieces, state, last, name):
@@ -82,16 +83,16 @@
     if last:
         out = shaped((rows, LAT), BF16)
     else:
-        out = [shaped((rows, LANES), F32)] * 2 + [shaped((rows, LAT), F32)]
+        out = [shaped((rows, LANES), F32)] * 2 + [shaped((rows, LAT), F32), shaped((8, LANES), F32)]
     body = functools.partial(attention_body, len(pieces), not state, last)
     specs = [SMEM] + [VMEM] * (2 + len(pieces) + len(state))
     args = (spots, queries, base, *pieces, *state)
     return kernel(body, name, out, specs, args, 4 * rows * count * WIDE * CLAIM, (2 * count * WIDE + 2**20) * CLAIM, rows * count * CLAIM)
 
 
-def dispatch_body(copies, routes, tokens, *refs):
-    out = refs[-1]
-    count = tokens.shape[0]
+def dispatch_body(order, spots, routes, *refs):
+    pieces, out = refs[: len(order)], refs[-1]
+    count = routes.shape[1]
     slot = lax.broadcasted_iota(I32, (EXPERTS * CAP, count), 0)
     named = routes[0:1, :] == slot // CAP
     for k in range(1, TOPK):
@@ -100,50 +101,48 @@
     earlier = lax.broadcasted_iota(I32, (count, count), 0) < lax.broadcasted_iota(I32, (count, count), 1)
     rank = jnp.dot(hot.astype(BF16), earlier.astype(F32).astype(BF16), preferred_element_type=F32)
     placed = jnp.where(rank == (slot % CAP).astype(F32), hot, 0.0).astype(BF16)
-    sent = jnp.dot(placed, tokens[...], preferred_element_type=F32).astype(BF16)
-    owners = out.shape[0] // copies
-    out[...] = jnp.zeros(out.shape, BF16)
-    for i in range(copies):
-        out[i * owners : (i + 1) * owners, :, : tokens.shape[1]] = sent.reshape(owners, -1, tokens.shape[1])
-
-
-def cut_body(spots, gate, up, *outs):
+    owners = out.shape[0]
+    for j, piece in enumerate(pieces):
+        tokens = piece[piece.shape[0] - count :, :LANES]
+        sent = jnp.dot(placed, tokens, preferred_element_type=F32).astype(BF16)
+        out[:, :, j * LANES : (j + 1) * LANES] = sent.reshape(owners, -1, LANES)
+
+
+def cut_body(spots, gate, up, tokens, *outs):
     parts = len(outs)
-    units = gate.shape[2] // parts
+    held, feats, width = gate.shape
+    units = width // parts
     for j, out in enumerate(outs):
         at = pl.multiple_of(lax.rem(spots[0] + j, parts) * units, LANES)
-        out[:, :, :units] = gate[:, :, pl.ds(at, units)]
-        out[:, :, units:] = up[:, :, pl.ds(at, units)]
-
-
-def first_body(order, spots, arrived, *refs):
+        for e in range(held):
+            out[e * feats : (e + 1) * feats, :units] = gate[e, :, pl.ds(at, units)]
+            out[e * feats : (e + 1) * feats, units:] = up[e, :, pl.ds(at, units)]
+        out[held * feats :, :] = jnp.zeros((out.shape[0] - held * feats, 2 * units), BF16)
+        out[held * feats :, : tokens.shape[1]] = tokens[...]
+
+
+def first_body(feats, arrived, *refs):
     weights, out = refs[:-1], refs[-1]
-    held, feats = weights[0].shape[:2]
-    owners = arrived.shape[0] // len(weights)
-    for e in range(held):
+    owners = arrived.shape[0]
+    for e in range(arrived.shape[1] // CAP):
         total = 0.0
-        for j, matrix in zip(order, weights):
-            at = lax.rem(spots[0] + j, len(weights)) * owners
-            rows = arrived[pl.ds(at, owners), e * CAP : (e + 1) * CAP, :].reshape(owners * CAP, LANES)
-            total = total + jnp.dot(rows[:, :feats], matrix[e], preferred_element_type=F32)
+        for j, matrix in enumerate(weights):
+            rows = arrived[:, e * CAP : (e + 1) * CAP, j * LANES : (j + 1) * LANES].reshape(owners * CAP, LANES)
+            part = matrix[e * feats : (e + 1) * feats, :]
+            total = total + jnp.dot(rows[:, :feats], part, preferred_element_type=F32)
         out[e * owners * CAP : (e + 1) * owners * CAP, :] = total.astype(BF16)
 
 
-def add_body(parts, total, rounded):
+def hidden_body(parts, out, token):
     sums = parts[0].astype(F32)
     for i in range(1, parts.shape[0]):
         sums = sums + parts[i].astype(F32)
-    total[...] = sums
-    rounded[...] = sums.astype(BF16)
-
-
-def hidden_body(total, other, out):
-    sums = total[...] + other[...].astype(F32)
     units = sums.shape[1] // 2
     gate = sums[:, :units]
     hidden = (gate / (1.0 + jnp.exp(-gate)) * sums[:, units:]).astype(BF16)
     for i in range(out.shape[0]):
         out[i] = hidden
+    token[...] = jnp.zeros(token.shape, F32)
 
 
 def second_body(deep, across, hidden, down, out):
@@ -177,15 +176,16 @@
     out[...] = mixed.astype(BF16)
 
 
-def hold(array, after):
+def hold(arrays, after):
     return pl.pallas_call(
-        lambda array, after, out: None,
-        out_shape=shaped(array.shape, array.dtype),
-        in_specs=[AFTER] * 2,
-        out_specs=AFTER,
-        input_output_aliases={0: 0},
+        lambda *refs: None,
+        out_shape=[shaped(a.shape, a.dtype) for a in arrays],
+        in_specs=[AFTER] * (len(arrays) + len(after)),
+        out_specs=[AFTER] * len(arrays),
+        input_output_aliases={i: i for i in range(len(arrays))},
+        compiler_params=pltpu.CompilerParams(vmem_limit_bytes=2**20),
         name="hold",
-    )(array, after)
+    )(*arrays, *after)
 
 
 def exchange(array, axes):
@@ -213,37 +213,31 @@
     column = column.reshape(nz * nh * own, WIDE)
 
     cut = kernel(
-        cut_body, "cut", [shaped((held, feats, 2 * units), BF16)] * nx,
-        [SMEM, VMEM, VMEM], (where_x, w_gate, w_up), 2**10, 2**21,
+        cut_body, "cut", [shaped((held * feats + tokens, 2 * units), BF16)] * nx,
+        [SMEM] + [VMEM] * 3, (where_x, w_gate, w_up, moe_input), 2**10, 2**21,
     )
     weights = [cut[0]] + [shift(cut[j], "x", j) for j in range(1, nx)]
+    order = [0] + [nx - j for j in range(1, nx)]
     outgoing = kernel(
-        functools.partial(dispatch_body, nx), "dispatch", shaped((nx * owners, slots, LANES), BF16),
-        [VMEM, VMEM] + [AFTER] * nx, (routes.T, moe_input, column, *weights[1:]), 2**20, 2**18,
-    )
-    arrived = exchange(outgoing, ("x", "l", "c"))
+        functools.partial(dispatch_body, order), "dispatch", shaped((owners, slots, nx * LANES), BF16),
+        [SMEM] + [VMEM] * (1 + nx) + [AFTER], (where_x, routes.T, *weights, column), 2**20, 2**18,
+    )
+    arrived = exchange(outgoing, ("l", "c"))
     column = column.T
-    others = [shift(column, "x", 1), shift(column, "x", -1)]
-
-    order = [0] + [nx - j for j in range(1, nx)]
+    others = [shift(column, "x", 1), shift(column, "x", -1), shift(column, "x", 2)]
+
     parts = kernel(
-        functools.partial(first_body, order), "first", shaped((held * owners * CAP, 2 * units), BF16),
-        [SMEM] + [VMEM] * (1 + nx), (where_x, arrived, *weights), 2**28, 2**21,
-    )
-    others.append(shift(hold(column, parts), "x", 2))
-    parts = exchange(parts.reshape(nz, -1, 2 * units), "z")
-    rows = parts.shape[1]
-    total, rounded = kernel(
-        add_body, "add", [shaped((rows, 2 * units), F32), shaped((rows, 2 * units), BF16)],
-        [VMEM], (parts,), 2**18, 2**19,
-    )
-    hidden = kernel(
-        hidden_body, "hidden", shaped((nz * nx, rows, units), BF16),
-        [VMEM] * 2, (total, shift(rounded, "h", 1)), 2**18, 2**20, 2**14,
-    )
-    hidden = exchange(hidden, ("z", "x"))
+        functools.partial(first_body, feats), "first", shaped((held * owners * CAP, 2 * units), BF16),
+        [VMEM] * (1 + nx), (arrived, *weights), 2**28, 2**21,
+    )
+    parts = exchange(parts.reshape(nz * nh, -1, 2 * units), ("z", "h"))
+    hidden, token = kernel(
+        hidden_body, "hidden", [shaped((nz * nh * nx, parts.shape[1], units), BF16), shaped((8, LANES), F32)],
+        [VMEM], (parts,), 2**18, 2**20, 2**14,
+    )
+    hidden = exchange(hidden, ("z", "h", "x"))
     result = kernel(
-        functools.partial(second_body, nz, nx), "second", shaped((owners, slots, LANES), BF16),
+        functools.partial(second_body, nz * nh, nx), "second", shaped((owners, slots, LANES), BF16),
         [VMEM] * 2, (hidden, w_down), 2**27, 2**21,
     )
     back = exchange(result, ("l", "c"))
@@ -268,9 +262,8 @@
         both = [p for piece in pieces for p in (piece, shift(piece, "c", 1))]
         return attend(marks, query_rows, base, both, state, last, name)
 
-    state = call([0], [column], [], False, "attend_own")
-    state = call([1, 2], others[:2], state, False, "attend_near")
-    mixed = call([3], [hold(others[2], state[0])], state, True, "attend_far")
+    *state, seen = call([0], [column], [], False, "attend_own")
+    mixed = call([1, 2, 3], hold(others, [token, seen]), state, True, "attend_rest")
     attention_out = mixed.reshape(queries.shape[0], H * LAT)
     return (attention_out, moe_output)
 

time: 153 us -> 158 us (1.033)
  the two profiles are of different devices: /device:TPU:1 before, /device:TPU:63 now
where the time goes in v6:
time: 158 us; the launch traced here: 157 us
  starting transfers between devices  74.2 us (47%)
  waiting for transfers between devices  31.5 us (20%)
  blocking collectives  20.5 us (13%)
  Pallas kernels  17.8 us (11%)
  local copies, waits for them, and re-layouts  11.1 us (7%)
  between operations  1.65 us (1%)
    all_to_all x4, starting transfers between devices, exchange(): return lax.all_to_all(array, axes, split_axis=0, concat_axis=0, tiled=False)  47.2 us
    ppermute x10, waiting for transfers between devices, shift(): lax.ppermute(array, axis, [(i, (i + by) % size) for i in range(size)])  30.1 us
    ppermute x10, starting transfers between devices, shift(): lax.ppermute(array, axis, [(i, (i + by) % size) for i in range(size)])  27 us
    all_to_all x1, blocking collectives, exchange(): return lax.all_to_all(array, axes, split_axis=0, concat_axis=0, tiled=False)  20.5 us
    pallas_call x8, Pallas kernels, kernel(): pl.pallas_call(body, out_shape=out_shape, in_specs=specs, out_specs=jax.t...  17.8 us
    unnamed x33, local copies, waits for them, and re-layouts  6.86 us
  transfers between devices with their start and end apart: 14, of which 5 were waited for; matrix products, arithmetic and copies ran while one was open for 3% of the time, Pallas kernels for 10%

profile of v6, /device:TPU:63, one launch (start us, length us, event | category | flops | bytes accessed | tf_op | source)
XLA Modules:
  0.0 157.0 jit_solution(17733193248430224957)
XLA Ops:
  0.6 0.0 copy-start
  0.7 0.9 copy-done
  1.5 1.0 broadcast_in_dim.2
  2.5 15.3 %all-to-all-start = ((bf16[16,40,576]{2,1,0:T(8,128)(2,1)}), bf16[16,40,576]{2,1,0:T(8,128)(2,1)S(1)}, u32[]{:S(2)}, u32[]{:S(2)}) async-start(bf16[16,40,576]{2,1,0:T(8,128)(2,1)} %broadcast_in_dim.2), calls=%async_computation | async-start | bytes 1638400 | tf_op jit(solution)/shard_map/all_to_all | solution.py:192
  17.8 0.0 copy-done.3
  17.8 0.0 copy-done.4
  17.8 0.0 copy-done.6
  17.8 0.1 cut.1
  17.9 2.1 %collective-permute-start.3 = (bf16[192,768]{1,0:T(8,128)(2,1)S(1)}, bf16[192,768]{1,0:T(8,128)(2,1)S(1)}, u32[]{:S(2)}, u32[]{:S(2)}) collective-permute-start(bf16[192,768]{1,0:T(8,128)(2,1)S(1)} %get-tuple-element.16), channel_id=1, source_target_pairs={{0,8},{8,16},{16,24},{24,0},{1,9},{9,17},{17,25},{25,1},{2,10},{10... | collective-permute-start | bytes 884744 | tf_op jit(solution)/shard_map/ppermute | solution.py:197
  20.0 0.0 copy-start.5
  20.0 4.0 %collective-permute-start.4 = (bf16[192,768]{1,0:T(8,128)(2,1)S(1)}, bf16[192,768]{1,0:T(8,128)(2,1)S(1)}, u32[]{:S(2)}, u32[]{:S(2)}) collective-permute-start(bf16[192,768]{1,0:T(8,128)(2,1)S(1)} %get-tuple-element.17), channel_id=1, source_target_pairs={{0,16},{8,24},{16,0},{24,8},{1,17},{9,25},{17,1},{25,9},{2,18},{10... | collective-permute-start | bytes 884744 | tf_op jit(solution)/shard_map/ppermute | solution.py:197
  24.1 1.9 %collective-permute-start.5 = (bf16[192,768]{1,0:T(8,128)(2,1)S(1)}, bf16[192,768]{1,0:T(8,128)(2,1)S(1)}, u32[]{:S(2)}, u32[]{:S(2)}) collective-permute-start(bf16[192,768]{1,0:T(8,128)(2,1)S(1)} %get-tuple-element.18), channel_id=1, source_target_pairs={{0,24},{8,0},{16,8},{24,16},{1,25},{9,1},{17,9},{25,17},{2,26},{10... | collective-permute-start | bytes 884744 | tf_op jit(solution)/shard_map/ppermute | solution.py:197
  26.0 1.0 collective-permute-done.3.refs_1_
  27.1 3.4 %collective-permute-done.4.refs_2_ = bf16[192,768]{1,0:T(8,128)(2,1)S(1)} collective-permute-done((bf16[192,768]{1,0:T(8,128)(2,1)S(1)}, bf16[192,768]{1,0:T(8,128)(2,1)S(1)}, u32[]{:S(2)}, u32[]{:S(2)}) %collective-permute-start.4) | collective-permute-done | bytes 294944 | tf_op jit(solution)/shard_map/ppermute | solution.py:197
  30.4 7.4 %collective-permute-done.5.refs_3_ = bf16[192,768]{1,0:T(8,128)(2,1)S(1)} collective-permute-done((bf16[192,768]{1,0:T(8,128)(2,1)S(1)}, bf16[192,768]{1,0:T(8,128)(2,1)S(1)}, u32[]{:S(2)}, u32[]{:S(2)}) %collective-permute-start.5) | collective-permute-done | bytes 294944 | tf_op jit(solution)/shard_map/ppermute | solution.py:197
  37.8 1.5 all-to-all-done
  39.3 0.0 copy-done.5
  39.3 0.4 dispatch.1
  39.7 20.5 %all_to_all.25.arrived = bf16[8,32,512]{2,1,0:T(8,128)(2,1)S(1)} all-to-all(bf16[8,32,512]{2,1,0:T(8,128)(2,1)S(1)} %dispatch.1), channel_id=1, replica_groups=mesh['z'=8,'h'=2,'x'=4,'l'=4,'c'=2] {'l','c'}, dimensions={0} | all-to-all | bytes 524288 | tf_op jit(solution)/shard_map/all_to_all | solution.py:192
  60.2 1.3 first.1
  61.4 11.4 %all-to-all-start.2 = ((bf16[16,16,768]{2,1,0:T(8,128)(2,1)}), bf16[16,16,768]{2,1,0:T(8,128)(2,1)S(1)}, u32[]{:S(2)}, u32[]{:S(2)}) async-start(bf16[16,16,768]{2,1,0:T(8,128)(2,1)} %bitcast.10), calls=%async_computation.2 | async-start | bytes 786432 | tf_op jit(solution)/shard_map/all_to_all | solution.py:192
  72.9 0.4 copy.19
  73.3 2.9 %collective-permute-start.6 = (bf16[576,640]{1,0:T(8,128)(2,1)S(1)}, bf16[576,640]{1,0:T(8,128)(2,1)}, u32[]{:S(2)}, u32[]{:S(2)}) collective-permute-start(bf16[576,640]{1,0:T(8,128)(2,1)S(1)} %bitcast.15), channel_id=1, source_target_pairs={{0,1},{1,0},{2,3},{3,2},{4,5},{5,4},{6,7},{7,6},{8,9},{9,8},{10,11... | collective-permute-start | bytes 2211848 | tf_op jit(solution)/shard_map/ppermute | solution.py:197
  76.8 0.0 copy-done.13
  76.9 1.6 reshape.61.queries
  78.4 0.1 iota_add_fusion
  78.5 0.1 add.93.base
  78.6 0.1 pad_add_fusion.spots
  78.7 2.1 %collective-permute-start = (bf16[576,640]{1,0:T(8,128)(2,1)S(1)}, bf16[576,640]{1,0:T(8,128)(2,1)S(1)}, u32[]{:S(2)}, u32[]{:S(2)}) collective-permute-start(bf16[576,640]{1,0:T(8,128)(2,1)S(1)} %bitcast.16), channel_id=1, source_target_pairs={{0,8},{8,16},{16,24},{24,0},{1,9},{9,17},{17,25},{25,1},{2,10},{10... | collective-permute-start | bytes 2211848 | tf_op jit(solution)/shard_map/ppermute | solution.py:197
  80.8 3.2 %collective-permute-start.1 = (bf16[576,640]{1,0:T(8,128)(2,1)S(1)}, bf16[576,640]{1,0:T(8,128)(2,1)S(1)}, u32[]{:S(2)}, u32[]{:S(2)}) collective-permute-start(bf16[576,640]{1,0:T(8,128)(2,1)S(1)} %bitcast.17), channel_id=1, source_target_pairs={{0,24},{8,0},{16,8},{24,16},{1,25},{9,1},{17,9},{25,17},{2,26},{10... | collective-permute-start | bytes 2211848 | tf_op jit(solution)/shard_map/ppermute | solution.py:197
  84.0 3.0 %collective-permute-start.2 = (bf16[576,640]{1,0:T(8,128)(2,1)S(1)}, bf16[576,640]{1,0:T(8,128)(2,1)}, u32[]{:S(2)}, u32[]{:S(2)}) collective-permute-start(bf16[576,640]{1,0:T(8,128)(2,1)S(1)} %bitcast.18), channel_id=1, source_target_pairs={{0,16},{8,24},{16,0},{24,8},{1,17},{9,25},{17,1},{25,9},{2,18},{10... | collective-permute-start | bytes 2211848 | tf_op jit(solution)/shard_map/ppermute | solution.py:197
  87.0 0.0 all-to-all-done.2.parts
  87.0 1.0 hidden.1
  88.0 14.7 %all-to-all-start.3 = ((bf16[64,16,384]{2,1,0:T(8,128)(2,1)}), bf16[64,16,384]{2,1,0:T(8,128)(2,1)S(1)}, u32[]{:S(2)}, u32[]{:S(2)}) async-start(bf16[64,16,384]{2,1,0:T(8,128)(2,1)} %get-tuple-element.27), calls=%async_computation.3 | async-start | bytes 1572864 | tf_op jit(solution)/shard_map/all_to_all | solution.py:192
  102.7 0.0 collective-permute-done.6.refs_1_
  102.7 0.0 copy-start.1
  102.8 1.1 copy-done.1
  103.8 3.7 %attend_own.1 = (f32[512,128]{1,0:T(8,128)S(1)}, f32[512,128]{1,0:T(8,128)S(1)}, f32[512,512]{1,0:T(8,128)S(1)}, f32[8,128]{1,0:T(8,128)S(1)}) custom-call(s32[3]{0:T(128)S(1)} %pad_add_fusion.spots, bf16[512,576]{1,0:T(8,128)(2,1)S(1)} %copy-done.1, s32[1,640]{1,0:T(1,128)S(1)} %add.93.base, bf16[576,640]{1,0:T(8,128)(2,1)S(1)} %bitcast.19, ...), custom_call_target="tpu_custom_call" | custom-call | flops 24159191040 | bytes 40370176 | tf_op jit(solution)/shard_map/attend_own/pallas_call | solution.py:35
  107.6 0.0 copy-start.7
  107.6 0.0 copy-start.9
  107.6 0.0 collective-permute-done.refs_0_
  107.6 0.0 collective-permute-done.1.refs_1_
  107.6 18.2 %collective-permute-done.2.refs_2_ = bf16[576,640]{1,0:T(8,128)(2,1)} collective-permute-done((bf16[576,640]{1,0:T(8,128)(2,1)S(1)}, bf16[576,640]{1,0:T(8,128)(2,1)}, u32[]{:S(2)}, u32[]{:S(2)}) %collective-permute-start.2) | collective-permute-done | bytes 737312 | tf_op jit(solution)/shard_map/ppermute | solution.py:197
  125.8 0.0 copy-done.7
  125.9 3.4 %collective-permute-start.7 = (bf16[576,640]{1,0:T(8,128)(2,1)S(1)}, bf16[576,640]{1,0:T(8,128)(2,1)}, u32[]{:S(2)}, u32[]{:S(2)}) collective-permute-start(bf16[576,640]{1,0:T(8,128)(2,1)S(1)} %get-tuple-element.21.refs_0_), channel_id=1, source_target_pairs={{0,1},{1,0},{2,3},{3,2},{4,5},{5,4},{6,7},{7,6},{8,9},{9,8},{10,11... | collective-permute-start | bytes 2211848 | tf_op jit(solution)/shard_map/ppermute | solution.py:197
  129.3 1.9 %collective-permute-start.8 = (bf16[576,640]{1,0:T(8,128)(2,1)S(1)}, bf16[576,640]{1,0:T(8,128)(2,1)}, u32[]{:S(2)}, u32[]{:S(2)}) collective-permute-start(bf16[576,640]{1,0:T(8,128)(2,1)S(1)} %get-tuple-element.22.refs_2_), channel_id=1, source_target_pairs={{0,1},{1,0},{2,3},{3,2},{4,5},{5,4},{6,7},{7,6},{8,9},{9,8},{10,11... | collective-permute-start | bytes 2211848 | tf_op jit(solution)/shard_map/ppermute | solution.py:197
  131.2 2.4 %collective-permute-start.9 = (bf16[576,640]{1,0:T(8,128)(2,1)}, bf16[576,640]{1,0:T(8,128)(2,1)}, u32[]{:S(2)}, u32[]{:S(2)}) collective-permute-start(bf16[576,640]{1,0:T(8,128)(2,1)} %get-tuple-element.23.refs_4_), channel_id=1, source_target_pairs={{0,1},{1,0},{2,3},{3,2},{4,5},{5,4},{6,7},{7,6},{8,9},{9,8},{10,11... | collective-permute-start | bytes 2211848 | tf_op jit(solution)/shard_map/ppermute | solution.py:197
  133.7 0.1 copy.21.routes
  133.8 1.4 copy.20.down
  135.2 0.1 copy.22.gates
  135.3 0.1 stack.36.spots
  135.4 0.0 all-to-all-done.3.hidden
  135.4 1.0 second.1
  136.4 5.8 %all-to-all-start.4 = ((bf16[8,32,128]{2,1,0:T(8,128)(2,1)}), bf16[8,32,128]{2,1,0:T(8,128)(2,1)S(1)}, u32[]{:S(2)}, u32[]{:S(2)}) async-start(bf16[8,32,128]{2,1,0:T(8,128)(2,1)} %second.1), calls=%async_computation.4 | async-start | bytes 131072 | tf_op jit(solution)/shard_map/all_to_all | solution.py:192
  142.2 0.0 collective-permute-done.7.refs_1_
  142.2 0.0 collective-permute-done.8.refs_3_
  142.2 0.0 collective-permute-done.9.refs_5_
  142.2 1.1 copy-done.2
  143.3 1.2 copy-done.8
  144.5 0.9 copy-done.12
  145.5 9.4 %attend_rest.1 = bf16[512,512]{1,0:T(8,128)(2,1)S(1)} custom-call(s32[7]{0:T(128)S(1)} %stack.36.spots, bf16[512,576]{1,0:T(8,128)(2,1)S(1)} %copy-done.2, s32[1,640]{1,0:T(1,128)S(1)} %add.93.base, bf16[576,640]{1,0:T(8,128)(2,1)S(1)} %get-tuple-element.21.refs_0_, bf16[576,640]{1,0:T(8,128)(2,1)} %collective-permute-done.7.refs_1_, ...), custom_call_target="tpu_custom_call" | custom-call | flops 72477573120 | bytes 87556096 | tf_op jit(solution)/shard_map/attend_rest/pallas_call | solution.py:35
  154.8 1.2 reshape.65
  156.0 0.0 all-to-all-done.4.back
  156.0 1.0 combine.1
  (17 shorter events, 0.0 us)
Async XLA Ops:
  0.6 0.9 copy-start
  2.5 15.3 %copy-start.3 = (bf16[2,80,1536]{2,1,0:T(8,128)(2,1)S(1)}, bf16[2,80,1536]{2,1,0:T(8,128)(2,1)}, u32[]{:S(2)}) copy-start(bf16[2,80,1536]{2,1,0:T(8,128)(2,1)} %gate.1) | copy-start | bytes 1474564
  2.5 15.3 %copy-start.4 = (bf16[2,80,1536]{2,1,0:T(8,128)(2,1)S(1)}, bf16[2,80,1536]{2,1,0:T(8,128)(2,1)}, u32[]{:S(2)}) copy-start(bf16[2,80,1536]{2,1,0:T(8,128)(2,1)} %up.1) | copy-start | bytes 1474564
  2.5 15.3 %copy-start.6 = (bf16[32,80]{1,0:T(8,128)(2,1)S(1)}, bf16[32,80]{1,0:T(8,128)(2,1)}, u32[]{:S(2)}) copy-start(bf16[32,80]{1,0:T(8,128)(2,1)} %tokens.1) | copy-start | bytes 15364
  2.5 36.8 %all-to-all-start = ((bf16[16,40,576]{2,1,0:T(8,128)(2,1)}), bf16[16,40,576]{2,1,0:T(8,128)(2,1)S(1)}, u32[]{:S(2)}, u32[]{:S(2)}) async-start(bf16[16,40,576]{2,1,0:T(8,128)(2,1)} %broadcast_in_dim.2), calls=%async_computation | async-start | bytes 1638400 | tf_op jit(solution)/shard_map/all_to_all | solution.py:192
  17.9 9.2 %collective-permute-start.3 = (bf16[192,768]{1,0:T(8,128)(2,1)S(1)}, bf16[192,768]{1,0:T(8,128)(2,1)S(1)}, u32[]{:S(2)}, u32[]{:S(2)}) collective-permute-start(bf16[192,768]{1,0:T(8,128)(2,1)S(1)} %get-tuple-element.16), channel_id=1, source_target_pairs={{0,8},{8,16},{16,24},{24,0},{1,9},{9,17},{17,25},{25,1},{2,10},{10... | collective-permute-start | bytes 884744 | tf_op jit(solution)/shard_map/ppermute | solution.py:197
  20.0 19.3 %copy-start.5 = (s32[32,6]{0,1:T(8,128)S(1)}, s32[32,6]{0,1:T(8,128)}, u32[]{:S(2)}) copy-start(s32[32,6]{0,1:T(8,128)} %param.13) | copy-start | bytes 2308
  20.0 10.4 %collective-permute-start.4 = (bf16[192,768]{1,0:T(8,128)(2,1)S(1)}, bf16[192,768]{1,0:T(8,128)(2,1)S(1)}, u32[]{:S(2)}, u32[]{:S(2)}) collective-permute-start(bf16[192,768]{1,0:T(8,128)(2,1)S(1)} %get-tuple-element.17), channel_id=1, source_target_pairs={{0,16},{8,24},{16,0},{24,8},{1,17},{9,25},{17,1},{25,9},{2,18},{10... | collective-permute-start | bytes 884744 | tf_op jit(solution)/shard_map/ppermute | solution.py:197
  24.1 13.8 %collective-permute-start.5 = (bf16[192,768]{1,0:T(8,128)(2,1)S(1)}, bf16[192,768]{1,0:T(8,128)(2,1)S(1)}, u32[]{:S(2)}, u32[]{:S(2)}) collective-permute-start(bf16[192,768]{1,0:T(8,128)(2,1)S(1)} %get-tuple-element.18), channel_id=1, source_target_pairs={{0,24},{8,0},{16,8},{24,16},{1,25},{9,1},{17,9},{25,17},{2,26},{10... | collective-permute-start | bytes 884744 | tf_op jit(solution)/shard_map/ppermute | solution.py:197
  61.4 25.6 %all-to-all-start.2 = ((bf16[16,16,768]{2,1,0:T(8,128)(2,1)}), bf16[16,16,768]{2,1,0:T(8,128)(2,1)S(1)}, u32[]{:S(2)}, u32[]{:S(2)}) async-start(bf16[16,16,768]{2,1,0:T(8,128)(2,1)} %bitcast.10), calls=%async_computation.2 | async-start | bytes 786432 | tf_op jit(solution)/shard_map/all_to_all | solution.py:192
  72.9 4.0 %copy-start.13 = (bf16[4,73728]{1,0:T(4,128)(2,1)S(1)}, bf16[4,73728]{1,0:T(4,128)(2,1)}, u32[]{:S(2)}) copy-start(bf16[4,73728]{1,0:T(4,128)(2,1)} %param.9) | copy-start | bytes 1769476
  73.3 29.5 %collective-permute-start.6 = (bf16[576,640]{1,0:T(8,128)(2,1)S(1)}, bf16[576,640]{1,0:T(8,128)(2,1)}, u32[]{:S(2)}, u32[]{:S(2)}) collective-permute-start(bf16[576,640]{1,0:T(8,128)(2,1)S(1)} %bitcast.15), channel_id=1, source_target_pairs={{0,1},{1,0},{2,3},{3,2},{4,5},{5,4},{6,7},{7,6},{8,9},{9,8},{10,11... | collective-permute-start | bytes 2211848 | tf_op jit(solution)/shard_map/ppermute | solution.py:197
  78.7 28.9 %collective-permute-start = (bf16[576,640]{1,0:T(8,128)(2,1)S(1)}, bf16[576,640]{1,0:T(8,128)(2,1)S(1)}, u32[]{:S(2)}, u32[]{:S(2)}) collective-permute-start(bf16[576,640]{1,0:T(8,128)(2,1)S(1)} %bitcast.16), channel_id=1, source_target_pairs={{0,8},{8,16},{16,24},{24,0},{1,9},{9,17},{17,25},{25,1},{2,10},{10... | collective-permute-start | bytes 2211848 | tf_op jit(solution)/shard_map/ppermute | solution.py:197
  80.8 26.8 %collective-permute-start.1 = (bf16[576,640]{1,0:T(8,128)(2,1)S(1)}, bf16[576,640]{1,0:T(8,128)(2,1)S(1)}, u32[]{:S(2)}, u32[]{:S(2)}) collective-permute-start(bf16[576,640]{1,0:T(8,128)(2,1)S(1)} %bitcast.17), channel_id=1, source_target_pairs={{0,24},{8,0},{16,8},{24,16},{1,25},{9,1},{17,9},{25,17},{2,26},{10... | collective-permute-start | bytes 2211848 | tf_op jit(solution)/shard_map/ppermute | solution.py:197
  84.0 41.9 %collective-permute-start.2 = (bf16[576,640]{1,0:T(8,128)(2,1)S(1)}, bf16[576,640]{1,0:T(8,128)(2,1)}, u32[]{:S(2)}, u32[]{:S(2)}) collective-permute-start(bf16[576,640]{1,0:T(8,128)(2,1)S(1)} %bitcast.18), channel_id=1, source_target_pairs={{0,16},{8,24},{16,0},{24,8},{1,17},{9,25},{17,1},{25,9},{2,18},{10... | collective-permute-start | bytes 2211848 | tf_op jit(solution)/shard_map/ppermute | solution.py:197
  88.0 47.3 %all-to-all-start.3 = ((bf16[64,16,384]{2,1,0:T(8,128)(2,1)}), bf16[64,16,384]{2,1,0:T(8,128)(2,1)S(1)}, u32[]{:S(2)}, u32[]{:S(2)}) async-start(bf16[64,16,384]{2,1,0:T(8,128)(2,1)} %get-tuple-element.27), calls=%async_computation.3 | async-start | bytes 1572864 | tf_op jit(solution)/shard_map/all_to_all | solution.py:192
  102.7 1.1 copy-start.1
  107.6 18.3 %copy-start.7 = (f32[512,512]{1,0:T(8,128)}, f32[512,512]{1,0:T(8,128)S(1)}, u32[]{:S(2)}) copy-start(f32[512,512]{1,0:T(8,128)S(1)} %get-tuple-element.26.refs_8_) | copy-start | bytes 3145732
  107.6 18.3 %copy-start.9 = (f32[512,128]{1,0:T(8,128)}, f32[512,128]{1,0:T(8,128)S(1)}, u32[]{:S(2)}) copy-start(f32[512,128]{1,0:T(8,128)S(1)} %get-tuple-element.24.refs_6_) | copy-start | bytes 786436
  107.6 18.3 %copy-start.11 = (f32[512,128]{1,0:T(8,128)}, f32[512,128]{1,0:T(8,128)S(1)}, u32[]{:S(2)}) copy-start(f32[512,128]{1,0:T(8,128)S(1)} %get-tuple-element.25.refs_7_) | copy-start | bytes 786436
  125.9 16.3 %collective-permute-start.7 = (bf16[576,640]{1,0:T(8,128)(2,1)S(1)}, bf16[576,640]{1,0:T(8,128)(2,1)}, u32[]{:S(2)}, u32[]{:S(2)}) collective-permute-start(bf16[576,640]{1,0:T(8,128)(2,1)S(1)} %get-tuple-element.21.refs_0_), channel_id=1, source_target_pairs={{0,1},{1,0},{2,3},{3,2},{4,5},{5,4},{6,7},{7,6},{8,9},{9,8},{10,11... | collective-permute-start | bytes 2211848 | tf_op jit(solution)/shard_map/ppermute | solution.py:197
  129.3 12.9 %collective-permute-start.8 = (bf16[576,640]{1,0:T(8,128)(2,1)S(1)}, bf16[576,640]{1,0:T(8,128)(2,1)}, u32[]{:S(2)}, u32[]{:S(2)}) collective-permute-start(bf16[576,640]{1,0:T(8,128)(2,1)S(1)} %get-tuple-element.22.refs_2_), channel_id=1, source_target_pairs={{0,1},{1,0},{2,3},{3,2},{4,5},{5,4},{6,7},{7,6},{8,9},{9,8},{10,11... | collective-permute-start | bytes 2211848 | tf_op jit(solution)/shard_map/ppermute | solution.py:197
  131.2 11.0 %collective-permute-start.9 = (bf16[576,640]{1,0:T(8,128)(2,1)}, bf16[576,640]{1,0:T(8,128)(2,1)}, u32[]{:S(2)}, u32[]{:S(2)}) collective-permute-start(bf16[576,640]{1,0:T(8,128)(2,1)} %get-tuple-element.23.refs_4_), channel_id=1, source_target_pairs={{0,1},{1,0},{2,3},{3,2},{4,5},{5,4},{6,7},{7,6},{8,9},{9,8},{10,11... | collective-permute-start | bytes 2211848 | tf_op jit(solution)/shard_map/ppermute | solution.py:197
  133.8 1.4 copy-start.14
  135.4 6.8 %copy-start.10 = (f32[512,128]{1,0:T(8,128)S(1)}, f32[512,128]{1,0:T(8,128)}, u32[]{:S(2)}) copy-start(f32[512,128]{1,0:T(8,128)} %copy-done.9) | copy-start | bytes 786436
  136.4 19.6 %all-to-all-start.4 = ((bf16[8,32,128]{2,1,0:T(8,128)(2,1)}), bf16[8,32,128]{2,1,0:T(8,128)(2,1)S(1)}, u32[]{:S(2)}, u32[]{:S(2)}) async-start(bf16[8,32,128]{2,1,0:T(8,128)(2,1)} %second.1), calls=%async_computation.4 | async-start | bytes 131072 | tf_op jit(solution)/shard_map/all_to_all | solution.py:192
  142.2 1.1 copy-start.2
  143.3 1.2 copy-start.8
  144.5 0.9 copy-start.12

commit v7 on v3

--- a/solution.py
+++ b/solution.py
@@ -16,6 +16,7 @@
 EXPERTS = 16
 CAP = 16
 LANES = 128
+CLAIM = 8
 
 SCALE_LOG2 = 192.0 ** (-0.5) * math.log2(math.e)
 F32 = jnp.float32
@@ -36,7 +37,7 @@
         out_shape=out_shape,
         in_specs=specs,
         out_specs=jax.tree.map(lambda _: VMEM, out_shape),
-        compiler_params=pltpu.CompilerParams(vmem_limit_bytes=24 * 2**20),
+        compiler_params=pltpu.CompilerParams(vmem_limit_bytes=(24 if special > 2**16 else 12) * 2**20),
         cost_estimate=pl.CostEstimate(flops=flops, bytes_accessed=moved, transcendentals=special),
         name=name,
     )(*args)
@@ -71,9 +72,10 @@
     if last:
         refs[-1][...] = (acc / den).astype(BF16)
     else:
-        refs[-3][...] = jnp.broadcast_to(new, (rows, LANES))
-        refs[-2][...] = jnp.broadcast_to(den, (rows, LANES))
-        refs[-1][...] = acc
+        refs[-4][...] = jnp.broadcast_to(new, (rows, LANES))
+        refs[-3][...] = jnp.broadcast_to(den, (rows, LANES))
+        refs[-2][...] = acc
+        refs[-1][...] = jnp.zeros(refs[-1].shape, F32)
 
 
 def attend(spots, queries, base, pieces, state, last, name):
@@ -81,11 +83,11 @@
     if last:
         out = shaped((rows, LAT), BF16)
     else:
-        out = [shaped((rows, LANES), F32)] * 2 + [shaped((rows, LAT), F32)]
+        out = [shaped((rows, LANES), F32)] * 2 + [shaped((rows, LAT), F32), shaped((8, LANES), F32)]
     body = functools.partial(attention_body, len(pieces), not state, last)
     specs = [SMEM] + [VMEM] * (2 + len(pieces) + len(state))
     args = (spots, queries, base, *pieces, *state)
-    return kernel(body, name, out, specs, args, 4 * rows * count * WIDE, 2 * count * WIDE + 2**20, rows * count)
+    return kernel(body, name, out, specs, args, 4 * rows * count * WIDE // CLAIM, (2 * count * WIDE + 2**20) // CLAIM, rows * count // CLAIM)
 
 
 def dispatch_body(copies, routes, tokens, out):
@@ -140,13 +142,15 @@
     rounded[...] = sums.astype(BF16)
 
 
-def hidden_body(total, other, out):
+def hidden_body(total, other, *refs):
+    out, token = refs[-2:]
     sums = total[...] + other[...].astype(F32)
     units = sums.shape[1] // 2
     gate = sums[:, :units]
     hidden = (gate / (1.0 + jnp.exp(-gate)) * sums[:, units:]).astype(BF16)
     for i in range(out.shape[0]):
         out[i] = hidden
+    token[...] = jnp.zeros(token.shape, F32)
 
 
 def second_body(deep, across, hidden, down, out):
@@ -180,15 +184,16 @@
     out[...] = mixed.astype(BF16)
 
 
-def hold(array, after):
+def hold(arrays, after):
     return pl.pallas_call(
-        lambda array, after, out: None,
-        out_shape=shaped(array.shape, array.dtype),
-        in_specs=[AFTER] * 2,
-        out_specs=AFTER,
-        input_output_aliases={0: 0},
+        lambda *refs: None,
+        out_shape=[shaped(a.shape, a.dtype) for a in arrays],
+        in_specs=[AFTER] * (len(arrays) + len(after)),
+        out_specs=[AFTER] * len(arrays),
+        input_output_aliases={i: i for i in range(len(arrays))},
+        compiler_params=pltpu.CompilerParams(vmem_limit_bytes=2**20),
         name="hold",
-    )(array, after)
+    )(*arrays, *after)
 
 
 def exchange(array, axes):
@@ -235,15 +240,17 @@
         functools.partial(first_body, order), "first", shaped((held * owners * CAP, 2 * units), BF16),
         [SMEM, AFTER] + [VMEM] * (1 + nx), (where_x, column, arrived, *weights), 2**28, 2**21,
     )
+    others = [shift(column, "x", 1), shift(column, "x", -1), shift(column, "x", 2)]
     parts = exchange(parts.reshape(nz, -1, 2 * units), "z")
     rows = parts.shape[1]
     total, rounded = kernel(
         add_body, "add", [shaped((rows, 2 * units), F32), shaped((rows, 2 * units), BF16)],
         [VMEM], (parts,), 2**18, 2**19,
     )
-    hidden = kernel(
-        hidden_body, "hidden", shaped((nz * nx, rows, units), BF16),
-        [VMEM] * 2, (total, shift(rounded, "h", 1)), 2**18, 2**20, 2**14,
+    added = shift(rounded, "h", 1)
+    hidden, token = kernel(
+        hidden_body, "hidden", [shaped((nz * nx, rows, units), BF16), shaped((8, LANES), F32)],
+        [VMEM] * 2 + [AFTER] * 2, (total, added, *others[:2]), 2**18, 2**20, 2**14,
     )
     hidden = exchange(hidden, ("z", "x"))
     result = kernel(
@@ -256,7 +263,6 @@
         [VMEM] * 3, (routes, gate_values, back), 2**20, 2**18,
     )
 
-    others = [shift(column, "x", 1), shift(column, "x", -1), shift(column, "x", 2)]
     sources = [x_at, x_at + nx - 1, x_at + 1, x_at + 2]
     at_z = lax.broadcasted_iota(I32, (nz, nh, own), 0)
     at_h = (lax.broadcasted_iota(I32, (nz, nh, own), 1) + h_at) % nh
@@ -273,9 +279,8 @@
         both = [p for piece in pieces for p in (piece, shift(piece, "c", 1))]
         return attend(marks, query_rows, base, both, state, last, name)
 
-    state = call([0], [column], [], False, "attend_own")
-    state = call([1, 2], others[:2], state, False, "attend_near")
-    mixed = call([3], [hold(others[2], state[0])], state, True, "attend_far")
+    *state, seen = call([0, 1, 2], [column, *hold(others[:2], [token])], [], False, "attend_near")
+    mixed = call([3], hold(others[2:], [token, seen]), state, True, "attend_far")
     attention_out = mixed.reshape(queries.shape[0], H * LAT)
     return (attention_out, moe_output)
 

time: 152 us -> 150 us (0.987)
  local copies, waits for them, and re-layouts: 11.7 us -> 9.18 us
    all_to_all x5, waiting for transfers between devices: 20.3 us -> 29.4 us  [exchange(): return lax.all_to_all(array, axes, split_axis=0, concat_axis=0, tiled=False)]
    ppermute x12, waiting for transfers between devices: 25.4 us -> 16.6 us  [shift(): lax.ppermute(array, axis, [(i, (i + by) % size) for i in range(size)])]
    unnamed x41 -> x23, local copies, waits for them, and re-layouts: 7.88 us -> 4.24 us
    pallas_call x11 -> x10, Pallas kernels: 20.9 us -> 20.7 us  [kernel(): pl.pallas_call(body, out_shape=out_shape, in_specs=specs, out_specs=jax.t...]
  transfers between devices with their start and end apart: 17 -> 17, of which waited for: 6 -> 7; matrix products, arithmetic and copies ran while one was open for 3% -> 4% of each run, Pallas kernels for 12% -> 10%
where the time goes in v7:
time: 150 us; the launch traced here: 149 us
  starting transfers between devices  70.9 us (47%)
  waiting for transfers between devices  46 us (31%)
  Pallas kernels  20.7 us (14%)
  local copies, waits for them, and re-layouts  9.18 us (6%)
  between operations  1.71 us (1%)
    ppermute x12, starting transfers between devices, shift(): lax.ppermute(array, axis, [(i, (i + by) % size) for i in range(size)])  39.3 us
    all_to_all x5, starting transfers between devices, exchange(): return lax.all_to_all(array, axes, split_axis=0, concat_axis=0, tiled=False)  31.6 us
    all_to_all x5, waiting for transfers between devices, exchange(): return lax.all_to_all(array, axes, split_axis=0, concat_axis=0, tiled=False)  29.4 us
    pallas_call x10, Pallas kernels, kernel(): pl.pallas_call(body, out_shape=out_shape, in_specs=specs, out_specs=jax.t...  20.7 us
    ppermute x12, waiting for transfers between devices, shift(): lax.ppermute(array, axis, [(i, (i + by) % size) for i in range(size)])  16.6 us
    unnamed x23, local copies, waits for them, and re-layouts  4.24 us
  transfers between devices with their start and end apart: 17, of which 7 were waited for; matrix products, arithmetic and copies ran while one was open for 4% of the time, Pallas kernels for 10%

profile of v7, /device:TPU:1, one launch (start us, length us, event | category | flops | bytes accessed | tf_op | source)
XLA Modules:
  0.0 148.7 jit_solution(1211607592174245019)
XLA Ops:
  0.6 0.0 copy-start
  0.6 0.0 copy-start.5
  0.7 0.7 copy-done.5
  1.4 0.7 copy-done.7
  2.1 1.0 dispatch.1
  3.1 10.4 %all-to-all-start = ((bf16[32,32,128]{2,1,0:T(8,128)(2,1)}), bf16[32,32,128]{2,1,0:T(8,128)(2,1)S(1)}, u32[]{:S(2)}, u32[]{:S(2)}) async-start(bf16[32,32,128]{2,1,0:T(8,128)(2,1)} %dispatch.1), calls=%async_computation | async-start | bytes 524288 | tf_op jit(solution)/shard_map/all_to_all | solution.py:200
  13.5 3.4 %collective-permute-start = (bf16[40,576]{1,0:T(8,128)(2,1)S(1)}, bf16[40,576]{1,0:T(8,128)(2,1)S(1)}, u32[]{:S(2)}, u32[]{:S(2)}) collective-permute-start(bf16[40,576]{1,0:T(8,128)(2,1)S(1)} %constant_dynamic-slice_fusion), channel_id=1, source_target_pairs={{0,32},{32,0},{1,33},{33,1},{2,34},{34,2},{3,35},{35,3},{4,36},{36... | collective-permute-start | bytes 138248 | tf_op jit(solution)/shard_map/ppermute | solution.py:205
  16.9 5.7 %collective-permute-done = bf16[40,576]{1,0:T(8,128)(2,1)S(1)} collective-permute-done((bf16[40,576]{1,0:T(8,128)(2,1)S(1)}, bf16[40,576]{1,0:T(8,128)(2,1)S(1)}, u32[]{:S(2)}, u32[]{:S(2)}) %collective-permute-start) | collective-permute-done | bytes 46112 | tf_op jit(solution)/shard_map/ppermute | solution.py:205
  22.6 4.5 %all-to-all-done.after.arrived = bf16[32,32,128]{2,1,0:T(8,128)(2,1)S(1)} async-done(((bf16[32,32,128]{2,1,0:T(8,128)(2,1)}), bf16[32,32,128]{2,1,0:T(8,128)(2,1)S(1)}, u32[]{:S(2)}, u32[]{:S(2)}) %all-to-all-start) | async-done | bytes 262176 | tf_op jit(solution)/shard_map/all_to_all | solution.py:200
  27.1 1.0 pair.1
  28.1 6.5 %all-to-all-start.1 = ((bf16[8,80,576]{2,1,0:T(8,128)(2,1)}), bf16[8,80,576]{2,1,0:T(8,128)(2,1)}, u32[]{:S(2)}, u32[]{:S(2)}) async-start(bf16[8,80,576]{2,1,0:T(8,128)(2,1)} %pair.1), calls=%async_computation.1 | async-start | bytes 1638400 | tf_op jit(solution)/shard_map/all_to_all | solution.py:200
  34.5 0.1 cut.1
  34.6 2.3 %collective-permute-start.2 = (bf16[2,80,768]{2,1,0:T(8,128)(2,1)S(1)}, bf16[2,80,768]{2,1,0:T(8,128)(2,1)S(1)}, u32[]{:S(2)}, u32[]{:S(2)}) collective-permute-start(bf16[2,80,768]{2,1,0:T(8,128)(2,1)S(1)} %get-tuple-element.17), channel_id=1, source_target_pairs={{0,8},{8,16},{16,24},{24,0},{1,9},{9,17},{17,25},{25,1},{2,10},{10... | collective-permute-start | bytes 737288 | tf_op jit(solution)/shard_map/ppermute | solution.py:205
  36.9 3.9 %collective-permute-start.3 = (bf16[2,80,768]{2,1,0:T(8,128)(2,1)S(1)}, bf16[2,80,768]{2,1,0:T(8,128)(2,1)S(1)}, u32[]{:S(2)}, u32[]{:S(2)}) collective-permute-start(bf16[2,80,768]{2,1,0:T(8,128)(2,1)S(1)} %get-tuple-element.18), channel_id=1, source_target_pairs={{0,16},{8,24},{16,0},{24,8},{1,17},{9,25},{17,1},{25,9},{2,18},{10... | collective-permute-start | bytes 737288 | tf_op jit(solution)/shard_map/ppermute | solution.py:205
  40.8 3.0 %collective-permute-start.4 = (bf16[2,80,768]{2,1,0:T(8,128)(2,1)S(1)}, bf16[2,80,768]{2,1,0:T(8,128)(2,1)S(1)}, u32[]{:S(2)}, u32[]{:S(2)}) collective-permute-start(bf16[2,80,768]{2,1,0:T(8,128)(2,1)S(1)} %get-tuple-element.19), channel_id=1, source_target_pairs={{0,24},{8,0},{16,8},{24,16},{1,25},{9,1},{17,9},{25,17},{2,26},{10... | collective-permute-start | bytes 737288 | tf_op jit(solution)/shard_map/ppermute | solution.py:205
  43.8 15.2 %all-to-all-done.1 = bf16[8,80,576]{2,1,0:T(8,128)(2,1)} async-done(((bf16[8,80,576]{2,1,0:T(8,128)(2,1)}), bf16[8,80,576]{2,1,0:T(8,128)(2,1)}, u32[]{:S(2)}, u32[]{:S(2)}) %all-to-all-start.1) | async-done | bytes 737312 | tf_op jit(solution)/shard_map/all_to_all | solution.py:200
  59.0 1.5 %copy.18 = bf16[640,576]{0,1:T(8,128)(2,1)S(1)} copy(bf16[640,576]{1,0:T(8,128)(2,1)} %bitcast.3) | data formatting | bytes 1474560 | tf_op jit(solution)/shard_map/reshape | solution.py:231
  60.5 0.0 collective-permute-done.2.refs_1_
  60.5 0.0 collective-permute-done.3.refs_2_
  60.5 0.0 collective-permute-done.4.refs_3_
  60.5 1.3 first.1
  61.8 3.5 %all-to-all-start.2 = ((bf16[8,32,768]{2,1,0:T(8,128)(2,1)}), bf16[8,32,768]{2,1,0:T(8,128)(2,1)S(1)}, u32[]{:S(2)}, u32[]{:S(2)}) async-start(bf16[8,32,768]{2,1,0:T(8,128)(2,1)} %bitcast.6), calls=%async_computation.2 | async-start | bytes 786432 | tf_op jit(solution)/shard_map/all_to_all | solution.py:200
  65.3 3.0 %collective-permute-start.7 = (bf16[576,640]{1,0:T(8,128)(2,1)S(1)}, bf16[576,640]{1,0:T(8,128)(2,1)S(1)}, u32[]{:S(2)}, u32[]{:S(2)}) collective-permute-start(bf16[576,640]{1,0:T(8,128)(2,1)S(1)} %bitcast.14), channel_id=1, source_target_pairs={{0,24},{8,0},{16,8},{24,16},{1,25},{9,1},{17,9},{25,17},{2,26},{10... | collective-permute-start | bytes 2211848 | tf_op jit(solution)/shard_map/ppermute | solution.py:205
  68.3 2.3 %collective-permute-start.6 = (bf16[576,640]{1,0:T(8,128)(2,1)S(1)}, bf16[576,640]{1,0:T(8,128)(2,1)S(1)}, u32[]{:S(2)}, u32[]{:S(2)}) collective-permute-start(bf16[576,640]{1,0:T(8,128)(2,1)S(1)} %bitcast.15), channel_id=1, source_target_pairs={{0,8},{8,16},{16,24},{24,0},{1,9},{9,17},{17,25},{25,1},{2,10},{10... | collective-permute-start | bytes 2211848 | tf_op jit(solution)/shard_map/ppermute | solution.py:205
  70.6 9.8 %all-to-all-done.2.parts = bf16[8,32,768]{2,1,0:T(8,128)(2,1)S(1)} async-done(((bf16[8,32,768]{2,1,0:T(8,128)(2,1)}), bf16[8,32,768]{2,1,0:T(8,128)(2,1)S(1)}, u32[]{:S(2)}, u32[]{:S(2)}) %all-to-all-start.2) | async-done | bytes 393248 | tf_op jit(solution)/shard_map/all_to_all | solution.py:200
  80.3 0.1 add.126
  80.4 5.5 %collective-permute-start.5 = (bf16[32,768]{1,0:T(8,128)(2,1)S(1)}, bf16[32,768]{1,0:T(8,128)(2,1)S(1)}, u32[]{:S(2)}, u32[]{:S(2)}) collective-permute-start(bf16[32,768]{1,0:T(8,128)(2,1)S(1)} %get-tuple-element.21), channel_id=1, source_target_pairs={{0,32},{32,0},{1,33},{33,1},{2,34},{34,2},{3,35},{35,3},{4,36},{36... | collective-permute-start | bytes 147464 | tf_op jit(solution)/shard_map/ppermute | solution.py:205
  85.9 0.0 collective-permute-done.7.refs_1_
  85.9 2.7 %collective-permute-done.6.refs_0_ = bf16[576,640]{1,0:T(8,128)(2,1)S(1)} collective-permute-done((bf16[576,640]{1,0:T(8,128)(2,1)S(1)}, bf16[576,640]{1,0:T(8,128)(2,1)S(1)}, u32[]{:S(2)}, u32[]{:S(2)}) %collective-permute-start.6) | collective-permute-done | bytes 737312 | tf_op jit(solution)/shard_map/ppermute | solution.py:205
  88.6 0.6 collective-permute-done.5.other
  89.2 1.0 hidden.1
  90.2 6.2 %all-to-all-start.3 = ((bf16[32,32,384]{2,1,0:T(8,128)(2,1)}), bf16[32,32,384]{2,1,0:T(8,128)(2,1)}, u32[]{:S(2)}, u32[]{:S(2)}) async-start(bf16[32,32,384]{2,1,0:T(8,128)(2,1)} %get-tuple-element.29), calls=%async_computation.3 | async-start | bytes 1572864 | tf_op jit(solution)/shard_map/all_to_all | solution.py:200
  96.4 4.2 %collective-permute-start.8 = (bf16[576,640]{1,0:T(8,128)(2,1)S(1)}, bf16[576,640]{1,0:T(8,128)(2,1)}, u32[]{:S(2)}, u32[]{:S(2)}) collective-permute-start(bf16[576,640]{1,0:T(8,128)(2,1)S(1)} %bitcast.16), channel_id=1, source_target_pairs={{0,1},{1,0},{2,3},{3,2},{4,5},{5,4},{6,7},{7,6},{8,9},{9,8},{10,11... | collective-permute-start | bytes 2211848 | tf_op jit(solution)/shard_map/ppermute | solution.py:205
  100.6 1.9 %collective-permute-start.9 = (bf16[576,640]{1,0:T(8,128)(2,1)S(1)}, bf16[576,640]{1,0:T(8,128)(2,1)}, u32[]{:S(2)}, u32[]{:S(2)}) collective-permute-start(bf16[576,640]{1,0:T(8,128)(2,1)S(1)} %get-tuple-element.23.refs_2_), channel_id=1, source_target_pairs={{0,1},{1,0},{2,3},{3,2},{4,5},{5,4},{6,7},{7,6},{8,9},{9,8},{10,11... | collective-permute-start | bytes 2211848 | tf_op jit(solution)/shard_map/ppermute | solution.py:205
  102.5 2.4 %collective-permute-start.10 = (bf16[576,640]{1,0:T(8,128)(2,1)S(1)}, bf16[576,640]{1,0:T(8,128)(2,1)}, u32[]{:S(2)}, u32[]{:S(2)}) collective-permute-start(bf16[576,640]{1,0:T(8,128)(2,1)S(1)} %get-tuple-element.24.refs_4_), channel_id=1, source_target_pairs={{0,1},{1,0},{2,3},{3,2},{4,5},{5,4},{6,7},{7,6},{8,9},{9,8},{10,11... | collective-permute-start | bytes 2211848 | tf_op jit(solution)/shard_map/ppermute | solution.py:205
  104.9 4.9 %collective-permute-start.1 = (bf16[576,640]{1,0:T(8,128)(2,1)S(1)}, bf16[576,640]{1,0:T(8,128)(2,1)}, u32[]{:S(2)}, u32[]{:S(2)}) collective-permute-start(bf16[576,640]{1,0:T(8,128)(2,1)S(1)} %bitcast.17), channel_id=1, source_target_pairs={{0,16},{8,24},{16,0},{24,8},{1,17},{9,25},{17,1},{25,9},{2,18},{10... | collective-permute-start | bytes 2211848 | tf_op jit(solution)/shard_map/ppermute | solution.py:205
  110.5 0.1 iota.26
  110.5 0.1 iota.27
  110.7 0.1 iota.29
  110.7 0.1 iota.30
  110.8 0.1 iota.32
  110.9 1.7 %reshape.101.queries = bf16[512,576]{1,0:T(8,128)(2,1)S(1)} reshape(bf16[4,73728]{1,0:T(4,128)(2,1)} %param.9) | data formatting | bytes 1179648 | tf_op jit(solution)/shard_map/reshape | solution.py:270
  112.7 0.1 stack.39.spots
  112.8 0.0 collective-permute-done.8.refs_1_
  112.8 0.0 collective-permute-done.9.refs_3_
  112.8 0.0 collective-permute-done.10.refs_5_
  112.8 9.1 %attend_near.1 = (f32[512,128]{1,0:T(8,128)S(1)}, f32[512,128]{1,0:T(8,128)S(1)}, f32[512,512]{1,0:T(8,128)S(1)}, f32[8,128]{1,0:T(8,128)S(1)}) custom-call(s32[7]{0:T(128)S(1)} %stack.39.spots, bf16[512,576]{1,0:T(8,128)(2,1)S(1)} %reshape.101.queries, s32[1,640]{1,0:T(1,128)S(1)} %multiply_add_fusion.base, bf16[576,640]{1,0:T(8,128)(2,1)S(1)} %bitcast.18, ...), custom_call_target="tpu_custom_call" | custom-call | flops 566231040 | bytes 684032 | tf_op jit(solution)/shard_map/attend_near/pallas_call | solution.py:35
  121.9 1.0 copy-done.1
  122.9 7.6 %collective-permute-done.1.refs_0_ = bf16[576,640]{1,0:T(8,128)(2,1)} collective-permute-done((bf16[576,640]{1,0:T(8,128)(2,1)S(1)}, bf16[576,640]{1,0:T(8,128)(2,1)}, u32[]{:S(2)}, u32[]{:S(2)}) %collective-permute-start.1) | collective-permute-done | bytes 737312 | tf_op jit(solution)/shard_map/ppermute | solution.py:205
  130.5 2.7 %collective-permute-start.11 = (bf16[576,640]{1,0:T(8,128)(2,1)}, bf16[576,640]{1,0:T(8,128)(2,1)}, u32[]{:S(2)}, u32[]{:S(2)}) collective-permute-start(bf16[576,640]{1,0:T(8,128)(2,1)} %hold.3.refs_0_), channel_id=1, source_target_pairs={{0,1},{1,0},{2,3},{3,2},{4,5},{5,4},{6,7},{7,6},{8,9},{9,8},{10,11... | collective-permute-start | bytes 2211848 | tf_op jit(solution)/shard_map/ppermute | solution.py:205
  133.2 0.0 copy-start.6
  133.2 0.7 copy-done.6
  133.9 0.1 copy.20.routes
  133.9 0.6 copy-done.9
  134.5 0.1 copy.21.gates
  134.6 0.4 copy.19.down
  135.1 0.0 all-to-all-done.3.hidden
  135.1 2.2 %second.1 = bf16[8,32,128]{2,1,0:T(8,128)(2,1)} custom-call(bf16[32,32,384]{2,1,0:T(8,128)(2,1)} %all-to-all-done.3.hidden, bf16[2,1536,80]{2,1,0:T(8,128)(2,1)S(1)} %copy.19.down), custom_call_target="tpu_custom_call" | custom-call | flops 134217728 | bytes 2097152 | tf_op jit(solution)/shard_map/second/pallas_call | solution.py:35
  137.3 5.1 %all-to-all-start.4 = ((bf16[8,32,128]{2,1,0:T(8,128)(2,1)}), bf16[8,32,128]{2,1,0:T(8,128)(2,1)S(1)}, u32[]{:S(2)}, u32[]{:S(2)}) async-start(bf16[8,32,128]{2,1,0:T(8,128)(2,1)} %second.1), calls=%async_computation.4 | async-start | bytes 131072 | tf_op jit(solution)/shard_map/all_to_all | solution.py:200
  142.4 0.1 pad_add_fusion.spots
  142.5 0.0 collective-permute-done.11.refs_1_
  142.5 4.0 %attend_far.1 = bf16[512,512]{1,0:T(8,128)(2,1)S(1)} custom-call(s32[3]{0:T(128)S(1)} %pad_add_fusion.spots, bf16[512,576]{1,0:T(8,128)(2,1)S(1)} %reshape.101.queries, s32[1,640]{1,0:T(1,128)S(1)} %multiply_add_fusion.base, bf16[576,640]{1,0:T(8,128)(2,1)} %hold.3.refs_0_, bf16[576,640]{1,0:T(8,128)(2,1)} %collective-permute-done.11.refs_1_, ...), custom_call_target="tpu_custom_call" | custom-call | flops 188743680 | bytes 315392 | tf_op jit(solution)/shard_map/attend_far/pallas_call | solution.py:35
  146.5 1.2 reshape.105
  147.7 1.0 combine.1
  (21 shorter events, 0.1 us)
Async XLA Ops:
  0.6 12.9 %copy-start = (bf16[80,576]{1,0:T(8,128)(2,1)S(1)}, bf16[80,576]{1,0:T(8,128)(2,1)}, u32[]{:S(2)}) copy-start(bf16[80,576]{1,0:T(8,128)(2,1)} %param.10) | copy-start | bytes 276484
  0.6 0.7 copy-start.5
  1.4 0.7 copy-start.7
  3.1 24.0 %all-to-all-start = ((bf16[32,32,128]{2,1,0:T(8,128)(2,1)}), bf16[32,32,128]{2,1,0:T(8,128)(2,1)S(1)}, u32[]{:S(2)}, u32[]{:S(2)}) async-start(bf16[32,32,128]{2,1,0:T(8,128)(2,1)} %dispatch.1), calls=%async_computation | async-start | bytes 524288 | tf_op jit(solution)/shard_map/all_to_all | solution.py:200
  13.5 9.1 %collective-permute-start = (bf16[40,576]{1,0:T(8,128)(2,1)S(1)}, bf16[40,576]{1,0:T(8,128)(2,1)S(1)}, u32[]{:S(2)}, u32[]{:S(2)}) collective-permute-start(bf16[40,576]{1,0:T(8,128)(2,1)S(1)} %constant_dynamic-slice_fusion), channel_id=1, source_target_pairs={{0,32},{32,0},{1,33},{33,1},{2,34},{34,2},{3,35},{35,3},{4,36},{36... | collective-permute-start | bytes 138248 | tf_op jit(solution)/shard_map/ppermute | solution.py:205
  28.1 6.5 %copy-start.3 = (bf16[2,80,1536]{2,1,0:T(8,128)(2,1)S(1)}, bf16[2,80,1536]{2,1,0:T(8,128)(2,1)}, u32[]{:S(2)}) copy-start(bf16[2,80,1536]{2,1,0:T(8,128)(2,1)} %gate.1) | copy-start | bytes 1474564
  28.1 6.5 %copy-start.4 = (bf16[2,80,1536]{2,1,0:T(8,128)(2,1)S(1)}, bf16[2,80,1536]{2,1,0:T(8,128)(2,1)}, u32[]{:S(2)}) copy-start(bf16[2,80,1536]{2,1,0:T(8,128)(2,1)} %up.1) | copy-start | bytes 1474564
  28.1 30.9 %all-to-all-start.1 = ((bf16[8,80,576]{2,1,0:T(8,128)(2,1)}), bf16[8,80,576]{2,1,0:T(8,128)(2,1)}, u32[]{:S(2)}, u32[]{:S(2)}) async-start(bf16[8,80,576]{2,1,0:T(8,128)(2,1)} %pair.1), calls=%async_computation.1 | async-start | bytes 1638400 | tf_op jit(solution)/shard_map/all_to_all | solution.py:200
  34.6 25.8 %collective-permute-start.2 = (bf16[2,80,768]{2,1,0:T(8,128)(2,1)S(1)}, bf16[2,80,768]{2,1,0:T(8,128)(2,1)S(1)}, u32[]{:S(2)}, u32[]{:S(2)}) collective-permute-start(bf16[2,80,768]{2,1,0:T(8,128)(2,1)S(1)} %get-tuple-element.17), channel_id=1, source_target_pairs={{0,8},{8,16},{16,24},{24,0},{1,9},{9,17},{17,25},{25,1},{2,10},{10... | collective-permute-start | bytes 737288 | tf_op jit(solution)/shard_map/ppermute | solution.py:205
  36.9 23.6 %collective-permute-start.3 = (bf16[2,80,768]{2,1,0:T(8,128)(2,1)S(1)}, bf16[2,80,768]{2,1,0:T(8,128)(2,1)S(1)}, u32[]{:S(2)}, u32[]{:S(2)}) collective-permute-start(bf16[2,80,768]{2,1,0:T(8,128)(2,1)S(1)} %get-tuple-element.18), channel_id=1, source_target_pairs={{0,16},{8,24},{16,0},{24,8},{1,17},{9,25},{17,1},{25,9},{2,18},{10... | collective-permute-start | bytes 737288 | tf_op jit(solution)/shard_map/ppermute | solution.py:205
  40.8 19.7 %collective-permute-start.4 = (bf16[2,80,768]{2,1,0:T(8,128)(2,1)S(1)}, bf16[2,80,768]{2,1,0:T(8,128)(2,1)S(1)}, u32[]{:S(2)}, u32[]{:S(2)}) collective-permute-start(bf16[2,80,768]{2,1,0:T(8,128)(2,1)S(1)} %get-tuple-element.19), channel_id=1, source_target_pairs={{0,24},{8,0},{16,8},{24,16},{1,25},{9,1},{17,9},{25,17},{2,26},{10... | collective-permute-start | bytes 737288 | tf_op jit(solution)/shard_map/ppermute | solution.py:205
  61.8 18.5 %all-to-all-start.2 = ((bf16[8,32,768]{2,1,0:T(8,128)(2,1)}), bf16[8,32,768]{2,1,0:T(8,128)(2,1)S(1)}, u32[]{:S(2)}, u32[]{:S(2)}) async-start(bf16[8,32,768]{2,1,0:T(8,128)(2,1)} %bitcast.6), calls=%async_computation.2 | async-start | bytes 786432 | tf_op jit(solution)/shard_map/all_to_all | solution.py:200
  65.3 20.7 %collective-permute-start.7 = (bf16[576,640]{1,0:T(8,128)(2,1)S(1)}, bf16[576,640]{1,0:T(8,128)(2,1)S(1)}, u32[]{:S(2)}, u32[]{:S(2)}) collective-permute-start(bf16[576,640]{1,0:T(8,128)(2,1)S(1)} %bitcast.14), channel_id=1, source_target_pairs={{0,24},{8,0},{16,8},{24,16},{1,25},{9,1},{17,9},{25,17},{2,26},{10... | collective-permute-start | bytes 2211848 | tf_op jit(solution)/shard_map/ppermute | solution.py:205
  68.3 20.3 %collective-permute-start.6 = (bf16[576,640]{1,0:T(8,128)(2,1)S(1)}, bf16[576,640]{1,0:T(8,128)(2,1)S(1)}, u32[]{:S(2)}, u32[]{:S(2)}) collective-permute-start(bf16[576,640]{1,0:T(8,128)(2,1)S(1)} %bitcast.15), channel_id=1, source_target_pairs={{0,8},{8,16},{16,24},{24,0},{1,9},{9,17},{17,25},{25,1},{2,10},{10... | collective-permute-start | bytes 2211848 | tf_op jit(solution)/shard_map/ppermute | solution.py:205
  80.4 8.8 %collective-permute-start.5 = (bf16[32,768]{1,0:T(8,128)(2,1)S(1)}, bf16[32,768]{1,0:T(8,128)(2,1)S(1)}, u32[]{:S(2)}, u32[]{:S(2)}) collective-permute-start(bf16[32,768]{1,0:T(8,128)(2,1)S(1)} %get-tuple-element.21), channel_id=1, source_target_pairs={{0,32},{32,0},{1,33},{33,1},{2,34},{34,2},{3,35},{35,3},{4,36},{36... | collective-permute-start | bytes 147464 | tf_op jit(solution)/shard_map/ppermute | solution.py:205
  90.2 44.8 %all-to-all-start.3 = ((bf16[32,32,384]{2,1,0:T(8,128)(2,1)}), bf16[32,32,384]{2,1,0:T(8,128)(2,1)}, u32[]{:S(2)}, u32[]{:S(2)}) async-start(bf16[32,32,384]{2,1,0:T(8,128)(2,1)} %get-tuple-element.29), calls=%async_computation.3 | async-start | bytes 1572864 | tf_op jit(solution)/shard_map/all_to_all | solution.py:200
  96.4 16.4 %collective-permute-start.8 = (bf16[576,640]{1,0:T(8,128)(2,1)S(1)}, bf16[576,640]{1,0:T(8,128)(2,1)}, u32[]{:S(2)}, u32[]{:S(2)}) collective-permute-start(bf16[576,640]{1,0:T(8,128)(2,1)S(1)} %bitcast.16), channel_id=1, source_target_pairs={{0,1},{1,0},{2,3},{3,2},{4,5},{5,4},{6,7},{7,6},{8,9},{9,8},{10,11... | collective-permute-start | bytes 2211848 | tf_op jit(solution)/shard_map/ppermute | solution.py:205
  100.6 12.2 %collective-permute-start.9 = (bf16[576,640]{1,0:T(8,128)(2,1)S(1)}, bf16[576,640]{1,0:T(8,128)(2,1)}, u32[]{:S(2)}, u32[]{:S(2)}) collective-permute-start(bf16[576,640]{1,0:T(8,128)(2,1)S(1)} %get-tuple-element.23.refs_2_), channel_id=1, source_target_pairs={{0,1},{1,0},{2,3},{3,2},{4,5},{5,4},{6,7},{7,6},{8,9},{9,8},{10,11... | collective-permute-start | bytes 2211848 | tf_op jit(solution)/shard_map/ppermute | solution.py:205
  102.5 10.3 %collective-permute-start.10 = (bf16[576,640]{1,0:T(8,128)(2,1)S(1)}, bf16[576,640]{1,0:T(8,128)(2,1)}, u32[]{:S(2)}, u32[]{:S(2)}) collective-permute-start(bf16[576,640]{1,0:T(8,128)(2,1)S(1)} %get-tuple-element.24.refs_4_), channel_id=1, source_target_pairs={{0,1},{1,0},{2,3},{3,2},{4,5},{5,4},{6,7},{7,6},{8,9},{9,8},{10,11... | collective-permute-start | bytes 2211848 | tf_op jit(solution)/shard_map/ppermute | solution.py:205
  104.9 25.6 %collective-permute-start.1 = (bf16[576,640]{1,0:T(8,128)(2,1)S(1)}, bf16[576,640]{1,0:T(8,128)(2,1)}, u32[]{:S(2)}, u32[]{:S(2)}) collective-permute-start(bf16[576,640]{1,0:T(8,128)(2,1)S(1)} %bitcast.17), channel_id=1, source_target_pairs={{0,16},{8,24},{16,0},{24,8},{1,17},{9,25},{17,1},{25,9},{2,18},{10... | collective-permute-start | bytes 2211848 | tf_op jit(solution)/shard_map/ppermute | solution.py:205
  121.9 1.0 copy-start.1
  130.5 4.2 %copy-start.8 = (bf16[2,1536,80]{1,2,0:T(8,128)(2,1)S(1)}, bf16[2,1536,80]{1,2,0:T(8,128)(2,1)}, u32[]{:S(2)}) copy-start(bf16[2,1536,80]{1,2,0:T(8,128)(2,1)} %param.17) | copy-start | bytes 1474564
  130.5 12.0 %collective-permute-start.11 = (bf16[576,640]{1,0:T(8,128)(2,1)}, bf16[576,640]{1,0:T(8,128)(2,1)}, u32[]{:S(2)}, u32[]{:S(2)}) collective-permute-start(bf16[576,640]{1,0:T(8,128)(2,1)} %hold.3.refs_0_), channel_id=1, source_target_pairs={{0,1},{1,0},{2,3},{3,2},{4,5},{5,4},{6,7},{7,6},{8,9},{9,8},{10,11... | collective-permute-start | bytes 2211848 | tf_op jit(solution)/shard_map/ppermute | solution.py:205
  133.2 0.7 copy-start.6
  133.9 0.7 copy-start.9
  135.0 7.4 %copy-start.2 = (f32[512,512]{1,0:T(8,128)S(1)}, f32[512,512]{1,0:T(8,128)}, u32[]{:S(2)}) copy-start(f32[512,512]{1,0:T(8,128)} %copy-done.1) | copy-start | bytes 3145732
  137.3 10.4 %all-to-all-start.4 = ((bf16[8,32,128]{2,1,0:T(8,128)(2,1)}), bf16[8,32,128]{2,1,0:T(8,128)(2,1)S(1)}, u32[]{:S(2)}, u32[]{:S(2)}) async-start(bf16[8,32,128]{2,1,0:T(8,128)(2,1)} %second.1), calls=%async_computation.4 | async-start | bytes 131072 | tf_op jit(solution)/shard_map/all_to_all | solution.py:200

commit v8 on v7

--- a/solution.py
+++ b/solution.py
@@ -121,8 +121,8 @@
         out[i] = rows[...]
 
 
-def first_body(order, spots, after, arrived, *refs):
-    weights, out = refs[:-1], refs[-1]
+def first_body(order, spots, arrived, *refs):
+    weights, out = refs[: len(order)], refs[-1]
     held, feats = weights[0].shape[:2]
     owners = arrived.shape[0] // len(weights)
     for e in range(held):
@@ -153,7 +153,8 @@
     token[...] = jnp.zeros(token.shape, F32)
 
 
-def second_body(deep, across, hidden, down, out):
+def second_body(deep, across, hidden, down, *refs):
+    out = refs[-1]
     held, feats = down.shape[0], down.shape[2]
     units = hidden.shape[2]
     group = deep // held
@@ -228,7 +229,7 @@
         pair_body, "pair", shaped((nz,) + paired.shape, BF16), [VMEM, AFTER], (paired, arrived), 2**10, 2**20
     )
     column = exchange(paired, "z")
-    column = column.reshape(nz * nh * own, WIDE).T
+    raw = column.reshape(nz * nh * own, WIDE)
 
     cut = kernel(
         cut_body, "cut", [shaped((held, feats, 2 * units), BF16)] * nx,
@@ -236,10 +237,17 @@
     )
     weights = [cut[0]] + [shift(cut[j], "x", j) for j in range(1, nx)]
     order = [0] + [nx - j for j in range(1, nx)]
+    at_z = lax.broadcasted_iota(I32, (nz, nh, own), 0)
+    at_h = (lax.broadcasted_iota(I32, (nz, nh, own), 1) + h_at) % nh
+    base = ((at_z * nh + at_h) * nx * latents.shape[0] + lax.broadcasted_iota(I32, (nz, nh, own), 2)).reshape(1, -1)
+    query_rows = queries.reshape(queries.shape[0] * H, WIDE)
+
     parts = kernel(
         functools.partial(first_body, order), "first", shaped((held * owners * CAP, 2 * units), BF16),
-        [SMEM, AFTER] + [VMEM] * (1 + nx), (where_x, column, arrived, *weights), 2**28, 2**21,
-    )
+        [SMEM] + [VMEM] * (1 + nx) + [AFTER] * 3, (where_x, arrived, *weights, raw, query_rows, base), 2**28, 2**21,
+    )
+    column = raw.T
+    swapped = shift(column, "c", 1)
     others = [shift(column, "x", 1), shift(column, "x", -1), shift(column, "x", 2)]
     parts = exchange(parts.reshape(nz, -1, 2 * units), "z")
     rows = parts.shape[1]
@@ -250,12 +258,27 @@
     added = shift(rounded, "h", 1)
     hidden, token = kernel(
         hidden_body, "hidden", [shaped((nz * nx, rows, units), BF16), shaped((8, LANES), F32)],
-        [VMEM] * 2 + [AFTER] * 2, (total, added, *others[:2]), 2**18, 2**20, 2**14,
+        [VMEM] * 2 + [AFTER] * 3, (total, added, *others[:2], swapped), 2**18, 2**20, 2**14,
     )
     hidden = exchange(hidden, ("z", "x"))
+    sources = [x_at, x_at + nx - 1, x_at + 1, x_at + 2]
+    spots = []
+    for source in sources:
+        first = (source % nx) * latents.shape[0]
+        spots.append([first + core * own, first + (nc - 1 - core) * own])
+
+    def call(which, pieces, state, last, name):
+        marks = jnp.stack([offsets[0]] + [s for i in which for s in spots[i]]).astype(I32)
+        both = [p for piece in pieces for p in (piece, swapped if piece is column else shift(piece, "c", 1))]
+        return attend(marks, query_rows, base, both, state, last, name)
+
+    near, far = hold(others[:2], [token])
+    *state, seen = call([0, 1, 2], [column, near, far], [], False, "attend_near")
+    (opposite,) = hold(others[2:], [seen])
+    mixed = call([3], [opposite], state, True, "attend_far")
     result = kernel(
         functools.partial(second_body, nz, nx), "second", shaped((owners, slots, LANES), BF16),
-        [VMEM] * 2, (hidden, w_down), 2**27, 2**21,
+        [VMEM] * 2 + [AFTER], (hidden, w_down, seen), 2**27, 2**21,
     )
     back = exchange(result, ("l", "c"))
     moe_output = kernel(
@@ -263,24 +286,6 @@
         [VMEM] * 3, (routes, gate_values, back), 2**20, 2**18,
     )
 
-    sources = [x_at, x_at + nx - 1, x_at + 1, x_at + 2]
-    at_z = lax.broadcasted_iota(I32, (nz, nh, own), 0)
-    at_h = (lax.broadcasted_iota(I32, (nz, nh, own), 1) + h_at) % nh
-    base = ((at_z * nh + at_h) * nx * latents.shape[0] + lax.broadcasted_iota(I32, (nz, nh, own), 2)).reshape(1, -1)
-    query_rows = queries.reshape(queries.shape[0] * H, WIDE)
-
-    spots = []
-    for source in sources:
-        first = (source % nx) * latents.shape[0]
-        spots.append([first + core * own, first + (nc - 1 - core) * own])
-
-    def call(which, pieces, state, last, name):
-        marks = jnp.stack([offsets[0]] + [s for i in which for s in spots[i]]).astype(I32)
-        both = [p for piece in pieces for p in (piece, shift(piece, "c", 1))]
-        return attend(marks, query_rows, base, both, state, last, name)
-
-    *state, seen = call([0, 1, 2], [column, *hold(others[:2], [token])], [], False, "attend_near")
-    mixed = call([3], hold(others[2:], [token, seen]), state, True, "attend_far")
     attention_out = mixed.reshape(queries.shape[0], H * LAT)
     return (attention_out, moe_output)
 

time: 150 us -> 153 us (1.020)
  starting transfers between devices: 70.9 us -> 74.7 us
  local copies, waits for them, and re-layouts: 9.18 us -> 12.8 us
  waiting for transfers between devices: 46 us -> 43 us
  Pallas kernels: 20.7 us -> 19.1 us
    all_to_all x5, waiting for transfers between devices: 29.4 us -> 22.8 us  [exchange(): return lax.all_to_all(array, axes, split_axis=0, concat_axis=0, tiled=False)]
    unnamed x23 -> x31, local copies, waits for them, and re-layouts: 4.24 us -> 8.18 us
    ppermute x12, waiting for transfers between devices: 16.6 us -> 20.2 us  [shift(): lax.ppermute(array, axis, [(i, (i + by) % size) for i in range(size)])]
    all_to_all x5, starting transfers between devices: 31.6 us -> 34.6 us  [exchange(): return lax.all_to_all(array, axes, split_axis=0, concat_axis=0, tiled=False)]
    pallas_call x10, Pallas kernels: 20.7 us -> 19.1 us  [kernel(): pl.pallas_call(body, out_shape=out_shape, in_specs=specs, out_specs=jax.t...]
where the time goes in v8:
time: 153 us; the launch traced here: 151 us
  starting transfers between devices  74.7 us (49%)
  waiting for transfers between devices  43 us (28%)
  Pallas kernels  19.1 us (12%)
  local copies, waits for them, and re-layouts  12.8 us (8%)
  between operations  1.67 us (1%)
    ppermute x12, starting transfers between devices, shift(): lax.ppermute(array, axis, [(i, (i + by) % size) for i in range(size)])  40.1 us
    all_to_all x5, starting transfers between devices, exchange(): return lax.all_to_all(array, axes, split_axis=0, concat_axis=0, tiled=False)  34.6 us
    all_to_all x5, waiting for transfers between devices, exchange(): return lax.all_to_all(array, axes, split_axis=0, concat_axis=0, tiled=False)  22.8 us
    ppermute x12, waiting for transfers between devices, shift(): lax.ppermute(array, axis, [(i, (i + by) % size) for i in range(size)])  20.2 us
    pallas_call x10, Pallas kernels, kernel(): pl.pallas_call(body, out_shape=out_shape, in_specs=specs, out_specs=jax.t...  19.1 us
    unnamed x31, local copies, waits for them, and re-layouts  8.18 us
  transfers between devices with their start and end apart: 17, of which 7 were waited for; matrix products, arithmetic and copies ran while one was open for 4% of the time, Pallas kernels for 10%

profile of v8, /device:TPU:1, one launch (start us, length us, event | category | flops | bytes accessed | tf_op | source)
XLA Modules:
  0.0 151.4 jit_solution(6829173509942100314)
XLA Ops:
  0.6 0.0 copy-start
  0.6 0.0 copy-start.10
  0.7 0.7 copy-done.10
  1.4 0.7 copy-done.12
  2.1 1.0 dispatch.1
  3.1 10.4 %all-to-all-start = ((bf16[32,32,128]{2,1,0:T(8,128)(2,1)}), bf16[32,32,128]{2,1,0:T(8,128)(2,1)S(1)}, u32[]{:S(2)}, u32[]{:S(2)}) async-start(bf16[32,32,128]{2,1,0:T(8,128)(2,1)} %dispatch.1), calls=%async_computation | async-start | bytes 524288 | tf_op jit(solution)/shard_map/all_to_all | solution.py:201
  13.5 3.4 %collective-permute-start = (bf16[40,576]{1,0:T(8,128)(2,1)S(1)}, bf16[40,576]{1,0:T(8,128)(2,1)S(1)}, u32[]{:S(2)}, u32[]{:S(2)}) collective-permute-start(bf16[40,576]{1,0:T(8,128)(2,1)S(1)} %constant_dynamic-slice_fusion), channel_id=1, source_target_pairs={{0,32},{32,0},{1,33},{33,1},{2,34},{34,2},{3,35},{35,3},{4,36},{36... | collective-permute-start | bytes 138248 | tf_op jit(solution)/shard_map/ppermute | solution.py:206
  16.9 5.7 %collective-permute-done = bf16[40,576]{1,0:T(8,128)(2,1)S(1)} collective-permute-done((bf16[40,576]{1,0:T(8,128)(2,1)S(1)}, bf16[40,576]{1,0:T(8,128)(2,1)S(1)}, u32[]{:S(2)}, u32[]{:S(2)}) %collective-permute-start) | collective-permute-done | bytes 46112 | tf_op jit(solution)/shard_map/ppermute | solution.py:206
  22.6 4.5 %all-to-all-done.after.arrived = bf16[32,32,128]{2,1,0:T(8,128)(2,1)S(1)} async-done(((bf16[32,32,128]{2,1,0:T(8,128)(2,1)}), bf16[32,32,128]{2,1,0:T(8,128)(2,1)S(1)}, u32[]{:S(2)}, u32[]{:S(2)}) %all-to-all-start) | async-done | bytes 262176 | tf_op jit(solution)/shard_map/all_to_all | solution.py:201
  27.1 1.0 pair.1
  28.1 6.5 %all-to-all-start.1 = ((bf16[8,80,576]{2,1,0:T(8,128)(2,1)}), bf16[8,80,576]{2,1,0:T(8,128)(2,1)S(1)}, u32[]{:S(2)}, u32[]{:S(2)}) async-start(bf16[8,80,576]{2,1,0:T(8,128)(2,1)} %pair.1), calls=%async_computation.1 | async-start | bytes 1638400 | tf_op jit(solution)/shard_map/all_to_all | solution.py:201
  34.5 0.8 cut.1
  35.3 2.3 %collective-permute-start.5 = (bf16[2,80,768]{2,1,0:T(8,128)(2,1)}, bf16[2,80,768]{2,1,0:T(8,128)(2,1)S(1)}, u32[]{:S(2)}, u32[]{:S(2)}) collective-permute-start(bf16[2,80,768]{2,1,0:T(8,128)(2,1)} %get-tuple-element.17), channel_id=1, source_target_pairs={{0,8},{8,16},{16,24},{24,0},{1,9},{9,17},{17,25},{25,1},{2,10},{10... | collective-permute-start | bytes 737288 | tf_op jit(solution)/shard_map/ppermute | solution.py:206
  37.6 3.9 %collective-permute-start.6 = (bf16[2,80,768]{2,1,0:T(8,128)(2,1)S(1)}, bf16[2,80,768]{2,1,0:T(8,128)(2,1)S(1)}, u32[]{:S(2)}, u32[]{:S(2)}) collective-permute-start(bf16[2,80,768]{2,1,0:T(8,128)(2,1)S(1)} %get-tuple-element.18), channel_id=1, source_target_pairs={{0,16},{8,24},{16,0},{24,8},{1,17},{9,25},{17,1},{25,9},{2,18},{10... | collective-permute-start | bytes 737288 | tf_op jit(solution)/shard_map/ppermute | solution.py:206
  41.5 3.0 %collective-permute-start.7 = (bf16[2,80,768]{2,1,0:T(8,128)(2,1)S(1)}, bf16[2,80,768]{2,1,0:T(8,128)(2,1)S(1)}, u32[]{:S(2)}, u32[]{:S(2)}) collective-permute-start(bf16[2,80,768]{2,1,0:T(8,128)(2,1)S(1)} %get-tuple-element.19), channel_id=1, source_target_pairs={{0,24},{8,0},{16,8},{24,16},{1,25},{9,1},{17,9},{25,17},{2,26},{10... | collective-permute-start | bytes 737288 | tf_op jit(solution)/shard_map/ppermute | solution.py:206
  44.5 0.1 iota.29
  44.6 0.1 iota.30
  44.7 0.1 iota.26
  44.7 0.1 iota.27
  44.9 0.1 iota.32
  45.0 1.7 %reshape.101.refs_5_.queries = bf16[512,576]{1,0:T(8,128)(2,1)S(1)} reshape(bf16[4,73728]{1,0:T(4,128)(2,1)} %param.9) | data formatting | bytes 1179648 | tf_op jit(solution)/shard_map/reshape | solution.py:243
  46.7 12.2 %all-to-all-done.1 = bf16[8,80,576]{2,1,0:T(8,128)(2,1)S(1)} async-done(((bf16[8,80,576]{2,1,0:T(8,128)(2,1)}), bf16[8,80,576]{2,1,0:T(8,128)(2,1)S(1)}, u32[]{:S(2)}, u32[]{:S(2)}) %all-to-all-start.1) | async-done | bytes 737312 | tf_op jit(solution)/shard_map/all_to_all | solution.py:201
  58.9 1.2 copy.19
  60.1 0.0 collective-permute-done.5.refs_1_
  60.1 0.0 collective-permute-done.6.refs_2_
  60.1 1.3 first.1
  61.4 3.5 %all-to-all-start.2 = ((bf16[8,32,768]{2,1,0:T(8,128)(2,1)}), bf16[8,32,768]{2,1,0:T(8,128)(2,1)S(1)}, u32[]{:S(2)}, u32[]{:S(2)}) async-start(bf16[8,32,768]{2,1,0:T(8,128)(2,1)} %bitcast.12), calls=%async_computation.2 | async-start | bytes 786432 | tf_op jit(solution)/shard_map/all_to_all | solution.py:201
  64.9 2.4 %collective-permute-start.2 = (bf16[576,640]{1,0:T(8,128)(2,1)}, bf16[576,640]{1,0:T(8,128)(2,1)S(1)}, u32[]{:S(2)}, u32[]{:S(2)}) collective-permute-start(bf16[576,640]{1,0:T(8,128)(2,1)} %bitcast.4.refs_0_), channel_id=1, source_target_pairs={{0,1},{1,0},{2,3},{3,2},{4,5},{5,4},{6,7},{7,6},{8,9},{9,8},{10,11... | collective-permute-start | bytes 2211848 | tf_op jit(solution)/shard_map/ppermute | solution.py:206
  67.2 2.3 %collective-permute-start.3 = (bf16[576,640]{1,0:T(8,128)(2,1)}, bf16[576,640]{1,0:T(8,128)(2,1)S(1)}, u32[]{:S(2)}, u32[]{:S(2)}) collective-permute-start(bf16[576,640]{1,0:T(8,128)(2,1)} %bitcast.4.refs_0_), channel_id=1, source_target_pairs={{0,8},{8,16},{16,24},{24,0},{1,9},{9,17},{17,25},{25,1},{2,10},{10... | collective-permute-start | bytes 2211848 | tf_op jit(solution)/shard_map/ppermute | solution.py:206
  69.5 4.2 %collective-permute-start.4 = (bf16[576,640]{1,0:T(8,128)(2,1)}, bf16[576,640]{1,0:T(8,128)(2,1)S(1)}, u32[]{:S(2)}, u32[]{:S(2)}) collective-permute-start(bf16[576,640]{1,0:T(8,128)(2,1)} %bitcast.4.refs_0_), channel_id=1, source_target_pairs={{0,24},{8,0},{16,8},{24,16},{1,25},{9,1},{17,9},{25,17},{2,26},{10... | collective-permute-start | bytes 2211848 | tf_op jit(solution)/shard_map/ppermute | solution.py:206
  73.7 6.2 %all-to-all-done.2.parts = bf16[8,32,768]{2,1,0:T(8,128)(2,1)S(1)} async-done(((bf16[8,32,768]{2,1,0:T(8,128)(2,1)}), bf16[8,32,768]{2,1,0:T(8,128)(2,1)S(1)}, u32[]{:S(2)}, u32[]{:S(2)}) %all-to-all-start.2) | async-done | bytes 393248 | tf_op jit(solution)/shard_map/all_to_all | solution.py:201
  79.9 0.1 add.126
  80.0 5.5 %collective-permute-start.8 = (bf16[32,768]{1,0:T(8,128)(2,1)S(1)}, bf16[32,768]{1,0:T(8,128)(2,1)S(1)}, u32[]{:S(2)}, u32[]{:S(2)}) collective-permute-start(bf16[32,768]{1,0:T(8,128)(2,1)S(1)} %get-tuple-element.21), channel_id=1, source_target_pairs={{0,32},{32,0},{1,33},{33,1},{2,34},{34,2},{3,35},{35,3},{4,36},{36... | collective-permute-start | bytes 147464 | tf_op jit(solution)/shard_map/ppermute | solution.py:206
  85.5 3.1 %collective-permute-done.3.refs_0_ = bf16[576,640]{1,0:T(8,128)(2,1)S(1)} collective-permute-done((bf16[576,640]{1,0:T(8,128)(2,1)}, bf16[576,640]{1,0:T(8,128)(2,1)S(1)}, u32[]{:S(2)}, u32[]{:S(2)}) %collective-permute-start.3) | collective-permute-done | bytes 737312 | tf_op jit(solution)/shard_map/ppermute | solution.py:206
  88.6 1.0 collective-permute-done.4.refs_1_
  89.6 0.0 collective-permute-done.8.other
  89.6 0.1 hidden.1
  89.7 0.9 copy-done.5
  90.6 10.3 %all-to-all-start.3 = ((bf16[32,32,384]{2,1,0:T(8,128)(2,1)}), bf16[32,32,384]{2,1,0:T(8,128)(2,1)S(1)}, u32[]{:S(2)}, u32[]{:S(2)}) async-start(bf16[32,32,384]{2,1,0:T(8,128)(2,1)} %copy-done.5), calls=%async_computation.3 | async-start | bytes 1572864 | tf_op jit(solution)/shard_map/all_to_all | solution.py:201
  100.9 3.3 %collective-permute-start.10 = (bf16[576,640]{1,0:T(8,128)(2,1)S(1)}, bf16[576,640]{1,0:T(8,128)(2,1)}, u32[]{:S(2)}, u32[]{:S(2)}) collective-permute-start(bf16[576,640]{1,0:T(8,128)(2,1)S(1)} %get-tuple-element.24.refs_4_), channel_id=1, source_target_pairs={{0,1},{1,0},{2,3},{3,2},{4,5},{5,4},{6,7},{7,6},{8,9},{9,8},{10,11... | collective-permute-start | bytes 2211848 | tf_op jit(solution)/shard_map/ppermute | solution.py:206
  104.2 1.9 %collective-permute-start.9 = (bf16[576,640]{1,0:T(8,128)(2,1)S(1)}, bf16[576,640]{1,0:T(8,128)(2,1)}, u32[]{:S(2)}, u32[]{:S(2)}) collective-permute-start(bf16[576,640]{1,0:T(8,128)(2,1)S(1)} %get-tuple-element.23.refs_2_), channel_id=1, source_target_pairs={{0,1},{1,0},{2,3},{3,2},{4,5},{5,4},{6,7},{7,6},{8,9},{9,8},{10,11... | collective-permute-start | bytes 2211848 | tf_op jit(solution)/shard_map/ppermute | solution.py:206
  106.2 4.9 %collective-permute-start.1 = (bf16[576,640]{1,0:T(8,128)(2,1)}, bf16[576,640]{1,0:T(8,128)(2,1)}, u32[]{:S(2)}, u32[]{:S(2)}) collective-permute-start(bf16[576,640]{1,0:T(8,128)(2,1)} %bitcast.4.refs_0_), channel_id=1, source_target_pairs={{0,16},{8,24},{16,0},{24,8},{1,17},{9,25},{17,1},{25,9},{2,18},{10... | collective-permute-start | bytes 2211848 | tf_op jit(solution)/shard_map/ppermute | solution.py:206
  111.8 0.1 stack.39.spots
  111.9 0.0 collective-permute-done.10.refs_5_
  111.9 0.0 collective-permute-done.9.refs_3_
  111.9 1.1 copy-done.2
  113.0 9.1 %attend_near.1 = (f32[512,128]{1,0:T(8,128)S(1)}, f32[512,128]{1,0:T(8,128)S(1)}, f32[512,512]{1,0:T(8,128)S(1)}, f32[8,128]{1,0:T(8,128)S(1)}) custom-call(s32[7]{0:T(128)S(1)} %stack.39.spots, bf16[512,576]{1,0:T(8,128)(2,1)S(1)} %reshape.101.refs_5_.queries, s32[1,640]{1,0:T(1,128)S(1)} %multiply_add_fusion.refs_6_.base, ...), custom_call_target="tpu_custom_call" | custom-call | flops 566231040 | bytes 684032 | tf_op jit(solution)/shard_map/attend_near/pallas_call | solution.py:35
  122.1 1.0 copy-done.3
  123.0 10.4 %collective-permute-done.1.refs_0_ = bf16[576,640]{1,0:T(8,128)(2,1)} collective-permute-done((bf16[576,640]{1,0:T(8,128)(2,1)}, bf16[576,640]{1,0:T(8,128)(2,1)}, u32[]{:S(2)}, u32[]{:S(2)}) %collective-permute-start.1) | collective-permute-done | bytes 737312 | tf_op jit(solution)/shard_map/ppermute | solution.py:206
  133.5 3.1 %collective-permute-start.11 = (bf16[576,640]{1,0:T(8,128)(2,1)}, bf16[576,640]{1,0:T(8,128)(2,1)S(1)}, u32[]{:S(2)}, u32[]{:S(2)}) collective-permute-start(bf16[576,640]{1,0:T(8,128)(2,1)} %hold.3.refs_0_), channel_id=1, source_target_pairs={{0,1},{1,0},{2,3},{3,2},{4,5},{5,4},{6,7},{7,6},{8,9},{9,8},{10,11... | collective-permute-start | bytes 2211848 | tf_op jit(solution)/shard_map/ppermute | solution.py:206
  136.6 0.1 copy.21.routes
  136.7 1.4 copy.20.down
  138.1 0.1 copy.22.gates
  138.2 0.0 all-to-all-done.3.hidden
  138.2 1.0 second.1
  139.2 4.0 %all-to-all-start.4 = ((bf16[8,32,128]{2,1,0:T(8,128)(2,1)}), bf16[8,32,128]{2,1,0:T(8,128)(2,1)S(1)}, u32[]{:S(2)}, u32[]{:S(2)}) async-start(bf16[8,32,128]{2,1,0:T(8,128)(2,1)} %second.1), calls=%async_computation.4 | async-start | bytes 131072 | tf_op jit(solution)/shard_map/all_to_all | solution.py:201
  143.2 0.1 pad_add_fusion.spots
  143.2 0.0 collective-permute-done.11.refs_1_
  143.2 1.2 copy-done.4
  144.5 0.9 copy-done.9
  145.4 3.8 %attend_far.1 = bf16[512,512]{1,0:T(8,128)(2,1)S(1)} custom-call(s32[3]{0:T(128)S(1)} %pad_add_fusion.spots, bf16[512,576]{1,0:T(8,128)(2,1)S(1)} %reshape.101.refs_5_.queries, s32[1,640]{1,0:T(1,128)S(1)} %multiply_add_fusion.refs_6_.base, bf16[576,640]{1,0:T(8,128)(2,1)} %hold.3.refs_0_, bf16[576,640]{1,0:T(8,128)(2,1)S(1)} %collective-permute-done.11.refs_1_, ...), custom_call_target="tpu_custom_call" | custom-call | flops 188743680 | bytes 315392 | tf_op jit(solution)/shard_map/attend_far/pallas_call | solution.py:35
  149.2 1.2 reshape.105
  150.4 0.0 all-to-all-done.4.back
  150.4 1.0 combine.1
  (29 shorter events, 0.1 us)
Async XLA Ops:
  0.6 12.9 %copy-start = (bf16[80,576]{1,0:T(8,128)(2,1)S(1)}, bf16[80,576]{1,0:T(8,128)(2,1)}, u32[]{:S(2)}) copy-start(bf16[80,576]{1,0:T(8,128)(2,1)} %param.10) | copy-start | bytes 276484
  0.6 0.7 copy-start.10
  1.4 0.7 copy-start.12
  3.1 24.0 %all-to-all-start = ((bf16[32,32,128]{2,1,0:T(8,128)(2,1)}), bf16[32,32,128]{2,1,0:T(8,128)(2,1)S(1)}, u32[]{:S(2)}, u32[]{:S(2)}) async-start(bf16[32,32,128]{2,1,0:T(8,128)(2,1)} %dispatch.1), calls=%async_computation | async-start | bytes 524288 | tf_op jit(solution)/shard_map/all_to_all | solution.py:201
  13.5 9.1 %collective-permute-start = (bf16[40,576]{1,0:T(8,128)(2,1)S(1)}, bf16[40,576]{1,0:T(8,128)(2,1)S(1)}, u32[]{:S(2)}, u32[]{:S(2)}) collective-permute-start(bf16[40,576]{1,0:T(8,128)(2,1)S(1)} %constant_dynamic-slice_fusion), channel_id=1, source_target_pairs={{0,32},{32,0},{1,33},{33,1},{2,34},{34,2},{3,35},{35,3},{4,36},{36... | collective-permute-start | bytes 138248 | tf_op jit(solution)/shard_map/ppermute | solution.py:206
  28.1 6.5 %copy-start.6 = (bf16[2,80,1536]{2,1,0:T(8,128)(2,1)S(1)}, bf16[2,80,1536]{2,1,0:T(8,128)(2,1)}, u32[]{:S(2)}) copy-start(bf16[2,80,1536]{2,1,0:T(8,128)(2,1)} %gate.1) | copy-start | bytes 1474564
  28.1 6.5 %copy-start.7 = (bf16[2,80,1536]{2,1,0:T(8,128)(2,1)S(1)}, bf16[2,80,1536]{2,1,0:T(8,128)(2,1)}, u32[]{:S(2)}) copy-start(bf16[2,80,1536]{2,1,0:T(8,128)(2,1)} %up.1) | copy-start | bytes 1474564
  28.1 30.8 %all-to-all-start.1 = ((bf16[8,80,576]{2,1,0:T(8,128)(2,1)}), bf16[8,80,576]{2,1,0:T(8,128)(2,1)S(1)}, u32[]{:S(2)}, u32[]{:S(2)}) async-start(bf16[8,80,576]{2,1,0:T(8,128)(2,1)} %pair.1), calls=%async_computation.1 | async-start | bytes 1638400 | tf_op jit(solution)/shard_map/all_to_all | solution.py:201
  35.3 24.8 %collective-permute-start.5 = (bf16[2,80,768]{2,1,0:T(8,128)(2,1)}, bf16[2,80,768]{2,1,0:T(8,128)(2,1)S(1)}, u32[]{:S(2)}, u32[]{:S(2)}) collective-permute-start(bf16[2,80,768]{2,1,0:T(8,128)(2,1)} %get-tuple-element.17), channel_id=1, source_target_pairs={{0,8},{8,16},{16,24},{24,0},{1,9},{9,17},{17,25},{25,1},{2,10},{10... | collective-permute-start | bytes 737288 | tf_op jit(solution)/shard_map/ppermute | solution.py:206
  37.6 22.5 %collective-permute-start.6 = (bf16[2,80,768]{2,1,0:T(8,128)(2,1)S(1)}, bf16[2,80,768]{2,1,0:T(8,128)(2,1)S(1)}, u32[]{:S(2)}, u32[]{:S(2)}) collective-permute-start(bf16[2,80,768]{2,1,0:T(8,128)(2,1)S(1)} %get-tuple-element.18), channel_id=1, source_target_pairs={{0,16},{8,24},{16,0},{24,8},{1,17},{9,25},{17,1},{25,9},{2,18},{10... | collective-permute-start | bytes 737288 | tf_op jit(solution)/shard_map/ppermute | solution.py:206
  41.5 18.6 %collective-permute-start.7 = (bf16[2,80,768]{2,1,0:T(8,128)(2,1)S(1)}, bf16[2,80,768]{2,1,0:T(8,128)(2,1)S(1)}, u32[]{:S(2)}, u32[]{:S(2)}) collective-permute-start(bf16[2,80,768]{2,1,0:T(8,128)(2,1)S(1)} %get-tuple-element.19), channel_id=1, source_target_pairs={{0,24},{8,0},{16,8},{24,16},{1,25},{9,1},{17,9},{25,17},{2,26},{10... | collective-permute-start | bytes 737288 | tf_op jit(solution)/shard_map/ppermute | solution.py:206
  61.4 18.5 %all-to-all-start.2 = ((bf16[8,32,768]{2,1,0:T(8,128)(2,1)}), bf16[8,32,768]{2,1,0:T(8,128)(2,1)S(1)}, u32[]{:S(2)}, u32[]{:S(2)}) async-start(bf16[8,32,768]{2,1,0:T(8,128)(2,1)} %bitcast.12), calls=%async_computation.2 | async-start | bytes 786432 | tf_op jit(solution)/shard_map/all_to_all | solution.py:201
  64.9 20.6 %collective-permute-start.2 = (bf16[576,640]{1,0:T(8,128)(2,1)}, bf16[576,640]{1,0:T(8,128)(2,1)S(1)}, u32[]{:S(2)}, u32[]{:S(2)}) collective-permute-start(bf16[576,640]{1,0:T(8,128)(2,1)} %bitcast.4.refs_0_), channel_id=1, source_target_pairs={{0,1},{1,0},{2,3},{3,2},{4,5},{5,4},{6,7},{7,6},{8,9},{9,8},{10,11... | collective-permute-start | bytes 2211848 | tf_op jit(solution)/shard_map/ppermute | solution.py:206
  67.2 21.4 %collective-permute-start.3 = (bf16[576,640]{1,0:T(8,128)(2,1)}, bf16[576,640]{1,0:T(8,128)(2,1)S(1)}, u32[]{:S(2)}, u32[]{:S(2)}) collective-permute-start(bf16[576,640]{1,0:T(8,128)(2,1)} %bitcast.4.refs_0_), channel_id=1, source_target_pairs={{0,8},{8,16},{16,24},{24,0},{1,9},{9,17},{17,25},{25,1},{2,10},{10... | collective-permute-start | bytes 2211848 | tf_op jit(solution)/shard_map/ppermute | solution.py:206
  69.5 20.1 %collective-permute-start.4 = (bf16[576,640]{1,0:T(8,128)(2,1)}, bf16[576,640]{1,0:T(8,128)(2,1)S(1)}, u32[]{:S(2)}, u32[]{:S(2)}) collective-permute-start(bf16[576,640]{1,0:T(8,128)(2,1)} %bitcast.4.refs_0_), channel_id=1, source_target_pairs={{0,24},{8,0},{16,8},{24,16},{1,25},{9,1},{17,9},{25,17},{2,26},{10... | collective-permute-start | bytes 2211848 | tf_op jit(solution)/shard_map/ppermute | solution.py:206
  80.0 9.6 %collective-permute-start.8 = (bf16[32,768]{1,0:T(8,128)(2,1)S(1)}, bf16[32,768]{1,0:T(8,128)(2,1)S(1)}, u32[]{:S(2)}, u32[]{:S(2)}) collective-permute-start(bf16[32,768]{1,0:T(8,128)(2,1)S(1)} %get-tuple-element.21), channel_id=1, source_target_pairs={{0,32},{32,0},{1,33},{33,1},{2,34},{34,2},{3,35},{35,3},{4,36},{36... | collective-permute-start | bytes 147464 | tf_op jit(solution)/shard_map/ppermute | solution.py:206
  85.5 4.2 %copy-start.1 = (bf16[576,640]{1,0:T(8,128)(2,1)}, bf16[576,640]{1,0:T(8,128)(2,1)S(1)}, u32[]{:S(2)}) copy-start(bf16[576,640]{1,0:T(8,128)(2,1)S(1)} %collective-permute-done.2.refs_2_.refs_1_) | copy-start | bytes 2211844
  89.7 0.9 copy-start.5
  90.6 47.6 %all-to-all-start.3 = ((bf16[32,32,384]{2,1,0:T(8,128)(2,1)}), bf16[32,32,384]{2,1,0:T(8,128)(2,1)S(1)}, u32[]{:S(2)}, u32[]{:S(2)}) async-start(bf16[32,32,384]{2,1,0:T(8,128)(2,1)} %copy-done.5), calls=%async_computation.3 | async-start | bytes 1572864 | tf_op jit(solution)/shard_map/all_to_all | solution.py:201
  100.9 10.9 %collective-permute-start.10 = (bf16[576,640]{1,0:T(8,128)(2,1)S(1)}, bf16[576,640]{1,0:T(8,128)(2,1)}, u32[]{:S(2)}, u32[]{:S(2)}) collective-permute-start(bf16[576,640]{1,0:T(8,128)(2,1)S(1)} %get-tuple-element.24.refs_4_), channel_id=1, source_target_pairs={{0,1},{1,0},{2,3},{3,2},{4,5},{5,4},{6,7},{7,6},{8,9},{9,8},{10,11... | collective-permute-start | bytes 2211848 | tf_op jit(solution)/shard_map/ppermute | solution.py:206
  104.2 7.6 %collective-permute-start.9 = (bf16[576,640]{1,0:T(8,128)(2,1)S(1)}, bf16[576,640]{1,0:T(8,128)(2,1)}, u32[]{:S(2)}, u32[]{:S(2)}) collective-permute-start(bf16[576,640]{1,0:T(8,128)(2,1)S(1)} %get-tuple-element.23.refs_2_), channel_id=1, source_target_pairs={{0,1},{1,0},{2,3},{3,2},{4,5},{5,4},{6,7},{7,6},{8,9},{9,8},{10,11... | collective-permute-start | bytes 2211848 | tf_op jit(solution)/shard_map/ppermute | solution.py:206
  106.2 27.3 %collective-permute-start.1 = (bf16[576,640]{1,0:T(8,128)(2,1)}, bf16[576,640]{1,0:T(8,128)(2,1)}, u32[]{:S(2)}, u32[]{:S(2)}) collective-permute-start(bf16[576,640]{1,0:T(8,128)(2,1)} %bitcast.4.refs_0_), channel_id=1, source_target_pairs={{0,16},{8,24},{16,0},{24,8},{1,17},{9,25},{17,1},{25,9},{2,18},{10... | collective-permute-start | bytes 2211848 | tf_op jit(solution)/shard_map/ppermute | solution.py:206
  111.9 1.1 copy-start.2
  122.1 1.0 copy-start.3
  123.0 10.4 %copy-start.8 = (f32[512,128]{1,0:T(8,128)}, f32[512,128]{1,0:T(8,128)S(1)}, u32[]{:S(2)}) copy-start(f32[512,128]{1,0:T(8,128)S(1)} %get-tuple-element.27.refs_3_) | copy-start | bytes 786436
  133.5 3.1 %copy-start.11 = (s32[32,6]{0,1:T(8,128)S(1)}, s32[32,6]{0,1:T(8,128)}, u32[]{:S(2)}) copy-start(s32[32,6]{0,1:T(8,128)} %param.13) | copy-start | bytes 2308
  133.5 9.8 %collective-permute-start.11 = (bf16[576,640]{1,0:T(8,128)(2,1)}, bf16[576,640]{1,0:T(8,128)(2,1)S(1)}, u32[]{:S(2)}, u32[]{:S(2)}) collective-permute-start(bf16[576,640]{1,0:T(8,128)(2,1)} %hold.3.refs_0_), channel_id=1, source_target_pairs={{0,1},{1,0},{2,3},{3,2},{4,5},{5,4},{6,7},{7,6},{8,9},{9,8},{10,11... | collective-permute-start | bytes 2211848 | tf_op jit(solution)/shard_map/ppermute | solution.py:206
  136.7 1.4 copy-start.13
  139.2 11.2 %all-to-all-start.4 = ((bf16[8,32,128]{2,1,0:T(8,128)(2,1)}), bf16[8,32,128]{2,1,0:T(8,128)(2,1)S(1)}, u32[]{:S(2)}, u32[]{:S(2)}) async-start(bf16[8,32,128]{2,1,0:T(8,128)(2,1)} %second.1), calls=%async_computation.4 | async-start | bytes 131072 | tf_op jit(solution)/shard_map/all_to_all | solution.py:201
  143.2 1.2 copy-start.4
  144.5 0.9 copy-start.9

commit v9 on v8

--- a/solution.py
+++ b/solution.py
@@ -256,11 +256,6 @@
         [VMEM], (parts,), 2**18, 2**19,
     )
     added = shift(rounded, "h", 1)
-    hidden, token = kernel(
-        hidden_body, "hidden", [shaped((nz * nx, rows, units), BF16), shaped((8, LANES), F32)],
-        [VMEM] * 2 + [AFTER] * 3, (total, added, *others[:2], swapped), 2**18, 2**20, 2**14,
-    )
-    hidden = exchange(hidden, ("z", "x"))
     sources = [x_at, x_at + nx - 1, x_at + 1, x_at + 2]
     spots = []
     for source in sources:
@@ -272,10 +267,16 @@
         both = [p for piece in pieces for p in (piece, swapped if piece is column else shift(piece, "c", 1))]
         return attend(marks, query_rows, base, both, state, last, name)
 
-    near, far = hold(others[:2], [token])
-    *state, seen = call([0, 1, 2], [column, near, far], [], False, "attend_near")
-    (opposite,) = hold(others[2:], [seen])
+    *state, seen = call([0], [column], [], False, "attend_own")
+    near, far, opposite = hold(others, [added, seen])
+    hidden, token = kernel(
+        hidden_body, "hidden", [shaped((nz * nx, rows, units), BF16), shaped((8, LANES), F32)],
+        [VMEM] * 2 + [AFTER] * 2, (total, added, opposite, seen), 2**18, 2**20, 2**14,
+    )
+    near, far, opposite = hold([near, far, opposite], [token])
+    *state, seen = call([1, 2], [near, far], state, False, "attend_near")
     mixed = call([3], [opposite], state, True, "attend_far")
+    hidden = exchange(hidden, ("z", "x"))
     result = kernel(
         functools.partial(second_body, nz, nx), "second", shaped((owners, slots, LANES), BF16),
         [VMEM] * 2 + [AFTER], (hidden, w_down, seen), 2**27, 2**21,

time: 153 us -> 156 us (1.020)
  local copies, waits for them, and re-layouts: 12.8 us -> 16.9 us
  waiting for transfers between devices: 43 us -> 40.4 us
  Pallas kernels: 19.1 us -> 21.7 us
    all_to_all x5, waiting for transfers between devices: 22.8 us -> 12.6 us  [exchange(): return lax.all_to_all(array, axes, split_axis=0, concat_axis=0, tiled=False)]
    ppermute x12, waiting for transfers between devices: 20.2 us -> 27.8 us  [shift(): lax.ppermute(array, axis, [(i, (i + by) % size) for i in range(size)])]
    unnamed x31 -> x41, local copies, waits for them, and re-layouts: 8.18 us -> 12.3 us
    ppermute x12, starting transfers between devices: 40.1 us -> 36.5 us  [shift(): lax.ppermute(array, axis, [(i, (i + by) % size) for i in range(size)])]
    all_to_all x5, starting transfers between devices: 34.6 us -> 37.5 us  [exchange(): return lax.all_to_all(array, axes, split_axis=0, concat_axis=0, tiled=False)]
    pallas_call x10 -> x11, Pallas kernels: 19.1 us -> 21.7 us  [kernel(): pl.pallas_call(body, out_shape=out_shape, in_specs=specs, out_specs=jax.t...]
  transfers between devices with their start and end apart: 17 -> 17, of which waited for: 7 -> 9; matrix products, arithmetic and copies ran while one was open for 4% -> 5% of each run, Pallas kernels for 10% -> 11%
where the time goes in v9:
time: 156 us; the launch traced here: 155 us
  starting transfers between devices  74 us (47%)
  waiting for transfers between devices  40.4 us (26%)
  Pallas kernels  21.7 us (14%)
  local copies, waits for them, and re-layouts  16.9 us (11%)
  between operations  1.71 us (1%)
    all_to_all x5, starting transfers between devices, exchange(): return lax.all_to_all(array, axes, split_axis=0, concat_axis=0, tiled=False)  37.5 us
    ppermute x12, starting transfers between devices, shift(): lax.ppermute(array, axis, [(i, (i + by) % size) for i in range(size)])  36.5 us
    ppermute x12, waiting for transfers between devices, shift(): lax.ppermute(array, axis, [(i, (i + by) % size) for i in range(size)])  27.8 us
    pallas_call x11, Pallas kernels, kernel(): pl.pallas_call(body, out_shape=out_shape, in_specs=specs, out_specs=jax.t...  21.7 us
    all_to_all x5, waiting for transfers between devices, exchange(): return lax.all_to_all(array, axes, split_axis=0, concat_axis=0, tiled=False)  12.6 us
    unnamed x41, local copies, waits for them, and re-layouts  12.3 us
  transfers between devices with their start and end apart: 17, of which 9 were waited for; matrix products, arithmetic and copies ran while one was open for 5% of the time, Pallas kernels for 11%

profile of v9, /device:TPU:1, one launch (start us, length us, event | category | flops | bytes accessed | tf_op | source)
XLA Modules:
  0.0 154.9 jit_solution(9319143122046884734)
XLA Ops:
  0.6 0.0 copy-start
  0.7 0.7 copy-done.15
  1.4 0.7 copy-done.17
  2.1 1.0 dispatch.1
  3.1 10.4 %all-to-all-start = ((bf16[32,32,128]{2,1,0:T(8,128)(2,1)}), bf16[32,32,128]{2,1,0:T(8,128)(2,1)S(1)}, u32[]{:S(2)}, u32[]{:S(2)}) async-start(bf16[32,32,128]{2,1,0:T(8,128)(2,1)} %dispatch.1), calls=%async_computation | async-start | bytes 524288 | tf_op jit(solution)/shard_map/all_to_all | solution.py:201
  13.5 3.4 %collective-permute-start = (bf16[40,576]{1,0:T(8,128)(2,1)S(1)}, bf16[40,576]{1,0:T(8,128)(2,1)S(1)}, u32[]{:S(2)}, u32[]{:S(2)}) collective-permute-start(bf16[40,576]{1,0:T(8,128)(2,1)S(1)} %constant_dynamic-slice_fusion), channel_id=1, source_target_pairs={{0,32},{32,0},{1,33},{33,1},{2,34},{34,2},{3,35},{35,3},{4,36},{36... | collective-permute-start | bytes 138248 | tf_op jit(solution)/shard_map/ppermute | solution.py:206
  16.9 5.7 %collective-permute-done = bf16[40,576]{1,0:T(8,128)(2,1)S(1)} collective-permute-done((bf16[40,576]{1,0:T(8,128)(2,1)S(1)}, bf16[40,576]{1,0:T(8,128)(2,1)S(1)}, u32[]{:S(2)}, u32[]{:S(2)}) %collective-permute-start) | collective-permute-done | bytes 46112 | tf_op jit(solution)/shard_map/ppermute | solution.py:206
  22.6 4.5 %all-to-all-done.after.arrived = bf16[32,32,128]{2,1,0:T(8,128)(2,1)S(1)} async-done(((bf16[32,32,128]{2,1,0:T(8,128)(2,1)}), bf16[32,32,128]{2,1,0:T(8,128)(2,1)S(1)}, u32[]{:S(2)}, u32[]{:S(2)}) %all-to-all-start) | async-done | bytes 262176 | tf_op jit(solution)/shard_map/all_to_all | solution.py:201
  27.1 1.0 pair.1
  28.1 6.5 %all-to-all-start.1 = ((bf16[8,80,576]{2,1,0:T(8,128)(2,1)}), bf16[8,80,576]{2,1,0:T(8,128)(2,1)S(1)}, u32[]{:S(2)}, u32[]{:S(2)}) async-start(bf16[8,80,576]{2,1,0:T(8,128)(2,1)} %pair.1), calls=%async_computation.1 | async-start | bytes 1638400 | tf_op jit(solution)/shard_map/all_to_all | solution.py:201
  34.5 0.8 cut.1
  35.3 2.3 %collective-permute-start.4 = (bf16[2,80,768]{2,1,0:T(8,128)(2,1)}, bf16[2,80,768]{2,1,0:T(8,128)(2,1)S(1)}, u32[]{:S(2)}, u32[]{:S(2)}) collective-permute-start(bf16[2,80,768]{2,1,0:T(8,128)(2,1)} %get-tuple-element.25), channel_id=1, source_target_pairs={{0,8},{8,16},{16,24},{24,0},{1,9},{9,17},{17,25},{25,1},{2,10},{10... | collective-permute-start | bytes 737288 | tf_op jit(solution)/shard_map/ppermute | solution.py:206
  37.6 3.9 %collective-permute-start.5 = (bf16[2,80,768]{2,1,0:T(8,128)(2,1)S(1)}, bf16[2,80,768]{2,1,0:T(8,128)(2,1)S(1)}, u32[]{:S(2)}, u32[]{:S(2)}) collective-permute-start(bf16[2,80,768]{2,1,0:T(8,128)(2,1)S(1)} %get-tuple-element.26), channel_id=1, source_target_pairs={{0,16},{8,24},{16,0},{24,8},{1,17},{9,25},{17,1},{25,9},{2,18},{10... | collective-permute-start | bytes 737288 | tf_op jit(solution)/shard_map/ppermute | solution.py:206
  41.5 3.0 %collective-permute-start.6 = (bf16[2,80,768]{2,1,0:T(8,128)(2,1)S(1)}, bf16[2,80,768]{2,1,0:T(8,128)(2,1)S(1)}, u32[]{:S(2)}, u32[]{:S(2)}) collective-permute-start(bf16[2,80,768]{2,1,0:T(8,128)(2,1)S(1)} %get-tuple-element.27), channel_id=1, source_target_pairs={{0,24},{8,0},{16,8},{24,16},{1,25},{9,1},{17,9},{25,17},{2,26},{10... | collective-permute-start | bytes 737288 | tf_op jit(solution)/shard_map/ppermute | solution.py:206
  44.5 0.1 iota.29
  44.6 0.1 iota.30
  44.7 0.1 iota.26
  44.7 0.1 iota.27
  44.9 0.1 iota.32
  44.9 1.7 %reshape.101.refs_5_.queries = bf16[512,576]{1,0:T(8,128)(2,1)S(1)} reshape(bf16[4,73728]{1,0:T(4,128)(2,1)} %param.9) | data formatting | bytes 1179648 | tf_op jit(solution)/shard_map/reshape | solution.py:243
  46.7 3.6 %collective-permute-done.5.refs_2_ = bf16[2,80,768]{2,1,0:T(8,128)(2,1)S(1)} collective-permute-done((bf16[2,80,768]{2,1,0:T(8,128)(2,1)S(1)}, bf16[2,80,768]{2,1,0:T(8,128)(2,1)S(1)}, u32[]{:S(2)}, u32[]{:S(2)}) %collective-permute-start.5) | collective-permute-done | bytes 245792 | tf_op jit(solution)/shard_map/ppermute | solution.py:206
  50.3 2.8 %collective-permute-done.6.refs_3_ = bf16[2,80,768]{2,1,0:T(8,128)(2,1)S(1)} collective-permute-done((bf16[2,80,768]{2,1,0:T(8,128)(2,1)S(1)}, bf16[2,80,768]{2,1,0:T(8,128)(2,1)S(1)}, u32[]{:S(2)}, u32[]{:S(2)}) %collective-permute-start.6) | collective-permute-done | bytes 245792 | tf_op jit(solution)/shard_map/ppermute | solution.py:206
  53.1 5.8 %all-to-all-done.1 = bf16[8,80,576]{2,1,0:T(8,128)(2,1)S(1)} async-done(((bf16[8,80,576]{2,1,0:T(8,128)(2,1)}), bf16[8,80,576]{2,1,0:T(8,128)(2,1)S(1)}, u32[]{:S(2)}, u32[]{:S(2)}) %all-to-all-start.1) | async-done | bytes 737312 | tf_op jit(solution)/shard_map/all_to_all | solution.py:201
  58.9 1.3 first.1
  60.2 3.5 %all-to-all-start.2 = ((bf16[8,32,768]{2,1,0:T(8,128)(2,1)}), bf16[8,32,768]{2,1,0:T(8,128)(2,1)S(1)}, u32[]{:S(2)}, u32[]{:S(2)}) async-start(bf16[8,32,768]{2,1,0:T(8,128)(2,1)} %bitcast.6), calls=%async_computation.2 | async-start | bytes 786432 | tf_op jit(solution)/shard_map/all_to_all | solution.py:201
  63.6 1.2 copy.22
  64.8 2.4 %collective-permute-start.8 = (bf16[576,640]{1,0:T(8,128)(2,1)}, bf16[576,640]{1,0:T(8,128)(2,1)}, u32[]{:S(2)}, u32[]{:S(2)}) collective-permute-start(bf16[576,640]{1,0:T(8,128)(2,1)} %bitcast.4.refs_0_), channel_id=1, source_target_pairs={{0,1},{1,0},{2,3},{3,2},{4,5},{5,4},{6,7},{7,6},{8,9},{9,8},{10,11... | collective-permute-start | bytes 2211848 | tf_op jit(solution)/shard_map/ppermute | solution.py:206
  67.2 2.3 %collective-permute-start.1 = (bf16[576,640]{1,0:T(8,128)(2,1)}, bf16[576,640]{1,0:T(8,128)(2,1)S(1)}, u32[]{:S(2)}, u32[]{:S(2)}) collective-permute-start(bf16[576,640]{1,0:T(8,128)(2,1)} %bitcast.4.refs_0_), channel_id=1, source_target_pairs={{0,8},{8,16},{16,24},{24,0},{1,9},{9,17},{17,25},{25,1},{2,10},{10... | collective-permute-start | bytes 2211848 | tf_op jit(solution)/shard_map/ppermute | solution.py:206
  69.5 4.2 %collective-permute-start.2 = (bf16[576,640]{1,0:T(8,128)(2,1)}, bf16[576,640]{1,0:T(8,128)(2,1)S(1)}, u32[]{:S(2)}, u32[]{:S(2)}) collective-permute-start(bf16[576,640]{1,0:T(8,128)(2,1)} %bitcast.4.refs_0_), channel_id=1, source_target_pairs={{0,24},{8,0},{16,8},{24,16},{1,25},{9,1},{17,9},{25,17},{2,26},{10... | collective-permute-start | bytes 2211848 | tf_op jit(solution)/shard_map/ppermute | solution.py:206
  73.7 2.0 %collective-permute-start.3 = (bf16[576,640]{1,0:T(8,128)(2,1)}, bf16[576,640]{1,0:T(8,128)(2,1)S(1)}, u32[]{:S(2)}, u32[]{:S(2)}) collective-permute-start(bf16[576,640]{1,0:T(8,128)(2,1)} %bitcast.4.refs_0_), channel_id=1, source_target_pairs={{0,16},{8,24},{16,0},{24,8},{1,17},{9,25},{17,1},{25,9},{2,18},{10... | collective-permute-start | bytes 2211848 | tf_op jit(solution)/shard_map/ppermute | solution.py:206
  76.4 2.3 %all-to-all-done.2.parts = bf16[8,32,768]{2,1,0:T(8,128)(2,1)S(1)} async-done(((bf16[8,32,768]{2,1,0:T(8,128)(2,1)}), bf16[8,32,768]{2,1,0:T(8,128)(2,1)S(1)}, u32[]{:S(2)}, u32[]{:S(2)}) %all-to-all-start.2) | async-done | bytes 393248 | tf_op jit(solution)/shard_map/all_to_all | solution.py:201
  78.7 0.1 add.130
  78.7 5.5 %collective-permute-start.7 = (bf16[32,768]{1,0:T(8,128)(2,1)S(1)}, bf16[32,768]{1,0:T(8,128)(2,1)S(1)}, u32[]{:S(2)}, u32[]{:S(2)}) collective-permute-start(bf16[32,768]{1,0:T(8,128)(2,1)S(1)} %get-tuple-element.28), channel_id=1, source_target_pairs={{0,32},{32,0},{1,33},{33,1},{2,34},{34,2},{3,35},{35,3},{4,36},{36... | collective-permute-start | bytes 147464 | tf_op jit(solution)/shard_map/ppermute | solution.py:206
  84.3 0.1 pad_add_fusion.1.spots
  84.3 4.0 %attend_own.1 = (f32[512,128]{1,0:T(8,128)S(1)}, f32[512,128]{1,0:T(8,128)S(1)}, f32[512,512]{1,0:T(8,128)S(1)}, f32[8,128]{1,0:T(8,128)S(1)}) custom-call(s32[3]{0:T(128)S(1)} %pad_add_fusion.1.spots, bf16[512,576]{1,0:T(8,128)(2,1)S(1)} %reshape.101.refs_5_.queries, s32[1,640]{1,0:T(1,128)S(1)} %multiply_add_fusion.refs_6_.base, ...), custom_call_target="tpu_custom_call" | custom-call | flops 188743680 | bytes 315392 | tf_op jit(solution)/shard_map/attend_own/pallas_call | solution.py:35
  88.4 0.0 copy-start.11
  88.4 0.5 collective-permute-done.1.refs_0_
  88.9 1.2 collective-permute-done.2.refs_1_
  90.1 13.9 %collective-permute-done.3.refs_2_ = bf16[576,640]{1,0:T(8,128)(2,1)S(1)} collective-permute-done((bf16[576,640]{1,0:T(8,128)(2,1)}, bf16[576,640]{1,0:T(8,128)(2,1)S(1)}, u32[]{:S(2)}, u32[]{:S(2)}) %collective-permute-start.3) | collective-permute-done | bytes 737312 | tf_op jit(solution)/shard_map/ppermute | solution.py:206
  104.1 0.1 hidden.1
  104.2 0.9 copy-done.6
  105.1 11.7 %all-to-all-start.3 = ((bf16[32,32,384]{2,1,0:T(8,128)(2,1)}), bf16[32,32,384]{2,1,0:T(8,128)(2,1)}, u32[]{:S(2)}, u32[]{:S(2)}) async-start(bf16[32,32,384]{2,1,0:T(8,128)(2,1)} %copy-done.6), calls=%async_computation.3 | async-start | bytes 1572864 | tf_op jit(solution)/shard_map/all_to_all | solution.py:201
  116.8 3.3 %collective-permute-start.10 = (bf16[576,640]{1,0:T(8,128)(2,1)S(1)}, bf16[576,640]{1,0:T(8,128)(2,1)}, u32[]{:S(2)}, u32[]{:S(2)}) collective-permute-start(bf16[576,640]{1,0:T(8,128)(2,1)S(1)} %get-tuple-element.36.refs_0_), channel_id=1, source_target_pairs={{0,1},{1,0},{2,3},{3,2},{4,5},{5,4},{6,7},{7,6},{8,9},{9,8},{10,11... | collective-permute-start | bytes 2211848 | tf_op jit(solution)/shard_map/ppermute | solution.py:206
  120.1 1.9 %collective-permute-start.11 = (bf16[576,640]{1,0:T(8,128)(2,1)S(1)}, bf16[576,640]{1,0:T(8,128)(2,1)}, u32[]{:S(2)}, u32[]{:S(2)}) collective-permute-start(bf16[576,640]{1,0:T(8,128)(2,1)S(1)} %get-tuple-element.37.refs_2_), channel_id=1, source_target_pairs={{0,1},{1,0},{2,3},{3,2},{4,5},{5,4},{6,7},{7,6},{8,9},{9,8},{10,11... | collective-permute-start | bytes 2211848 | tf_op jit(solution)/shard_map/ppermute | solution.py:206
  122.0 2.4 %collective-permute-start.9 = (bf16[576,640]{1,0:T(8,128)(2,1)S(1)}, bf16[576,640]{1,0:T(8,128)(2,1)}, u32[]{:S(2)}, u32[]{:S(2)}) collective-permute-start(bf16[576,640]{1,0:T(8,128)(2,1)S(1)} %get-tuple-element.35.refs_0_), channel_id=1, source_target_pairs={{0,1},{1,0},{2,3},{3,2},{4,5},{5,4},{6,7},{7,6},{8,9},{9,8},{10,11... | collective-permute-start | bytes 2211848 | tf_op jit(solution)/shard_map/ppermute | solution.py:206
  124.5 0.7 copy-done.16
  125.2 0.1 copy.24.routes
  125.2 2.2 %copy.23.down = bf16[2,1536,80]{2,1,0:T(8,128)(2,1)} copy(bf16[2,1536,80]{1,2,0:T(8,128)(2,1)} %param.17) | data formatting | bytes 983040 | tf_op args[8]
  127.5 0.1 copy.25.gates
  127.6 0.1 stack.43.spots
  127.7 1.2 copy-done.3
  128.9 0.9 copy-done.12
  129.8 0.9 copy-done.14
  130.8 6.5 %attend_near.1 = (f32[512,128]{1,0:T(8,128)S(1)}, f32[512,128]{1,0:T(8,128)S(1)}, f32[512,512]{1,0:T(8,128)S(1)}, f32[8,128]{1,0:T(8,128)S(1)}) custom-call(s32[5]{0:T(128)S(1)} %stack.43.spots, bf16[512,576]{1,0:T(8,128)(2,1)S(1)} %reshape.101.refs_5_.queries, s32[1,640]{1,0:T(1,128)S(1)} %multiply_add_fusion.refs_6_.base, ...), custom_call_target="tpu_custom_call" | custom-call | flops 377487360 | bytes 499712 | tf_op jit(solution)/shard_map/attend_near/pallas_call | solution.py:35
  137.3 1.0 copy-done.4
  138.3 0.7 copy-done.9
  139.0 1.1 copy-done.1
  140.1 2.2 %second.1 = bf16[8,32,128]{2,1,0:T(8,128)(2,1)} custom-call(bf16[32,32,384]{2,1,0:T(8,128)(2,1)} %all-to-all-done.3.hidden, bf16[2,1536,80]{2,1,0:T(8,128)(2,1)S(1)} %copy-done.1, f32[8,128]{1,0:T(8,128)S(1)} %get-tuple-element.45.refs_0_), custom_call_target="tpu_custom_call" | custom-call | flops 134217728 | bytes 2097152 | tf_op jit(solution)/shard_map/second/pallas_call | solution.py:35
  142.3 5.5 %all-to-all-start.4 = ((bf16[8,32,128]{2,1,0:T(8,128)(2,1)}), bf16[8,32,128]{2,1,0:T(8,128)(2,1)S(1)}, u32[]{:S(2)}, u32[]{:S(2)}) async-start(bf16[8,32,128]{2,1,0:T(8,128)(2,1)} %second.1), calls=%async_computation.4 | async-start | bytes 131072 | tf_op jit(solution)/shard_map/all_to_all | solution.py:201
  147.9 0.1 pad_add_fusion.spots
  147.9 0.9 copy-done.10
  148.9 3.8 %attend_far.1 = bf16[512,512]{1,0:T(8,128)(2,1)S(1)} custom-call(s32[3]{0:T(128)S(1)} %pad_add_fusion.spots, bf16[512,576]{1,0:T(8,128)(2,1)S(1)} %reshape.101.refs_5_.queries, s32[1,640]{1,0:T(1,128)S(1)} %multiply_add_fusion.refs_6_.base, bf16[576,640]{1,0:T(8,128)(2,1)S(1)} %get-tuple-element.35.refs_0_, bf16[576,640]{1,0:T(8,128)(2,1)} %collective-permute-done.9.refs_1_, ...), custom_call_target="tpu_custom_call" | custom-call | flops 188743680 | bytes 315392 | tf_op jit(solution)/shard_map/attend_far/pallas_call | solution.py:35
  152.7 1.2 reshape.105
  153.9 1.0 combine.1
  (41 shorter events, 0.1 us)
Async XLA Ops:
  0.6 12.9 %copy-start = (bf16[80,576]{1,0:T(8,128)(2,1)S(1)}, bf16[80,576]{1,0:T(8,128)(2,1)}, u32[]{:S(2)}) copy-start(bf16[80,576]{1,0:T(8,128)(2,1)} %param.10) | copy-start | bytes 276484
  0.6 0.7 copy-start.15
  1.4 0.7 copy-start.17
  3.1 24.0 %all-to-all-start = ((bf16[32,32,128]{2,1,0:T(8,128)(2,1)}), bf16[32,32,128]{2,1,0:T(8,128)(2,1)S(1)}, u32[]{:S(2)}, u32[]{:S(2)}) async-start(bf16[32,32,128]{2,1,0:T(8,128)(2,1)} %dispatch.1), calls=%async_computation | async-start | bytes 524288 | tf_op jit(solution)/shard_map/all_to_all | solution.py:201
  13.5 9.1 %collective-permute-start = (bf16[40,576]{1,0:T(8,128)(2,1)S(1)}, bf16[40,576]{1,0:T(8,128)(2,1)S(1)}, u32[]{:S(2)}, u32[]{:S(2)}) collective-permute-start(bf16[40,576]{1,0:T(8,128)(2,1)S(1)} %constant_dynamic-slice_fusion), channel_id=1, source_target_pairs={{0,32},{32,0},{1,33},{33,1},{2,34},{34,2},{3,35},{35,3},{4,36},{36... | collective-permute-start | bytes 138248 | tf_op jit(solution)/shard_map/ppermute | solution.py:206
  28.1 6.5 %copy-start.7 = (bf16[2,80,1536]{2,1,0:T(8,128)(2,1)S(1)}, bf16[2,80,1536]{2,1,0:T(8,128)(2,1)}, u32[]{:S(2)}) copy-start(bf16[2,80,1536]{2,1,0:T(8,128)(2,1)} %gate.1) | copy-start | bytes 1474564
  28.1 6.5 %copy-start.8 = (bf16[2,80,1536]{2,1,0:T(8,128)(2,1)S(1)}, bf16[2,80,1536]{2,1,0:T(8,128)(2,1)}, u32[]{:S(2)}) copy-start(bf16[2,80,1536]{2,1,0:T(8,128)(2,1)} %up.1) | copy-start | bytes 1474564
  28.1 30.8 %all-to-all-start.1 = ((bf16[8,80,576]{2,1,0:T(8,128)(2,1)}), bf16[8,80,576]{2,1,0:T(8,128)(2,1)S(1)}, u32[]{:S(2)}, u32[]{:S(2)}) async-start(bf16[8,80,576]{2,1,0:T(8,128)(2,1)} %pair.1), calls=%async_computation.1 | async-start | bytes 1638400 | tf_op jit(solution)/shard_map/all_to_all | solution.py:201
  35.3 11.4 %collective-permute-start.4 = (bf16[2,80,768]{2,1,0:T(8,128)(2,1)}, bf16[2,80,768]{2,1,0:T(8,128)(2,1)S(1)}, u32[]{:S(2)}, u32[]{:S(2)}) collective-permute-start(bf16[2,80,768]{2,1,0:T(8,128)(2,1)} %get-tuple-element.25), channel_id=1, source_target_pairs={{0,8},{8,16},{16,24},{24,0},{1,9},{9,17},{17,25},{25,1},{2,10},{10... | collective-permute-start | bytes 737288 | tf_op jit(solution)/shard_map/ppermute | solution.py:206
  37.6 12.7 %collective-permute-start.5 = (bf16[2,80,768]{2,1,0:T(8,128)(2,1)S(1)}, bf16[2,80,768]{2,1,0:T(8,128)(2,1)S(1)}, u32[]{:S(2)}, u32[]{:S(2)}) collective-permute-start(bf16[2,80,768]{2,1,0:T(8,128)(2,1)S(1)} %get-tuple-element.26), channel_id=1, source_target_pairs={{0,16},{8,24},{16,0},{24,8},{1,17},{9,25},{17,1},{25,9},{2,18},{10... | collective-permute-start | bytes 737288 | tf_op jit(solution)/shard_map/ppermute | solution.py:206
  41.5 11.6 %collective-permute-start.6 = (bf16[2,80,768]{2,1,0:T(8,128)(2,1)S(1)}, bf16[2,80,768]{2,1,0:T(8,128)(2,1)S(1)}, u32[]{:S(2)}, u32[]{:S(2)}) collective-permute-start(bf16[2,80,768]{2,1,0:T(8,128)(2,1)S(1)} %get-tuple-element.27), channel_id=1, source_target_pairs={{0,24},{8,0},{16,8},{24,16},{1,25},{9,1},{17,9},{25,17},{2,26},{10... | collective-permute-start | bytes 737288 | tf_op jit(solution)/shard_map/ppermute | solution.py:206
  60.2 18.5 %all-to-all-start.2 = ((bf16[8,32,768]{2,1,0:T(8,128)(2,1)}), bf16[8,32,768]{2,1,0:T(8,128)(2,1)S(1)}, u32[]{:S(2)}, u32[]{:S(2)}) async-start(bf16[8,32,768]{2,1,0:T(8,128)(2,1)} %bitcast.6), calls=%async_computation.2 | async-start | bytes 786432 | tf_op jit(solution)/shard_map/all_to_all | solution.py:201
  64.8 19.6 %collective-permute-start.8 = (bf16[576,640]{1,0:T(8,128)(2,1)}, bf16[576,640]{1,0:T(8,128)(2,1)}, u32[]{:S(2)}, u32[]{:S(2)}) collective-permute-start(bf16[576,640]{1,0:T(8,128)(2,1)} %bitcast.4.refs_0_), channel_id=1, source_target_pairs={{0,1},{1,0},{2,3},{3,2},{4,5},{5,4},{6,7},{7,6},{8,9},{9,8},{10,11... | collective-permute-start | bytes 2211848 | tf_op jit(solution)/shard_map/ppermute | solution.py:206
  67.2 21.7 %collective-permute-start.1 = (bf16[576,640]{1,0:T(8,128)(2,1)}, bf16[576,640]{1,0:T(8,128)(2,1)S(1)}, u32[]{:S(2)}, u32[]{:S(2)}) collective-permute-start(bf16[576,640]{1,0:T(8,128)(2,1)} %bitcast.4.refs_0_), channel_id=1, source_target_pairs={{0,8},{8,16},{16,24},{24,0},{1,9},{9,17},{17,25},{25,1},{2,10},{10... | collective-permute-start | bytes 2211848 | tf_op jit(solution)/shard_map/ppermute | solution.py:206
  69.5 20.7 %collective-permute-start.2 = (bf16[576,640]{1,0:T(8,128)(2,1)}, bf16[576,640]{1,0:T(8,128)(2,1)S(1)}, u32[]{:S(2)}, u32[]{:S(2)}) collective-permute-start(bf16[576,640]{1,0:T(8,128)(2,1)} %bitcast.4.refs_0_), channel_id=1, source_target_pairs={{0,24},{8,0},{16,8},{24,16},{1,25},{9,1},{17,9},{25,17},{2,26},{10... | collective-permute-start | bytes 2211848 | tf_op jit(solution)/shard_map/ppermute | solution.py:206
  73.7 30.4 %collective-permute-start.3 = (bf16[576,640]{1,0:T(8,128)(2,1)}, bf16[576,640]{1,0:T(8,128)(2,1)S(1)}, u32[]{:S(2)}, u32[]{:S(2)}) collective-permute-start(bf16[576,640]{1,0:T(8,128)(2,1)} %bitcast.4.refs_0_), channel_id=1, source_target_pairs={{0,16},{8,24},{16,0},{24,8},{1,17},{9,25},{17,1},{25,9},{2,18},{10... | collective-permute-start | bytes 2211848 | tf_op jit(solution)/shard_map/ppermute | solution.py:206
  78.7 25.3 %collective-permute-start.7 = (bf16[32,768]{1,0:T(8,128)(2,1)S(1)}, bf16[32,768]{1,0:T(8,128)(2,1)S(1)}, u32[]{:S(2)}, u32[]{:S(2)}) collective-permute-start(bf16[32,768]{1,0:T(8,128)(2,1)S(1)} %get-tuple-element.28), channel_id=1, source_target_pairs={{0,32},{32,0},{1,33},{33,1},{2,34},{34,2},{3,35},{35,3},{4,36},{36... | collective-permute-start | bytes 147464 | tf_op jit(solution)/shard_map/ppermute | solution.py:206
  88.3 15.7 %copy-start.2 = (f32[512,512]{1,0:T(8,128)}, f32[512,512]{1,0:T(8,128)S(1)}, u32[]{:S(2)}) copy-start(f32[512,512]{1,0:T(8,128)S(1)} %get-tuple-element.40.refs_6_) | copy-start | bytes 3145732
  88.4 15.7 %copy-start.11 = (f32[512,128]{1,0:T(8,128)}, f32[512,128]{1,0:T(8,128)S(1)}, u32[]{:S(2)}) copy-start(f32[512,128]{1,0:T(8,128)S(1)} %get-tuple-element.38.refs_4_) | copy-start | bytes 786436
  88.4 15.7 %copy-start.13 = (f32[512,128]{1,0:T(8,128)}, f32[512,128]{1,0:T(8,128)S(1)}, u32[]{:S(2)}) copy-start(f32[512,128]{1,0:T(8,128)S(1)} %get-tuple-element.39.refs_5_) | copy-start | bytes 786436
  104.2 0.9 copy-start.6
  105.1 33.9 %all-to-all-start.3 = ((bf16[32,32,384]{2,1,0:T(8,128)(2,1)}), bf16[32,32,384]{2,1,0:T(8,128)(2,1)}, u32[]{:S(2)}, u32[]{:S(2)}) async-start(bf16[32,32,384]{2,1,0:T(8,128)(2,1)} %copy-done.6), calls=%async_computation.3 | async-start | bytes 1572864 | tf_op jit(solution)/shard_map/all_to_all | solution.py:201
  116.8 10.9 %collective-permute-start.10 = (bf16[576,640]{1,0:T(8,128)(2,1)S(1)}, bf16[576,640]{1,0:T(8,128)(2,1)}, u32[]{:S(2)}, u32[]{:S(2)}) collective-permute-start(bf16[576,640]{1,0:T(8,128)(2,1)S(1)} %get-tuple-element.36.refs_0_), channel_id=1, source_target_pairs={{0,1},{1,0},{2,3},{3,2},{4,5},{5,4},{6,7},{7,6},{8,9},{9,8},{10,11... | collective-permute-start | bytes 2211848 | tf_op jit(solution)/shard_map/ppermute | solution.py:206
  120.1 7.6 %collective-permute-start.11 = (bf16[576,640]{1,0:T(8,128)(2,1)S(1)}, bf16[576,640]{1,0:T(8,128)(2,1)}, u32[]{:S(2)}, u32[]{:S(2)}) collective-permute-start(bf16[576,640]{1,0:T(8,128)(2,1)S(1)} %get-tuple-element.37.refs_2_), channel_id=1, source_target_pairs={{0,1},{1,0},{2,3},{3,2},{4,5},{5,4},{6,7},{7,6},{8,9},{9,8},{10,11... | collective-permute-start | bytes 2211848 | tf_op jit(solution)/shard_map/ppermute | solution.py:206
  122.0 25.9 %collective-permute-start.9 = (bf16[576,640]{1,0:T(8,128)(2,1)S(1)}, bf16[576,640]{1,0:T(8,128)(2,1)}, u32[]{:S(2)}, u32[]{:S(2)}) collective-permute-start(bf16[576,640]{1,0:T(8,128)(2,1)S(1)} %get-tuple-element.35.refs_0_), channel_id=1, source_target_pairs={{0,1},{1,0},{2,3},{3,2},{4,5},{5,4},{6,7},{7,6},{8,9},{9,8},{10,11... | collective-permute-start | bytes 2211848 | tf_op jit(solution)/shard_map/ppermute | solution.py:206
  124.5 0.7 copy-start.16
  125.2 2.2 %copy-start.18 = (f32[32,6]{0,1:T(8,128)S(1)}, f32[32,6]{0,1:T(8,128)}, u32[]{:S(2)}) copy-start(f32[32,6]{0,1:T(8,128)} %param.14) | copy-start | bytes 2308
  127.6 1.2 copy-start.3
  128.9 0.9 copy-start.12
  129.8 0.9 copy-start.14
  137.3 1.0 copy-start.4
  138.3 0.7 copy-start.9
  139.0 1.1 copy-start.1
  140.1 7.8 %copy-start.5 = (f32[512,512]{1,0:T(8,128)S(1)}, f32[512,512]{1,0:T(8,128)}, u32[]{:S(2)}) copy-start(f32[512,512]{1,0:T(8,128)} %copy-done.4) | copy-start | bytes 3145732
  142.3 11.6 %all-to-all-start.4 = ((bf16[8,32,128]{2,1,0:T(8,128)(2,1)}), bf16[8,32,128]{2,1,0:T(8,128)(2,1)S(1)}, u32[]{:S(2)}, u32[]{:S(2)}) async-start(bf16[8,32,128]{2,1,0:T(8,128)(2,1)} %second.1), calls=%async_computation.4 | async-start | bytes 131072 | tf_op jit(solution)/shard_map/all_to_all | solution.py:201
  147.9 1.0 copy-start.10

commit v10 on v7

--- a/solution.py
+++ b/solution.py
@@ -121,8 +121,8 @@
         out[i] = rows[...]
 
 
-def first_body(order, spots, after, arrived, *refs):
-    weights, out = refs[:-1], refs[-1]
+def first_body(order, spots, arrived, *refs):
+    weights, out = refs[: len(order)], refs[-1]
     held, feats = weights[0].shape[:2]
     owners = arrived.shape[0] // len(weights)
     for e in range(held):
@@ -228,7 +228,7 @@
         pair_body, "pair", shaped((nz,) + paired.shape, BF16), [VMEM, AFTER], (paired, arrived), 2**10, 2**20
     )
     column = exchange(paired, "z")
-    column = column.reshape(nz * nh * own, WIDE).T
+    raw = column.reshape(nz * nh * own, WIDE)
 
     cut = kernel(
         cut_body, "cut", [shaped((held, feats, 2 * units), BF16)] * nx,
@@ -236,10 +236,16 @@
     )
     weights = [cut[0]] + [shift(cut[j], "x", j) for j in range(1, nx)]
     order = [0] + [nx - j for j in range(1, nx)]
+    at_z = lax.broadcasted_iota(I32, (nz, nh, own), 0)
+    at_h = (lax.broadcasted_iota(I32, (nz, nh, own), 1) + h_at) % nh
+    base = ((at_z * nh + at_h) * nx * latents.shape[0] + lax.broadcasted_iota(I32, (nz, nh, own), 2)).reshape(1, -1)
+    query_rows = queries.reshape(queries.shape[0] * H, WIDE)
+
     parts = kernel(
         functools.partial(first_body, order), "first", shaped((held * owners * CAP, 2 * units), BF16),
-        [SMEM, AFTER] + [VMEM] * (1 + nx), (where_x, column, arrived, *weights), 2**28, 2**21,
-    )
+        [SMEM] + [VMEM] * (1 + nx) + [AFTER] * 3, (where_x, arrived, *weights, raw, query_rows, base), 2**28, 2**21,
+    )
+    column = raw.T
     others = [shift(column, "x", 1), shift(column, "x", -1), shift(column, "x", 2)]
     parts = exchange(parts.reshape(nz, -1, 2 * units), "z")
     rows = parts.shape[1]
@@ -264,11 +270,6 @@
     )
 
     sources = [x_at, x_at + nx - 1, x_at + 1, x_at + 2]
-    at_z = lax.broadcasted_iota(I32, (nz, nh, own), 0)
-    at_h = (lax.broadcasted_iota(I32, (nz, nh, own), 1) + h_at) % nh
-    base = ((at_z * nh + at_h) * nx * latents.shape[0] + lax.broadcasted_iota(I32, (nz, nh, own), 2)).reshape(1, -1)
-    query_rows = queries.reshape(queries.shape[0] * H, WIDE)
-
     spots = []
     for source in sources:
         first = (source % nx) * latents.shape[0]

time: 150 us -> 151 us (level)
  local copies, waits for them, and re-layouts: 9.18 us -> 12.4 us
  waiting for transfers between devices: 46 us -> 43.9 us
    all_to_all x5, waiting for transfers between devices: 29.4 us -> 25.2 us  [exchange(): return lax.all_to_all(array, axes, split_axis=0, concat_axis=0, tiled=False)]
    unnamed x23 -> x27, local copies, waits for them, and re-layouts: 4.24 us -> 7.72 us
    ppermute x12, waiting for transfers between devices: 16.6 us -> 18.7 us  [shift(): lax.ppermute(array, axis, [(i, (i + by) % size) for i in range(size)])]
  transfers between devices with their start and end apart: 17 -> 17, of which waited for: 7 -> 8; matrix products, arithmetic and copies ran while one was open for 4% -> 4% of each run, Pallas kernels for 10% -> 10%
where the time goes in v10:
time: 151 us; the launch traced here: 150 us
  starting transfers between devices  72.2 us (48%)
  waiting for transfers between devices  43.9 us (29%)
  Pallas kernels  19.3 us (13%)
  local copies, waits for them, and re-layouts  12.4 us (8%)
  between operations  1.67 us (1%)
    ppermute x12, starting transfers between devices, shift(): lax.ppermute(array, axis, [(i, (i + by) % size) for i in range(size)])  40.4 us
    all_to_all x5, starting transfers between devices, exchange(): return lax.all_to_all(array, axes, split_axis=0, concat_axis=0, tiled=False)  31.8 us
    all_to_all x5, waiting for transfers between devices, exchange(): return lax.all_to_all(array, axes, split_axis=0, concat_axis=0, tiled=False)  25.2 us
    pallas_call x10, Pallas kernels, kernel(): pl.pallas_call(body, out_shape=out_shape, in_specs=specs, out_specs=jax.t...  19.3 us
    ppermute x12, waiting for transfers between devices, shift(): lax.ppermute(array, axis, [(i, (i + by) % size) for i in range(size)])  18.7 us
    unnamed x27, local copies, waits for them, and re-layouts  7.72 us
  transfers between devices with their start and end apart: 17, of which 8 were waited for; matrix products, arithmetic and copies ran while one was open for 4% of the time, Pallas kernels for 10%

profile of v10, /device:TPU:1, one launch (start us, length us, event | category | flops | bytes accessed | tf_op | source)
XLA Modules:
  0.0 149.6 jit_solution(9988867414821302342)
XLA Ops:
  0.6 0.0 copy-start
  0.6 0.0 copy-start.8
  0.7 0.7 copy-done.8
  1.4 0.7 copy-done.10
  2.1 1.0 dispatch.1
  3.1 10.4 %all-to-all-start = ((bf16[32,32,128]{2,1,0:T(8,128)(2,1)}), bf16[32,32,128]{2,1,0:T(8,128)(2,1)S(1)}, u32[]{:S(2)}, u32[]{:S(2)}) async-start(bf16[32,32,128]{2,1,0:T(8,128)(2,1)} %dispatch.1), calls=%async_computation | async-start | bytes 524288 | tf_op jit(solution)/shard_map/all_to_all | solution.py:200
  13.5 3.4 %collective-permute-start = (bf16[40,576]{1,0:T(8,128)(2,1)S(1)}, bf16[40,576]{1,0:T(8,128)(2,1)S(1)}, u32[]{:S(2)}, u32[]{:S(2)}) collective-permute-start(bf16[40,576]{1,0:T(8,128)(2,1)S(1)} %constant_dynamic-slice_fusion), channel_id=1, source_target_pairs={{0,32},{32,0},{1,33},{33,1},{2,34},{34,2},{3,35},{35,3},{4,36},{36... | collective-permute-start | bytes 138248 | tf_op jit(solution)/shard_map/ppermute | solution.py:205
  16.9 5.7 %collective-permute-done = bf16[40,576]{1,0:T(8,128)(2,1)S(1)} collective-permute-done((bf16[40,576]{1,0:T(8,128)(2,1)S(1)}, bf16[40,576]{1,0:T(8,128)(2,1)S(1)}, u32[]{:S(2)}, u32[]{:S(2)}) %collective-permute-start) | collective-permute-done | bytes 46112 | tf_op jit(solution)/shard_map/ppermute | solution.py:205
  22.6 4.5 %all-to-all-done.after.arrived = bf16[32,32,128]{2,1,0:T(8,128)(2,1)S(1)} async-done(((bf16[32,32,128]{2,1,0:T(8,128)(2,1)}), bf16[32,32,128]{2,1,0:T(8,128)(2,1)S(1)}, u32[]{:S(2)}, u32[]{:S(2)}) %all-to-all-start) | async-done | bytes 262176 | tf_op jit(solution)/shard_map/all_to_all | solution.py:200
  27.1 1.0 pair.1
  28.1 6.5 %all-to-all-start.1 = ((bf16[8,80,576]{2,1,0:T(8,128)(2,1)}), bf16[8,80,576]{2,1,0:T(8,128)(2,1)S(1)}, u32[]{:S(2)}, u32[]{:S(2)}) async-start(bf16[8,80,576]{2,1,0:T(8,128)(2,1)} %pair.1), calls=%async_computation.1 | async-start | bytes 1638400 | tf_op jit(solution)/shard_map/all_to_all | solution.py:200
  34.5 0.8 cut.1
  35.3 2.3 %collective-permute-start.2 = (bf16[2,80,768]{2,1,0:T(8,128)(2,1)}, bf16[2,80,768]{2,1,0:T(8,128)(2,1)S(1)}, u32[]{:S(2)}, u32[]{:S(2)}) collective-permute-start(bf16[2,80,768]{2,1,0:T(8,128)(2,1)} %get-tuple-element.17), channel_id=1, source_target_pairs={{0,8},{8,16},{16,24},{24,0},{1,9},{9,17},{17,25},{25,1},{2,10},{10... | collective-permute-start | bytes 737288 | tf_op jit(solution)/shard_map/ppermute | solution.py:205
  37.6 3.9 %collective-permute-start.3 = (bf16[2,80,768]{2,1,0:T(8,128)(2,1)S(1)}, bf16[2,80,768]{2,1,0:T(8,128)(2,1)S(1)}, u32[]{:S(2)}, u32[]{:S(2)}) collective-permute-start(bf16[2,80,768]{2,1,0:T(8,128)(2,1)S(1)} %get-tuple-element.18), channel_id=1, source_target_pairs={{0,16},{8,24},{16,0},{24,8},{1,17},{9,25},{17,1},{25,9},{2,18},{10... | collective-permute-start | bytes 737288 | tf_op jit(solution)/shard_map/ppermute | solution.py:205
  41.5 3.0 %collective-permute-start.4 = (bf16[2,80,768]{2,1,0:T(8,128)(2,1)S(1)}, bf16[2,80,768]{2,1,0:T(8,128)(2,1)S(1)}, u32[]{:S(2)}, u32[]{:S(2)}) collective-permute-start(bf16[2,80,768]{2,1,0:T(8,128)(2,1)S(1)} %get-tuple-element.19), channel_id=1, source_target_pairs={{0,24},{8,0},{16,8},{24,16},{1,25},{9,1},{17,9},{25,17},{2,26},{10... | collective-permute-start | bytes 737288 | tf_op jit(solution)/shard_map/ppermute | solution.py:205
  44.5 0.1 iota.29
  44.6 0.1 iota.30
  44.7 0.1 iota.26
  44.7 0.1 iota.27
  44.8 0.1 iota.32
  44.9 1.7 %reshape.101.refs_5_.queries = bf16[512,576]{1,0:T(8,128)(2,1)S(1)} reshape(bf16[4,73728]{1,0:T(4,128)(2,1)} %param.9) | data formatting | bytes 1179648 | tf_op jit(solution)/shard_map/reshape | solution.py:242
  46.7 12.2 %all-to-all-done.1 = bf16[8,80,576]{2,1,0:T(8,128)(2,1)S(1)} async-done(((bf16[8,80,576]{2,1,0:T(8,128)(2,1)}), bf16[8,80,576]{2,1,0:T(8,128)(2,1)S(1)}, u32[]{:S(2)}, u32[]{:S(2)}) %all-to-all-start.1) | async-done | bytes 737312 | tf_op jit(solution)/shard_map/all_to_all | solution.py:200
  58.9 1.2 copy.19
  60.1 0.0 collective-permute-done.2.refs_1_
  60.1 0.0 collective-permute-done.3.refs_2_
  60.1 0.0 collective-permute-done.4.refs_3_
  60.1 1.3 first.1
  61.4 3.5 %all-to-all-start.2 = ((bf16[8,32,768]{2,1,0:T(8,128)(2,1)}), bf16[8,32,768]{2,1,0:T(8,128)(2,1)S(1)}, u32[]{:S(2)}, u32[]{:S(2)}) async-start(bf16[8,32,768]{2,1,0:T(8,128)(2,1)} %bitcast.6), calls=%async_computation.2 | async-start | bytes 786432 | tf_op jit(solution)/shard_map/all_to_all | solution.py:200
  64.8 2.3 %collective-permute-start.6 = (bf16[576,640]{1,0:T(8,128)(2,1)}, bf16[576,640]{1,0:T(8,128)(2,1)S(1)}, u32[]{:S(2)}, u32[]{:S(2)}) collective-permute-start(bf16[576,640]{1,0:T(8,128)(2,1)} %bitcast.4.refs_0_), channel_id=1, source_target_pairs={{0,8},{8,16},{16,24},{24,0},{1,9},{9,17},{17,25},{25,1},{2,10},{10... | collective-permute-start | bytes 2211848 | tf_op jit(solution)/shard_map/ppermute | solution.py:205
  67.1 4.2 %collective-permute-start.7 = (bf16[576,640]{1,0:T(8,128)(2,1)}, bf16[576,640]{1,0:T(8,128)(2,1)S(1)}, u32[]{:S(2)}, u32[]{:S(2)}) collective-permute-start(bf16[576,640]{1,0:T(8,128)(2,1)} %bitcast.4.refs_0_), channel_id=1, source_target_pairs={{0,24},{8,0},{16,8},{24,16},{1,25},{9,1},{17,9},{25,17},{2,26},{10... | collective-permute-start | bytes 2211848 | tf_op jit(solution)/shard_map/ppermute | solution.py:205
  71.4 8.6 %all-to-all-done.2.parts = bf16[8,32,768]{2,1,0:T(8,128)(2,1)S(1)} async-done(((bf16[8,32,768]{2,1,0:T(8,128)(2,1)}), bf16[8,32,768]{2,1,0:T(8,128)(2,1)S(1)}, u32[]{:S(2)}, u32[]{:S(2)}) %all-to-all-start.2) | async-done | bytes 393248 | tf_op jit(solution)/shard_map/all_to_all | solution.py:200
  79.9 0.1 add.126
  80.0 5.5 %collective-permute-start.5 = (bf16[32,768]{1,0:T(8,128)(2,1)S(1)}, bf16[32,768]{1,0:T(8,128)(2,1)S(1)}, u32[]{:S(2)}, u32[]{:S(2)}) collective-permute-start(bf16[32,768]{1,0:T(8,128)(2,1)S(1)} %get-tuple-element.21), channel_id=1, source_target_pairs={{0,32},{32,0},{1,33},{33,1},{2,34},{34,2},{3,35},{35,3},{4,36},{36... | collective-permute-start | bytes 147464 | tf_op jit(solution)/shard_map/ppermute | solution.py:205
  85.5 0.3 collective-permute-done.6.refs_0_
  85.7 1.0 collective-permute-done.7.refs_1_
  86.7 2.1 %collective-permute-done.5.other = bf16[32,768]{1,0:T(8,128)(2,1)S(1)} collective-permute-done((bf16[32,768]{1,0:T(8,128)(2,1)S(1)}, bf16[32,768]{1,0:T(8,128)(2,1)S(1)}, u32[]{:S(2)}, u32[]{:S(2)}) %collective-permute-start.5) | collective-permute-done | bytes 49184 | tf_op jit(solution)/shard_map/ppermute | solution.py:205
  88.8 0.1 hidden.1
  88.9 0.9 copy-done.3
  89.8 7.6 %all-to-all-start.3 = ((bf16[32,32,384]{2,1,0:T(8,128)(2,1)}), bf16[32,32,384]{2,1,0:T(8,128)(2,1)S(1)}, u32[]{:S(2)}, u32[]{:S(2)}) async-start(bf16[32,32,384]{2,1,0:T(8,128)(2,1)} %copy-done.3), calls=%async_computation.3 | async-start | bytes 1572864 | tf_op jit(solution)/shard_map/all_to_all | solution.py:200
  97.4 4.1 %collective-permute-start.8 = (bf16[576,640]{1,0:T(8,128)(2,1)}, bf16[576,640]{1,0:T(8,128)(2,1)}, u32[]{:S(2)}, u32[]{:S(2)}) collective-permute-start(bf16[576,640]{1,0:T(8,128)(2,1)} %bitcast.4.refs_0_), channel_id=1, source_target_pairs={{0,1},{1,0},{2,3},{3,2},{4,5},{5,4},{6,7},{7,6},{8,9},{9,8},{10,11... | collective-permute-start | bytes 2211848 | tf_op jit(solution)/shard_map/ppermute | solution.py:205
  101.5 1.9 %collective-permute-start.10 = (bf16[576,640]{1,0:T(8,128)(2,1)S(1)}, bf16[576,640]{1,0:T(8,128)(2,1)}, u32[]{:S(2)}, u32[]{:S(2)}) collective-permute-start(bf16[576,640]{1,0:T(8,128)(2,1)S(1)} %get-tuple-element.24.refs_4_), channel_id=1, source_target_pairs={{0,1},{1,0},{2,3},{3,2},{4,5},{5,4},{6,7},{7,6},{8,9},{9,8},{10,11... | collective-permute-start | bytes 2211848 | tf_op jit(solution)/shard_map/ppermute | solution.py:205
  103.4 2.4 %collective-permute-start.9 = (bf16[576,640]{1,0:T(8,128)(2,1)S(1)}, bf16[576,640]{1,0:T(8,128)(2,1)}, u32[]{:S(2)}, u32[]{:S(2)}) collective-permute-start(bf16[576,640]{1,0:T(8,128)(2,1)S(1)} %get-tuple-element.23.refs_2_), channel_id=1, source_target_pairs={{0,1},{1,0},{2,3},{3,2},{4,5},{5,4},{6,7},{7,6},{8,9},{9,8},{10,11... | collective-permute-start | bytes 2211848 | tf_op jit(solution)/shard_map/ppermute | solution.py:205
  105.9 4.9 %collective-permute-start.1 = (bf16[576,640]{1,0:T(8,128)(2,1)}, bf16[576,640]{1,0:T(8,128)(2,1)}, u32[]{:S(2)}, u32[]{:S(2)}) collective-permute-start(bf16[576,640]{1,0:T(8,128)(2,1)} %bitcast.4.refs_0_), channel_id=1, source_target_pairs={{0,16},{8,24},{16,0},{24,8},{1,17},{9,25},{17,1},{25,9},{2,18},{10... | collective-permute-start | bytes 2211848 | tf_op jit(solution)/shard_map/ppermute | solution.py:205
  111.5 0.1 stack.39.spots
  111.6 0.0 collective-permute-done.8.refs_1_
  111.6 9.3 %attend_near.1 = (f32[512,128]{1,0:T(8,128)S(1)}, f32[512,128]{1,0:T(8,128)S(1)}, f32[512,512]{1,0:T(8,128)S(1)}, f32[8,128]{1,0:T(8,128)S(1)}) custom-call(s32[7]{0:T(128)S(1)} %stack.39.spots, bf16[512,576]{1,0:T(8,128)(2,1)S(1)} %reshape.101.refs_5_.queries, s32[1,640]{1,0:T(1,128)S(1)} %multiply_add_fusion.refs_6_.base, ...), custom_call_target="tpu_custom_call" | custom-call | flops 566231040 | bytes 684032 | tf_op jit(solution)/shard_map/attend_near/pallas_call | solution.py:35
  120.9 1.0 copy-done.1
  121.9 9.7 %collective-permute-done.1.refs_0_ = bf16[576,640]{1,0:T(8,128)(2,1)} collective-permute-done((bf16[576,640]{1,0:T(8,128)(2,1)}, bf16[576,640]{1,0:T(8,128)(2,1)}, u32[]{:S(2)}, u32[]{:S(2)}) %collective-permute-start.1) | collective-permute-done | bytes 737312 | tf_op jit(solution)/shard_map/ppermute | solution.py:205
  131.6 2.5 %collective-permute-start.11 = (bf16[576,640]{1,0:T(8,128)(2,1)}, bf16[576,640]{1,0:T(8,128)(2,1)S(1)}, u32[]{:S(2)}, u32[]{:S(2)}) collective-permute-start(bf16[576,640]{1,0:T(8,128)(2,1)} %hold.3.refs_0_), channel_id=1, source_target_pairs={{0,1},{1,0},{2,3},{3,2},{4,5},{5,4},{6,7},{7,6},{8,9},{9,8},{10,11... | collective-permute-start | bytes 2211848 | tf_op jit(solution)/shard_map/ppermute | solution.py:205
  134.1 0.0 copy-start.9
  134.2 0.7 copy-done.9
  134.8 0.1 copy.21.routes
  134.9 1.4 copy.20.down
  136.3 0.1 copy.22.gates
  136.4 0.0 all-to-all-done.3.hidden
  136.4 1.0 second.1
  137.4 3.9 %all-to-all-start.4 = ((bf16[8,32,128]{2,1,0:T(8,128)(2,1)}), bf16[8,32,128]{2,1,0:T(8,128)(2,1)S(1)}, u32[]{:S(2)}, u32[]{:S(2)}) async-start(bf16[8,32,128]{2,1,0:T(8,128)(2,1)} %second.1), calls=%async_computation.4 | async-start | bytes 131072 | tf_op jit(solution)/shard_map/all_to_all | solution.py:200
  141.3 0.1 pad_add_fusion.spots
  141.4 0.0 collective-permute-done.11.refs_1_
  141.4 1.2 copy-done.2
  142.6 0.9 copy-done.7
  143.6 3.8 %attend_far.1 = bf16[512,512]{1,0:T(8,128)(2,1)S(1)} custom-call(s32[3]{0:T(128)S(1)} %pad_add_fusion.spots, bf16[512,576]{1,0:T(8,128)(2,1)S(1)} %reshape.101.refs_5_.queries, s32[1,640]{1,0:T(1,128)S(1)} %multiply_add_fusion.refs_6_.base, bf16[576,640]{1,0:T(8,128)(2,1)} %hold.3.refs_0_, bf16[576,640]{1,0:T(8,128)(2,1)S(1)} %collective-permute-done.11.refs_1_, ...), custom_call_target="tpu_custom_call" | custom-call | flops 188743680 | bytes 315392 | tf_op jit(solution)/shard_map/attend_far/pallas_call | solution.py:35
  147.4 1.2 reshape.105
  148.6 1.0 combine.1
  (25 shorter events, 0.1 us)
Async XLA Ops:
  0.6 12.9 %copy-start = (bf16[80,576]{1,0:T(8,128)(2,1)S(1)}, bf16[80,576]{1,0:T(8,128)(2,1)}, u32[]{:S(2)}) copy-start(bf16[80,576]{1,0:T(8,128)(2,1)} %param.10) | copy-start | bytes 276484
  0.6 0.7 copy-start.8
  1.4 0.7 copy-start.10
  3.1 24.0 %all-to-all-start = ((bf16[32,32,128]{2,1,0:T(8,128)(2,1)}), bf16[32,32,128]{2,1,0:T(8,128)(2,1)S(1)}, u32[]{:S(2)}, u32[]{:S(2)}) async-start(bf16[32,32,128]{2,1,0:T(8,128)(2,1)} %dispatch.1), calls=%async_computation | async-start | bytes 524288 | tf_op jit(solution)/shard_map/all_to_all | solution.py:200
  13.5 9.1 %collective-permute-start = (bf16[40,576]{1,0:T(8,128)(2,1)S(1)}, bf16[40,576]{1,0:T(8,128)(2,1)S(1)}, u32[]{:S(2)}, u32[]{:S(2)}) collective-permute-start(bf16[40,576]{1,0:T(8,128)(2,1)S(1)} %constant_dynamic-slice_fusion), channel_id=1, source_target_pairs={{0,32},{32,0},{1,33},{33,1},{2,34},{34,2},{3,35},{35,3},{4,36},{36... | collective-permute-start | bytes 138248 | tf_op jit(solution)/shard_map/ppermute | solution.py:205
  28.0 6.5 %copy-start.4 = (bf16[2,80,1536]{2,1,0:T(8,128)(2,1)S(1)}, bf16[2,80,1536]{2,1,0:T(8,128)(2,1)}, u32[]{:S(2)}) copy-start(bf16[2,80,1536]{2,1,0:T(8,128)(2,1)} %gate.1) | copy-start | bytes 1474564
  28.1 6.5 %copy-start.5 = (bf16[2,80,1536]{2,1,0:T(8,128)(2,1)S(1)}, bf16[2,80,1536]{2,1,0:T(8,128)(2,1)}, u32[]{:S(2)}) copy-start(bf16[2,80,1536]{2,1,0:T(8,128)(2,1)} %up.1) | copy-start | bytes 1474564
  28.1 30.8 %all-to-all-start.1 = ((bf16[8,80,576]{2,1,0:T(8,128)(2,1)}), bf16[8,80,576]{2,1,0:T(8,128)(2,1)S(1)}, u32[]{:S(2)}, u32[]{:S(2)}) async-start(bf16[8,80,576]{2,1,0:T(8,128)(2,1)} %pair.1), calls=%async_computation.1 | async-start | bytes 1638400 | tf_op jit(solution)/shard_map/all_to_all | solution.py:200
  35.3 24.8 %collective-permute-start.2 = (bf16[2,80,768]{2,1,0:T(8,128)(2,1)}, bf16[2,80,768]{2,1,0:T(8,128)(2,1)S(1)}, u32[]{:S(2)}, u32[]{:S(2)}) collective-permute-start(bf16[2,80,768]{2,1,0:T(8,128)(2,1)} %get-tuple-element.17), channel_id=1, source_target_pairs={{0,8},{8,16},{16,24},{24,0},{1,9},{9,17},{17,25},{25,1},{2,10},{10... | collective-permute-start | bytes 737288 | tf_op jit(solution)/shard_map/ppermute | solution.py:205
  37.6 22.5 %collective-permute-start.3 = (bf16[2,80,768]{2,1,0:T(8,128)(2,1)S(1)}, bf16[2,80,768]{2,1,0:T(8,128)(2,1)S(1)}, u32[]{:S(2)}, u32[]{:S(2)}) collective-permute-start(bf16[2,80,768]{2,1,0:T(8,128)(2,1)S(1)} %get-tuple-element.18), channel_id=1, source_target_pairs={{0,16},{8,24},{16,0},{24,8},{1,17},{9,25},{17,1},{25,9},{2,18},{10... | collective-permute-start | bytes 737288 | tf_op jit(solution)/shard_map/ppermute | solution.py:205
  41.5 18.6 %collective-permute-start.4 = (bf16[2,80,768]{2,1,0:T(8,128)(2,1)S(1)}, bf16[2,80,768]{2,1,0:T(8,128)(2,1)S(1)}, u32[]{:S(2)}, u32[]{:S(2)}) collective-permute-start(bf16[2,80,768]{2,1,0:T(8,128)(2,1)S(1)} %get-tuple-element.19), channel_id=1, source_target_pairs={{0,24},{8,0},{16,8},{24,16},{1,25},{9,1},{17,9},{25,17},{2,26},{10... | collective-permute-start | bytes 737288 | tf_op jit(solution)/shard_map/ppermute | solution.py:205
  61.4 18.5 %all-to-all-start.2 = ((bf16[8,32,768]{2,1,0:T(8,128)(2,1)}), bf16[8,32,768]{2,1,0:T(8,128)(2,1)S(1)}, u32[]{:S(2)}, u32[]{:S(2)}) async-start(bf16[8,32,768]{2,1,0:T(8,128)(2,1)} %bitcast.6), calls=%async_computation.2 | async-start | bytes 786432 | tf_op jit(solution)/shard_map/all_to_all | solution.py:200
  64.8 20.9 %collective-permute-start.6 = (bf16[576,640]{1,0:T(8,128)(2,1)}, bf16[576,640]{1,0:T(8,128)(2,1)S(1)}, u32[]{:S(2)}, u32[]{:S(2)}) collective-permute-start(bf16[576,640]{1,0:T(8,128)(2,1)} %bitcast.4.refs_0_), channel_id=1, source_target_pairs={{0,8},{8,16},{16,24},{24,0},{1,9},{9,17},{17,25},{25,1},{2,10},{10... | collective-permute-start | bytes 2211848 | tf_op jit(solution)/shard_map/ppermute | solution.py:205
  67.1 19.6 %collective-permute-start.7 = (bf16[576,640]{1,0:T(8,128)(2,1)}, bf16[576,640]{1,0:T(8,128)(2,1)S(1)}, u32[]{:S(2)}, u32[]{:S(2)}) collective-permute-start(bf16[576,640]{1,0:T(8,128)(2,1)} %bitcast.4.refs_0_), channel_id=1, source_target_pairs={{0,24},{8,0},{16,8},{24,16},{1,25},{9,1},{17,9},{25,17},{2,26},{10... | collective-permute-start | bytes 2211848 | tf_op jit(solution)/shard_map/ppermute | solution.py:205
  80.0 8.8 %collective-permute-start.5 = (bf16[32,768]{1,0:T(8,128)(2,1)S(1)}, bf16[32,768]{1,0:T(8,128)(2,1)S(1)}, u32[]{:S(2)}, u32[]{:S(2)}) collective-permute-start(bf16[32,768]{1,0:T(8,128)(2,1)S(1)} %get-tuple-element.21), channel_id=1, source_target_pairs={{0,32},{32,0},{1,33},{33,1},{2,34},{34,2},{3,35},{35,3},{4,36},{36... | collective-permute-start | bytes 147464 | tf_op jit(solution)/shard_map/ppermute | solution.py:205
  88.9 0.9 copy-start.3
  89.8 46.6 %all-to-all-start.3 = ((bf16[32,32,384]{2,1,0:T(8,128)(2,1)}), bf16[32,32,384]{2,1,0:T(8,128)(2,1)S(1)}, u32[]{:S(2)}, u32[]{:S(2)}) async-start(bf16[32,32,384]{2,1,0:T(8,128)(2,1)} %copy-done.3), calls=%async_computation.3 | async-start | bytes 1572864 | tf_op jit(solution)/shard_map/all_to_all | solution.py:200
  97.4 14.2 %collective-permute-start.8 = (bf16[576,640]{1,0:T(8,128)(2,1)}, bf16[576,640]{1,0:T(8,128)(2,1)}, u32[]{:S(2)}, u32[]{:S(2)}) collective-permute-start(bf16[576,640]{1,0:T(8,128)(2,1)} %bitcast.4.refs_0_), channel_id=1, source_target_pairs={{0,1},{1,0},{2,3},{3,2},{4,5},{5,4},{6,7},{7,6},{8,9},{9,8},{10,11... | collective-permute-start | bytes 2211848 | tf_op jit(solution)/shard_map/ppermute | solution.py:205
  101.5 10.1 %collective-permute-start.10 = (bf16[576,640]{1,0:T(8,128)(2,1)S(1)}, bf16[576,640]{1,0:T(8,128)(2,1)}, u32[]{:S(2)}, u32[]{:S(2)}) collective-permute-start(bf16[576,640]{1,0:T(8,128)(2,1)S(1)} %get-tuple-element.24.refs_4_), channel_id=1, source_target_pairs={{0,1},{1,0},{2,3},{3,2},{4,5},{5,4},{6,7},{7,6},{8,9},{9,8},{10,11... | collective-permute-start | bytes 2211848 | tf_op jit(solution)/shard_map/ppermute | solution.py:205
  103.4 8.1 %collective-permute-start.9 = (bf16[576,640]{1,0:T(8,128)(2,1)S(1)}, bf16[576,640]{1,0:T(8,128)(2,1)}, u32[]{:S(2)}, u32[]{:S(2)}) collective-permute-start(bf16[576,640]{1,0:T(8,128)(2,1)S(1)} %get-tuple-element.23.refs_2_), channel_id=1, source_target_pairs={{0,1},{1,0},{2,3},{3,2},{4,5},{5,4},{6,7},{7,6},{8,9},{9,8},{10,11... | collective-permute-start | bytes 2211848 | tf_op jit(solution)/shard_map/ppermute | solution.py:205
  105.9 25.7 %collective-permute-start.1 = (bf16[576,640]{1,0:T(8,128)(2,1)}, bf16[576,640]{1,0:T(8,128)(2,1)}, u32[]{:S(2)}, u32[]{:S(2)}) collective-permute-start(bf16[576,640]{1,0:T(8,128)(2,1)} %bitcast.4.refs_0_), channel_id=1, source_target_pairs={{0,16},{8,24},{16,0},{24,8},{1,17},{9,25},{17,1},{25,9},{2,18},{10... | collective-permute-start | bytes 2211848 | tf_op jit(solution)/shard_map/ppermute | solution.py:205
  120.9 1.0 copy-start.1
  121.9 9.7 %copy-start.6 = (f32[512,128]{1,0:T(8,128)}, f32[512,128]{1,0:T(8,128)S(1)}, u32[]{:S(2)}) copy-start(f32[512,128]{1,0:T(8,128)S(1)} %get-tuple-element.27.refs_3_) | copy-start | bytes 786436
  131.6 9.8 %collective-permute-start.11 = (bf16[576,640]{1,0:T(8,128)(2,1)}, bf16[576,640]{1,0:T(8,128)(2,1)S(1)}, u32[]{:S(2)}, u32[]{:S(2)}) collective-permute-start(bf16[576,640]{1,0:T(8,128)(2,1)} %hold.3.refs_0_), channel_id=1, source_target_pairs={{0,1},{1,0},{2,3},{3,2},{4,5},{5,4},{6,7},{7,6},{8,9},{9,8},{10,11... | collective-permute-start | bytes 2211848 | tf_op jit(solution)/shard_map/ppermute | solution.py:205
  134.1 0.7 copy-start.9
  134.9 1.4 copy-start.11
  137.4 11.2 %all-to-all-start.4 = ((bf16[8,32,128]{2,1,0:T(8,128)(2,1)}), bf16[8,32,128]{2,1,0:T(8,128)(2,1)S(1)}, u32[]{:S(2)}, u32[]{:S(2)}) async-start(bf16[8,32,128]{2,1,0:T(8,128)(2,1)} %second.1), calls=%async_computation.4 | async-start | bytes 131072 | tf_op jit(solution)/shard_map/all_to_all | solution.py:200
  141.4 1.2 copy-start.2
  142.6 0.9 copy-start.7
